TPU v7x, 128 devices: a whole 4x4x4 slice. The times are simulated.
128 devices in a mesh: seq: 16 (over z, y), exp: 8 (over x, core).
Axes of the slice: x: 4, y: 4, z: 4, core: 2. Of those that a mesh axis runs over, the one named last changes fastest.
Arguments:
- queries: bfloat16 [4096, 6144], P('seq', 'exp'), may hold values from -6 to 6
- key_rows: bfloat16 [4096, 6144], P('seq', 'exp'), may hold values from -6 to 6
- value_rows: bfloat16 [4096, 6144], P('seq', 'exp'), may hold values from -6 to 6
- log_decay: float32 [4096, 48], P('seq', 'exp'), may hold values from -1 to 0, as said below
- residual: bfloat16 [4096, 6144], P('seq', 'exp'), may hold values from -6 to 6
- head_gain: float32 [6144], P('exp'), may hold values from 0.1 to 1.9
- moe_gain: float32 [6144], replicated, may hold values from 0.1 to 1.9
- routes: int32 [4096, 2], P(('seq', 'exp')), may hold values from 0 to 7, all different within a row; in each aligned block of 32 rows (0 to 31, 32 to 63, ...) at most 10 rows name the same one
- route_weight: float32 [4096, 2], P(('seq', 'exp')), may hold values from 0.2 to 1
- up_weight: bfloat16 [8, 6144, 9216], P('exp', None, 'seq'), may hold values from -0.078125 to 0.078125
- down_weight: bfloat16 [8, 9216, 6144], P('exp', 'seq'), may hold values from -0.0625 to 0.0625
Outputs:
- layer_out: bfloat16 [4096, 6144], P(('seq', 'exp'))
Inputs may be any that keep to these rules, and one draw needn't show every extreme that they name: `log_decay`: every entry is negative. `routes`: A row names two different experts. In each aligned block of 32 rows no expert is named more than 10 times, a bound that some block reaches.
All inputs are finite; a program needn't handle non-finite values.
Results may differ from a plain program's by a relative error of at most 0.012.
Values may be sent and summed in bfloat16 or wider, within the bound.
No kernel may reach another device: no remote copies, remote signals or barrier semaphores. Data moves between devices by JAX's collectives and lax.ppermute only.
A program may use at most 192 MiB of HBM per device.

v0:
```python
import jax
import jax.numpy as jnp
from jax import lax
from jax.sharding import PartitionSpec as P

HEAD_DIM = 128
BLK = 256
EXPERTS = 8


def expert_part(received, up_weight, down_weight):
    hidden = jax.nn.silu(
        jnp.einsum("sxkd,xdh->sxkh", received, up_weight, preferred_element_type=jnp.float32)
    ).astype(jnp.bfloat16)
    return jnp.einsum(
        "sxkh,xhd->sxkd", hidden, down_weight, preferred_element_type=jnp.float32
    ).astype(jnp.bfloat16)


def per_device(
    queries,
    key_rows,
    value_rows,
    log_decay,
    residual,
    head_gain,
    moe_gain,
    routes,
    route_weight,
    up_weight,
    down_weight,
):
    token_count, feature_dim = queries.shape
    head_count = log_decay.shape[1]
    block_count = token_count // BLK
    shaped = (block_count, BLK, head_count, HEAD_DIM)
    query_blk = queries.reshape(shaped)
    key_blk = key_rows.reshape(shaped)
    value_blk = value_rows.reshape(shaped)
    cumulative = jnp.cumsum(log_decay.reshape(block_count, BLK, head_count), axis=1)
    totals = cumulative[:, -1, :]
    scores = jnp.einsum("bthd,bjhd->bhtj", query_blk, key_blk, preferred_element_type=jnp.float32)
    levels = jnp.transpose(cumulative, (0, 2, 1))
    spread = levels[:, :, :, None] - levels[:, :, None, :]
    causal = jnp.tril(jnp.ones((BLK, BLK), dtype=bool))[None, None]
    weights = (jnp.where(causal, jnp.exp(jnp.where(causal, spread, 0.0)), 0.0) * scores).astype(
        jnp.bfloat16
    )
    inner_part = jnp.einsum(
        "bhtj,bjhd->bthd", weights, value_blk, preferred_element_type=jnp.float32
    )
    fading = jnp.exp(totals[:, None, :] - cumulative)
    key_faded = (fading[..., None] * key_blk.astype(jnp.float32)).astype(jnp.bfloat16)
    block_states = jnp.einsum(
        "bjhd,bjhe->bhde", key_faded, value_blk, preferred_element_type=jnp.float32
    )

    def advance(running, pair_item):
        total_row, state_row = pair_item
        return (jnp.exp(total_row)[:, None, None] * running + state_row, running)

    empty_state = jnp.zeros((head_count, HEAD_DIM, HEAD_DIM), jnp.float32)
    own_state, local_prev = lax.scan(advance, empty_state, (totals, block_states))
    own_log = jnp.sum(totals, axis=0)
    logs_all, states_all = (
        lax.all_gather(own_log[None].astype(jnp.bfloat16), "seq", axis=0, tiled=True).astype(
            jnp.float32
        ),
        lax.all_gather(own_state[None].astype(jnp.bfloat16), "seq", axis=0, tiled=True).astype(
            jnp.float32
        ),
    )
    position = lax.axis_index("seq")
    below_me = jnp.arange(logs_all.shape[0])[:, None] < position
    inclusive = jnp.cumsum(logs_all, axis=0)
    before = jnp.sum(jnp.where(below_me, logs_all, 0.0), axis=0)
    factors = jnp.where(
        below_me, jnp.exp(jnp.where(below_me, before[None, :] - inclusive, 0.0)), 0.0
    )
    incoming = jnp.einsum("sh,shde->hde", factors, states_all, precision=lax.Precision.HIGHEST)
    starts = jnp.concatenate(
        [jnp.zeros((1, head_count), jnp.float32), jnp.cumsum(totals, axis=0)[:-1]], axis=0
    )
    carried = jnp.exp(starts)[:, :, None, None] * incoming[None] + local_prev
    query_faded = jnp.exp(cumulative)[..., None] * query_blk.astype(jnp.float32)
    carried_part = jnp.einsum(
        "bthd,bhde->bthe", query_faded, carried, precision=lax.Precision.HIGHEST
    )
    attention = carried_part + inner_part
    mean_square = jnp.mean(attention * attention, axis=-1, keepdims=True)
    normed = attention * lax.rsqrt(mean_square + 1e-06) * head_gain.reshape(head_count, HEAD_DIM)
    mixed_rows = (residual.astype(jnp.float32) + normed.reshape(token_count, feature_dim)).astype(
        jnp.bfloat16
    )
    token_rows = lax.all_to_all(mixed_rows, "exp", split_axis=0, concat_axis=1, tiled=True)
    row_count, model_dim = token_rows.shape
    token_float = token_rows.astype(jnp.float32)
    row_square = jnp.mean(token_float * token_float, axis=-1, keepdims=True)
    norm_rows = (token_float * lax.rsqrt(row_square + 1e-06) * moe_gain).astype(jnp.bfloat16)
    capacity = row_count * 10 // (4 * EXPERTS)
    flat_ids = routes.reshape(-1)
    onehot = (flat_ids[:, None] == jnp.arange(EXPERTS, dtype=jnp.int32)[None, :]).astype(jnp.int32)
    slot_rank = jnp.sum((jnp.cumsum(onehot, axis=0) - 1) * onehot, axis=1)
    slot_index = flat_ids * capacity + slot_rank
    placer = jnp.arange(EXPERTS * capacity, dtype=jnp.int32)[:, None] == slot_index[None, :]
    placer = jnp.any(placer.reshape(EXPERTS * capacity, row_count, 2), axis=2).astype(jnp.bfloat16)
    packed = jnp.dot(placer, norm_rows, preferred_element_type=jnp.float32).astype(jnp.bfloat16)
    seq_count = lax.axis_size("seq")
    exp_count = lax.axis_size("exp")
    local_experts = up_weight.shape[0]
    buffer = jnp.broadcast_to(
        packed.reshape(1, exp_count, local_experts, capacity, model_dim),
        (seq_count, exp_count, local_experts, capacity, model_dim),
    )
    buffer = buffer.reshape(seq_count * exp_count, local_experts, capacity, model_dim)
    answered = expert_part(
        lax.all_to_all(buffer, ("seq", "exp"), split_axis=0, concat_axis=0, tiled=True),
        up_weight,
        down_weight,
    )
    returned = lax.all_to_all(answered, ("seq", "exp"), split_axis=0, concat_axis=0, tiled=True)
    summed = jnp.sum(
        returned.reshape(seq_count, EXPERTS * capacity, model_dim), axis=0, dtype=jnp.float32
    )
    picked = jnp.take(summed, slot_index, axis=0).reshape(row_count, 2, model_dim)
    combined = jnp.sum(picked * route_weight[:, :, None], axis=1)
    return (token_float + combined).astype(jnp.bfloat16)


def solution(mesh):
    return jax.shard_map(
        per_device,
        mesh=mesh,
        in_specs=(
            P("seq", "exp"),
            P("seq", "exp"),
            P("seq", "exp"),
            P("seq", "exp"),
            P("seq", "exp"),
            P("exp"),
            P(),
            P(("seq", "exp"), None),
            P(("seq", "exp"), None),
            P("exp", None, "seq"),
            P("exp", "seq", None),
        ),
        out_specs=P(("seq", "exp"), None),
        check_vma=False,
    )
```

profile of v0, /device:TPU:84, one launch (start us, length us, event | category | flops | bytes accessed | tf_op | source)
XLA Modules:
  0.0 917.7 jit_solution(6794648060793290283)
XLA Ops:
  6.5 0.8 reshape.288
  7.3 1.8 reduce-window.6
  9.1 0.1 slice.14
  9.2 0.1 copy.134
  9.3 0.1 copy.136
  9.6 0.1 copy.141
  9.6 1.2 copy.142
  10.8 1.2 copy.143
  12.0 0.9 fusion.18
  12.9 0.0 all-gather.4.cloned.1.call-update
  13.0 19.4 %all-gather = bf16[16,1,6]{2,1,0:T(2,128)(2,1)S(1)} all-gather(bf16[1,1,6]{2,1,0:T(2,128)(2,1)S(1)} %slice.21), channel_id=2, replica_groups=mesh['seq'=16,'exp'=8] {'seq'}, dimensions={0}, use_global_device_ids=true | all-gather | bytes 204 | tf_op jit(solution)/shard_map/all_gather | solution.py:66
  32.4 0.1 copy.135
  32.5 0.1 copy.138
  32.6 0.1 copy.139
  32.7 0.1 copy.145
  32.8 0.2 copy.146
  33.0 0.1 copy.152
  33.1 0.1 reshape.299
  33.2 0.1 fusion.31
  33.3 0.1 reduce_window_sum.59
  33.4 0.1 select_reduce_fusion.1
  33.5 0.1 broadcast_bitcast_fusion
  33.6 0.1 select_bitcast_fusion
  33.7 26.5 %all-gather.4.cloned.1.call-done = bf16[96,128,128]{2,1,0:T(8,128)(2,1)} async-done(((bf16[6,128,128]{2,1,0:T(8,128)(2,1)}), bf16[96,128,128]{2,1,0:T(8,128)(2,1)}) %all-gather.4.cloned.1.call-update) | async-done | bytes 3145744 | tf_op jit(solution)/shard_map/all_gather | solution.py:69
  60.2 2.6 multiply_reduce_fusion
  62.8 0.0 copy-start.6
  62.8 0.9 fusion.23
  63.7 0.0 copy-start.3
  63.7 0.9 multiply_reduce_fusion.2
  64.6 0.2 multiply_multiply_fusion
  64.8 0.3 copy.150
  65.1 0.0 copy-start.4
  65.1 0.8 add_convert_fusion.1
  65.9 4.8 all-to-all-start
  70.7 0.2 select_reduce_fusion
  70.9 0.1 reduce_sum.65
  71.0 0.1 copy.153
  71.1 0.1 fusion.32
  71.2 5.3 all-to-all-done
  76.5 0.1 convert_bitcast_fusion.1
  76.5 0.1 copy.174
  76.6 0.2 fusion.19
  76.8 0.7 copy-done
  77.5 0.5 convolution_convert_fusion
  78.0 0.4 broadcast_in_dim.92
  78.4 0.0 slice-start
  78.5 3.2 broadcast_in_dim.93
  81.6 0.0 slice-start.1
  81.6 282.5 %all_to_all.23 = bf16[128,1,10,6144]{3,2,1,0:T(8,128)(2,1)} all-to-all(bf16[128,1,10,6144]{3,2,1,0:T(8,128)(2,1)S(1)} %bitcast.110), channel_id=1, replica_groups=mesh['seq'=16,'exp'=8] {'seq','exp'}, dimensions={0} | all-to-all | bytes 31457280 | tf_op jit(solution)/shard_map/all_to_all | solution.py:117
  364.1 31.7 %fusion.8 = bf16[128,1,10,576]{0,3,2,1:T(8,128)(2,1)} fusion(bf16[1,6144,576]{1,2,0:T(8,128)(2,1)S(1)} %bitcast.132, bf16[128,1,10,6144]{3,2,1,0:T(8,128)(2,1)} %all_to_all.23), kind=kOutput, calls=%fused_computation.14 | convolution fusion | flops 9063383040 | bytes 24281088 | tf_op jit(solution)/shard_map/sxkd,xdh->sxkh/dot_general | solution.py:13
  395.9 15.1 %convert_bitcast_fusion = bf16[128,1,10,6144]{3,0,2,1:T(8,128)(2,1)S(1)} fusion(bf16[1,576,6144]{2,1,0:T(8,128)(2,1)} %param.21, bf16[128,1,10,576]{0,3,2,1:T(8,128)(2,1)} %fusion.8), kind=kOutput, calls=%fused_computation.4 | convolution fusion | flops 9067560960 | bytes 24281088 | tf_op jit(solution)/shard_map/sxkh,xhd->sxkd/dot_general | solution.py:15
  411.0 48.8 %copy.156 = bf16[128,1,10,6144]{3,2,1,0:T(8,128)(2,1)} copy(bf16[128,1,10,6144]{3,0,2,1:T(8,128)(2,1)S(1)} %convert_bitcast_fusion) | data formatting | bytes 31457280 | tf_op jit(solution)/shard_map/convert_element_type | solution.py:17
  459.8 11.7 %all-to-all-start.2 = ((bf16[128,1,10,6144]{3,2,1,0:T(8,128)(2,1)}), bf16[128,1,10,6144]{3,2,1,0:T(8,128)(2,1)}, u32[]{:S(2)}, u32[]{:S(2)}) async-start(bf16[128,1,10,6144]{3,2,1,0:T(8,128)(2,1)} %copy.156), calls=%async_computation.2 | async-start | bytes 50331648 | tf_op jit(solution)/shard_map/all_to_all | solution.py:121
  471.5 0.1 copy.157
  471.5 0.1 mul.147
  471.6 0.1 copy.154
  471.8 0.1 copy.158
  471.9 388.3 %all-to-all-done.2 = bf16[128,1,10,6144]{3,2,1,0:T(8,128)(2,1)} async-done(((bf16[128,1,10,6144]{3,2,1,0:T(8,128)(2,1)}), bf16[128,1,10,6144]{3,2,1,0:T(8,128)(2,1)}, u32[]{:S(2)}, u32[]{:S(2)}) %all-to-all-start.2) | async-done | bytes 15728672 | tf_op jit(solution)/shard_map/all_to_all | solution.py:121
  860.2 31.5 %reshape.305 = f32[16,80,6144]{2,1,0:T(8,128)} reshape(bf16[128,1,10,6144]{3,2,1,0:T(8,128)(2,1)} %all-to-all-done.2) | data formatting | bytes 47185920 | tf_op jit(solution)/shard_map/convert_element_type | solution.py:122
  891.7 11.4 %reduce_sum.67 = f32[80,6144]{1,0:T(8,128)S(1)} reduce(f32[16,80,6144]{2,1,0:T(8,128)} %reshape.305, f32[]{:T(128)} %constant.38.clone.1), dimensions={0}, to_apply=%region_9.10 | reduce | flops 7372800 | bytes 33423364 | tf_op jit(solution)/shard_map/reduce_sum | solution.py:122
  903.1 2.2 gather_fusion
  905.3 2.3 gather.7
  907.6 2.4 multiply_reduce_fusion.1
  910.0 0.8 add_convert_fusion
  (34 shorter events, 0.3 us)
Async XLA Ops:
  6.5 26.3 %copy-start.2 = (bf16[256,768]{1,0:T(8,128)(2,1)S(1)}, bf16[256,768]{1,0:T(8,128)(2,1)}, u32[]{:S(2)}) copy-start(bf16[256,768]{1,0:T(8,128)(2,1)} %param.11) | copy-start | bytes 1179652
  6.5 26.5 %copy-start.5 = (s32[32,2]{0,1:T(2,128)S(1)}, s32[32,2]{0,1:T(2,128)}, u32[]{:S(2)}) copy-start(s32[32,2]{0,1:T(2,128)} %param.18) | copy-start | bytes 772
  6.5 53.6 %all-gather.4.cloned.1.call-start = ((), (), s32[]{:S(2)}) async-start(), calls=%async_computation.3 | async-start | bytes 3342336 | tf_op jit(solution)/shard_map/all_gather | solution.py:69
  62.8 1.8 copy-start.6
  63.7 1.3 copy-start.3
  65.1 12.5 %copy-start.4 = (f32[6144]{0:T(1024)S(1)}, f32[6144]{0:T(1024)}, u32[]{:S(2)}) copy-start(f32[6144]{0:T(1024)} %param.17) | copy-start | bytes 73732
  65.9 10.6 %all-to-all-start = ((bf16[8,32,768]{2,1,0:T(8,128)(2,1)}), bf16[8,32,768]{2,1,0:T(8,128)(2,1)S(1)}, u32[]{:S(2)}, u32[]{:S(2)}) async-start(bf16[8,32,768]{2,1,0:T(8,128)(2,1)} %bitcast.26), calls=%async_computation | async-start | bytes 786432 | tf_op jit(solution)/shard_map/all_to_all | solution.py:95
  76.6 0.9 copy-start
  78.4 285.7 %slice-start = ((s8[7077888]{0:T(1024)(128)(4,1)}), s8[4194304]{0:T(1024)(128)(4,1)S(1)}, s32[]{:S(2)}) async-start(s8[7077888]{0:T(1024)(128)(4,1)} %bitcast.131), calls=%async_computation.4 | async-start | bytes 8388608
  81.6 282.5 %slice-start.1 = ((s8[7077888]{0:T(1024)(128)(4,1)}), s8[2883584]{0:T(1024)(128)(4,1)S(1)}, s32[]{:S(2)}) async-start(s8[7077888]{0:T(1024)(128)(4,1)} %bitcast.131), calls=%async_computation.5 | async-start | bytes 5767168
  459.8 12.0 %copy-start.7 = (f32[32,2]{0,1:T(2,128)S(1)}, f32[32,2]{0,1:T(2,128)}, u32[]{:S(2)}) copy-start(f32[32,2]{0,1:T(2,128)} %param.19) | copy-start | bytes 772
  459.8 400.4 %all-to-all-start.2 = ((bf16[128,1,10,6144]{3,2,1,0:T(8,128)(2,1)}), bf16[128,1,10,6144]{3,2,1,0:T(8,128)(2,1)}, u32[]{:S(2)}, u32[]{:S(2)}) async-start(bf16[128,1,10,6144]{3,2,1,0:T(8,128)(2,1)} %copy.156), calls=%async_computation.2 | async-start | bytes 50331648 | tf_op jit(solution)/shard_map/all_to_all | solution.py:121
  905.3 4.7 copy-start.1
Sparse Core Ops, SparseCore 0:
  13.1 47.0 all-gather.3
where the time goes:
time: 919 us; the launch traced here: 918 us
  waiting for transfers between devices  420 us (46%)
  blocking collectives  302 us (33%)
  local copies, waits for them, and re-layouts  94.3 us (10%)
  matrix products  50.1 us (5%)
  other arithmetic  21.1 us (2%)
  starting transfers between devices  16.5 us (2%)
  between operations  13.7 us (1%)
    all_to_all x1, waiting for transfers between devices, per_device(): lax.all_to_all(answered, ('seq', 'exp'), split_axis=0, concat_axis=0, til...  388 us
    all_to_all x1, blocking collectives, per_device(): lax.all_to_all(buffer, ('seq', 'exp'), split_axis=0, concat_axis=0, tiled...  282 us
    convert_element_type x1, local copies, waits for them, and re-layouts, expert_part(): return jnp.einsum('sxkh,xhd->sxkd', hidden, down_weight, preferred_elemen...  48.8 us
    dot_general x1, matrix products, expert_part(): jnp.einsum('sxkd,xdh->sxkh', received, up_weight, preferred_element_type=...  31.7 us
    convert_element_type x1, local copies, waits for them, and re-layouts, per_device(): jnp.sum(returned.reshape(seq_count, EXPERTS * capacity, model_dim), axis=...  31.5 us
    all_gather x1, waiting for transfers between devices, per_device(): lax.all_gather(own_state[None].astype(jnp.bfloat16), 'seq', axis=0, tiled...  26.5 us
    all_gather x1, blocking collectives, per_device(): lax.all_gather(own_log[None].astype(jnp.bfloat16), 'seq', axis=0, tiled=T...  19.4 us
  transfers between devices with their start and end apart: 3, of which 3 were waited for; matrix products, arithmetic and copies ran while one was open for 0% of the time, Pallas kernels for 0%

commit v1 on v0

v1 whole, which is shorter than its diff:
```python
import jax
import jax.numpy as jnp
from jax import lax
from jax.experimental import pallas as pl
from jax.experimental.pallas import tpu as pltpu
from jax.sharding import Mesh
from jax.sharding import PartitionSpec as P

HEAD_DIM = 128
BLK = 256
EXPERTS = 8
CAP = 10
ROWS = 32
LOG_ROWS = 16
VMEM = 56 * 1024 * 1024
F32 = jnp.float32
BF16 = jnp.bfloat16
HIGH = lax.Precision.HIGHEST
SEQ = ("z", "y")
EXP = ("x", "core")


def params():
    return pltpu.CompilerParams(vmem_limit_bytes=VMEM)


def whole():
    return pl.BlockSpec(memory_space=pltpu.VMEM)


def call(kernel, out, *args):
    many = isinstance(out, (list, tuple))
    return pl.pallas_call(
        kernel,
        out_shape=out,
        in_specs=[whole()] * len(args),
        out_specs=[whole()] * len(out) if many else whole(),
        compiler_params=params(),
    )(*args)


def shape(dims, dtype):
    return jax.ShapeDtypeStruct(dims, dtype)


def split3(value):
    first = value.astype(BF16)
    rest = value - first.astype(F32)
    second = rest.astype(BF16)
    third = (rest - second.astype(F32)).astype(BF16)
    return first, second, third


def cumulated(decay):
    row = lax.broadcasted_iota(jnp.int32, (BLK, BLK), 0)
    col = lax.broadcasted_iota(jnp.int32, (BLK, BLK), 1)
    lower = (col <= row).astype(F32)
    return jnp.dot(lower, decay, preferred_element_type=F32, precision=HIGH)


def log_lines(logs):
    heads = logs.shape[1]
    wide = jnp.concatenate([logs, jnp.zeros((1, HEAD_DIM - heads), F32)], axis=1)
    parts = [p.astype(F32) for p in split3(wide)]
    lines = jnp.concatenate(parts + [jnp.zeros((LOG_ROWS - 3, HEAD_DIM), F32)], axis=0)
    return lines.astype(BF16)


def state_kernel(key_ref, value_ref, decay_ref, out_ref):
    heads = decay_ref.shape[1]
    cumul = cumulated(decay_ref[...])
    total = cumul[BLK - 1 :, :]
    fading = jnp.exp(total - cumul)
    for h in range(heads):
        cols = slice(h * HEAD_DIM, (h + 1) * HEAD_DIM)
        faded = (fading[:, h : h + 1] * key_ref[:, cols].astype(F32)).astype(BF16)
        own = lax.dot_general(
            faded, value_ref[:, cols], (((0,), (0,)), ((), ())), preferred_element_type=F32
        )
        out_ref[cols, :] = own.astype(BF16)
    out_ref[heads * HEAD_DIM :, :] = log_lines(total)


def inner_kernel(query_ref, key_ref, value_ref, decay_ref, out_ref):
    heads = decay_ref.shape[1]
    decay = decay_ref[...]
    cumul = cumulated(decay)
    row = lax.broadcasted_iota(jnp.int32, (BLK, BLK), 0)
    col = lax.broadcasted_iota(jnp.int32, (BLK, BLK), 1)
    upper = (row <= col).astype(F32)
    across = lax.dot_general(
        decay, upper, (((0,), (0,)), ((), ())), preferred_element_type=F32, precision=HIGH
    )
    causal = col <= row
    for h in range(heads):
        cols = slice(h * HEAD_DIM, (h + 1) * HEAD_DIM)
        scores = lax.dot_general(
            query_ref[:, cols],
            key_ref[:, cols],
            (((1,), (1,)), ((), ())),
            preferred_element_type=F32,
        )
        spread = cumul[:, h : h + 1] - across[h : h + 1, :]
        weights = jnp.where(causal, jnp.exp(jnp.where(causal, spread, 0.0)) * scores, 0.0)
        out_ref[:, cols] = jnp.dot(
            weights.astype(BF16), value_ref[:, cols], preferred_element_type=F32
        )


def read_logs(ref, i, heads):
    rows = ref[i, heads * HEAD_DIM :, :].astype(F32)
    return rows[0:1] + rows[1:2] + rows[2:3]


def line_kernel(place_ref, gathered_ref, line_ref, before_ref, log_ref):
    heads = gathered_ref.shape[1] // HEAD_DIM
    mine = place_ref[1]
    count = gathered_ref.shape[0]
    logs = [read_logs(gathered_ref, i, heads) for i in range(count)]
    below = [jnp.where(i < mine, logs[i], 0.0) for i in range(count)]
    to_end, to_me = [], []
    for i in range(count):
        to_end.append(jnp.exp(sum(logs[i + 1 :], jnp.zeros_like(logs[0]))))
        to_me.append(
            jnp.where(i < mine, jnp.exp(sum(below[i + 1 :], jnp.zeros_like(logs[0]))), 0.0)
        )
    for h in range(heads):
        rows = slice(h * HEAD_DIM, (h + 1) * HEAD_DIM)
        end = jnp.zeros((HEAD_DIM, HEAD_DIM), F32)
        me = jnp.zeros((HEAD_DIM, HEAD_DIM), F32)
        for i in range(count):
            state = gathered_ref[i, rows, :].astype(F32)
            end = end + to_end[i][:, h : h + 1] * state
            me = me + to_me[i][:, h : h + 1] * state
        line_ref[rows, :] = end.astype(BF16)
        before_ref[rows, :] = me
    line_ref[heads * HEAD_DIM :, :] = log_lines(sum(logs)[:, :heads])
    log_ref[...] = jnp.broadcast_to(sum(below), log_ref.shape)


def mix_kernel(
    place_ref,
    query_ref,
    decay_ref,
    inner_ref,
    residual_ref,
    gain_ref,
    lines_ref,
    before_ref,
    log_ref,
    routes_ref,
    mixed_ref,
    packed_ref,
):
    heads = decay_ref.shape[1]
    mine = place_ref[0]
    count = lines_ref.shape[0]
    logs = [read_logs(lines_ref, i, heads) for i in range(count)]
    below = [jnp.where(i < mine, logs[i], 0.0) for i in range(count)]
    here = log_ref[0:1, :]
    factors = [
        jnp.where(i < mine, jnp.exp(sum(below[i + 1 :], here)), 0.0) for i in range(count)
    ]
    fade = jnp.exp(cumulated(decay_ref[...]))
    for h in range(heads):
        cols = slice(h * HEAD_DIM, (h + 1) * HEAD_DIM)
        state = before_ref[cols, :]
        for i in range(count):
            state = state + factors[i][:, h : h + 1] * lines_ref[i, cols, :].astype(F32)
        faded = fade[:, h : h + 1] * query_ref[:, cols].astype(F32)
        attention = inner_ref[:, cols] + jnp.dot(
            faded, state, preferred_element_type=F32, precision=HIGH
        )
        square = jnp.mean(attention * attention, axis=-1, keepdims=True)
        normed = attention * lax.rsqrt(square + 1e-06) * gain_ref[:, cols]
        mixed_ref[:, cols] = (residual_ref[:, cols].astype(F32) + normed).astype(BF16)
    token = lax.broadcasted_iota(jnp.int32, (EXPERTS, BLK), 1)
    expert = lax.broadcasted_iota(jnp.int32, (EXPERTS, BLK), 0)
    names = (expert == routes_ref[0:1, :]) | (expert == routes_ref[1:2, :])
    row = lax.broadcasted_iota(jnp.int32, (BLK, BLK), 0)
    col = lax.broadcasted_iota(jnp.int32, (BLK, BLK), 1)
    earlier = ((row < col) & (row // ROWS == col // ROWS)).astype(BF16)
    rank = jnp.dot(names.astype(BF16), earlier, preferred_element_type=F32).astype(jnp.int32)
    slot = jnp.where(names, token // ROWS * CAP + rank, -1)
    slots = packed_ref.shape[1]
    which = lax.broadcasted_iota(jnp.int32, (slots, BLK), 0)
    mixed = mixed_ref[...]
    for e in range(EXPERTS):
        placer = (which == slot[e : e + 1, :]).astype(BF16)
        packed_ref[e] = jnp.dot(placer, mixed, preferred_element_type=F32).astype(BF16)


def norm_kernel(parts_ref, gain_ref, out_ref):
    parts, _, width = parts_ref.shape
    square = 0.0
    for j in range(parts):
        value = parts_ref[j].astype(F32)
        square = square + jnp.sum(value * value, axis=-1, keepdims=True)
    scale = lax.rsqrt(square / (parts * width) + 1e-06)
    for j in range(parts):
        cols = slice(j * width, (j + 1) * width)
        out_ref[:, cols] = (parts_ref[j].astype(F32) * scale * gain_ref[:, cols]).astype(BF16)


def expert_kernel(rows_ref, up_ref, down_ref, out_ref):
    value = jnp.dot(rows_ref[...], up_ref[...], preferred_element_type=F32)
    hidden = (value / (1.0 + jnp.exp(-value))).astype(BF16)
    out_ref[...] = jnp.dot(hidden, down_ref[...], preferred_element_type=F32).astype(BF16)


def expert_part(rows, up_weight, down_weight, tile):
    total, width = rows.shape
    units = up_weight.shape[-1]
    once = pl.Buffered(1)
    return pl.pallas_call(
        expert_kernel,
        grid=(total // tile,),
        out_shape=shape((total, width), BF16),
        in_specs=[
            pl.BlockSpec((tile, width), lambda i: (i, 0)),
            pl.BlockSpec((None, width, units), lambda i: (0, 0, 0), pipeline_mode=once),
            pl.BlockSpec((None, units, width), lambda i: (0, 0, 0), pipeline_mode=once),
        ],
        out_specs=pl.BlockSpec((tile, width), lambda i: (i, 0)),
        compiler_params=params(),
        cost_estimate=pl.CostEstimate(
            flops=4 * total * width * units,
            bytes_accessed=4 * (total + units) * width,
            transcendentals=total * units,
        ),
    )(rows, up_weight, down_weight)


def combine_kernel(routes_ref, weight_ref, returned_ref, mixed_ref, out_ref):
    rows = out_ref.shape[0]
    routes = routes_ref[...]
    expert = lax.broadcasted_iota(jnp.int32, (rows, EXPERTS), 1)
    names = [expert == routes[:, i : i + 1] for i in range(2)]
    row = lax.broadcasted_iota(jnp.int32, (rows, rows), 0)
    col = lax.broadcasted_iota(jnp.int32, (rows, rows), 1)
    earlier = (col < row).astype(BF16)
    rank = jnp.dot(
        earlier, (names[0] | names[1]).astype(BF16), preferred_element_type=F32
    ).astype(jnp.int32)
    place = lax.broadcasted_iota(jnp.int32, (rows, EXPERTS * CAP), 1)
    blend = jnp.zeros((rows, EXPERTS * CAP), F32)
    for i in range(2):
        slot = jnp.sum(jnp.where(names[i], expert * CAP + rank, 0), axis=1, keepdims=True)
        blend = blend + jnp.where(place == slot, weight_ref[:, i : i + 1], 0.0)
    parts = split3(blend)
    width = mixed_ref.shape[2]
    for j in range(mixed_ref.shape[0]):
        cols = slice(j * width, (j + 1) * width)
        value = returned_ref[:, cols]
        added = sum(jnp.dot(p, value, preferred_element_type=F32) for p in parts)
        out_ref[:, cols] = (mixed_ref[j].astype(F32) + added).astype(BF16)


def per_device(
    queries,
    key_rows,
    value_rows,
    log_decay,
    residual,
    head_gain,
    moe_gain,
    routes,
    route_weight,
    up_weight,
    down_weight,
):
    token_count, width = queries.shape
    heads = log_decay.shape[1]
    model = moe_gain.shape[0]
    exp_count = model // width
    slots = token_count // ROWS * CAP
    place = jnp.stack([lax.axis_index("z"), lax.axis_index("y")]).astype(jnp.int32)
    all_routes = lax.all_gather(routes, EXP, axis=0, tiled=True).T

    state_rows = heads * HEAD_DIM + LOG_ROWS
    sent = call(state_kernel, shape((state_rows, HEAD_DIM), BF16), key_rows, value_rows, log_decay)
    in_line = lax.all_gather(sent, "y", axis=0, tiled=False)
    inner = call(
        inner_kernel, shape((token_count, width), F32), queries, key_rows, value_rows, log_decay
    )
    scalar = pl.BlockSpec(memory_space=pltpu.SMEM)
    line, before, line_log = pl.pallas_call(
        line_kernel,
        out_shape=[
            shape((state_rows, HEAD_DIM), BF16),
            shape((heads * HEAD_DIM, HEAD_DIM), F32),
            shape((8, HEAD_DIM), F32),
        ],
        in_specs=[scalar, whole()],
        out_specs=[whole()] * 3,
        compiler_params=params(),
    )(place, in_line)
    lines = lax.all_gather(line, "z", axis=0, tiled=False)
    mixed, packed = pl.pallas_call(
        mix_kernel,
        out_shape=[
            shape((token_count, width), BF16),
            shape((EXPERTS, slots, width), BF16),
        ],
        in_specs=[scalar] + [whole()] * 9,
        out_specs=[whole()] * 2,
        compiler_params=params(),
    )(
        place,
        queries,
        log_decay,
        inner,
        residual,
        head_gain.reshape(1, width),
        lines,
        before,
        line_log,
        all_routes,
    )
    parts = lax.all_to_all(packed, EXP, split_axis=0, concat_axis=0, tiled=True)
    home = lax.all_to_all(
        mixed.reshape(exp_count, ROWS, width), EXP, split_axis=0, concat_axis=0, tiled=True
    )
    normed = call(norm_kernel, shape((slots, model), BF16), parts, moe_gain.reshape(1, model))
    rows = lax.all_gather(normed, SEQ, axis=0, tiled=True)
    partial = expert_part(rows, up_weight, down_weight, 256)
    summed = lax.psum_scatter(partial, SEQ, scatter_dimension=0, tiled=True)
    back = lax.all_to_all(
        summed.reshape(exp_count, CAP * model // HEAD_DIM, HEAD_DIM),
        EXP,
        split_axis=0,
        concat_axis=0,
        tiled=True,
    )
    returned = back.reshape(EXPERTS * CAP, model)
    return call(
        combine_kernel, shape((ROWS, model), BF16), routes, route_weight, returned, home
    )


def solution(mesh):
    fine = Mesh(mesh.devices.reshape(4, 4, 4, 2), ("z", "y", "x", "core"))
    both = ("z", "y", "x", "core")
    return jax.shard_map(
        per_device,
        mesh=fine,
        in_specs=(
            P(SEQ, EXP),
            P(SEQ, EXP),
            P(SEQ, EXP),
            P(SEQ, EXP),
            P(SEQ, EXP),
            P(EXP),
            P(),
            P(both, None),
            P(both, None),
            P(EXP, None, SEQ),
            P(EXP, SEQ, None),
        ),
        out_specs=P(both, None),
        check_vma=False,
    )
```

time: 919 us -> 378 us (0.41)
  the two profiles are of different devices: /device:TPU:84 before, /device:TPU:1 now
where the time goes in v1:
time: 378 us; the launch traced here: 377 us
  waiting for transfers between devices  203 us (54%)
  blocking collectives  83.6 us (22%)
  Pallas kernels  52.6 us (14%)
  local copies, waits for them, and re-layouts  19.1 us (5%)
  between operations  13.4 us (4%)
  starting transfers between devices  4.35 us (1%)
    reduce_scatter x1, waiting for transfers between devices, per_device(): summed = lax.psum_scatter(partial, SEQ, scatter_dimension=0, tiled=True)  105 us
    all_gather x1, waiting for transfers between devices, per_device(): rows = lax.all_gather(normed, SEQ, axis=0, tiled=True)  92.4 us
    pallas_call x1, Pallas kernels, expert_part(): pl.pallas_call(expert_kernel, grid=(total // tile,), out_shape=shape((tot...  33.3 us
    all_to_all x1, blocking collectives, per_device(): lax.all_to_all(summed.reshape(exp_count, CAP * model // HEAD_DIM, HEAD_DI...  19.6 us
    all_to_all x1, blocking collectives, per_device(): parts = lax.all_to_all(packed, EXP, split_axis=0, concat_axis=0, tiled=True)  18.9 us
    all_gather x1, blocking collectives, per_device(): all_routes = lax.all_gather(routes, EXP, axis=0, tiled=True).T  16 us
    unnamed x11, local copies, waits for them, and re-layouts  14.9 us
    all_gather x1, blocking collectives, per_device(): lines = lax.all_gather(line, 'z', axis=0, tiled=False)  14.7 us
  transfers between devices with their start and end apart: 3, of which 3 were waited for; matrix products, arithmetic and copies ran while one was open for 4% of the time, Pallas kernels for 0%

profile of v1, /device:TPU:1, one launch (start us, length us, event | category | flops | bytes accessed | tf_op | source)
XLA Modules:
  0.0 376.7 jit_solution(1945314082901564172)
XLA Ops:
  6.5 0.0 all-gather.5.cloned.1.call-start
  6.5 1.5 copy.22.decay_ref
  8.0 2.9 shard_map.110
  10.9 14.4 %all-gather = bf16[3136,128]{1,0:T(8,128)(2,1)} all-gather(bf16[784,128]{1,0:T(8,128)(2,1)} %shard_map.110), channel_id=2, replica_groups=mesh['z'=4,'y'=4,'x'=4,'core'=2] {'y'}, dimensions={0}, use_global_device_ids=true | all-gather | bytes 1003520 | tf_op jit(solution)/shard_map/all_gather | solution.py:282
  25.3 0.6 pad_add_fusion.place_ref
  25.9 2.3 shard_map.111
  28.2 14.7 %all-gather.1 = bf16[3136,128]{1,0:T(8,128)(2,1)} all-gather(bf16[784,128]{1,0:T(8,128)(2,1)} %get-tuple-element.10), channel_id=3, replica_groups=mesh['z'=4,'y'=4,'x'=4,'core'=2] {'z'}, dimensions={0}, use_global_device_ids=true | all-gather | bytes 1003520 | tf_op jit(solution)/shard_map/all_gather | solution.py:298
  43.0 3.4 shard_map.109.inner_ref
  46.4 16.0 %all-gather.2 = s32[8,32,2]{1,2,0:T(2,128)S(1)} all-gather(s32[1,32,2]{1,2,0:T(2,128)} %bitcast.14), channel_id=1, replica_groups=mesh['z'=4,'y'=4,'x'=4,'core'=2] {'x','core'}, dimensions={0}, use_global_device_ids=true | all-gather | bytes 2304 | tf_op jit(solution)/shard_map/all_gather | solution.py:278
  62.4 0.7 reshape.23
  63.1 1.3 reshape.15.gain_ref
  64.3 5.1 %shard_map.112 = (bf16[256,768]{1,0:T(8,128)(2,1)}, bf16[8,80,768]{2,1,0:T(8,128)(2,1)}) custom-call(s32[2]{0:T(128)} %pad_add_fusion.place_ref, bf16[256,768]{1,0:T(8,128)(2,1)} %query_ref.3, f32[256,6]{1,0:T(8,128)} %copy.22.decay_ref, f32[256,768]{1,0:T(8,128)} %shard_map.109.inner_ref, bf16[256,768]{1,0:T(8,128)(2,1)} %residual_ref.1, ...), custom_call_target="tpu_custom_call" | custom-call | tf_op jit(solution)/shard_map/pallas_call | solution.py:299
  69.5 18.9 %all_to_all.15.parts_ref = bf16[8,80,768]{2,1,0:T(8,128)(2,1)} all-to-all(bf16[8,80,768]{2,1,0:T(8,128)(2,1)} %get-tuple-element.13), channel_id=1, replica_groups=mesh['z'=4,'y'=4,'x'=4,'core'=2] {'x','core'}, dimensions={0} | all-to-all | bytes 1966080 | tf_op jit(solution)/shard_map/all_to_all | solution.py:320
  88.3 2.7 shard_map.113
  91.0 0.0 all-gather.5.cloned.1.call-update
  91.0 0.0 reduce-scatter.2.cloned.1.call-start
  91.1 10.6 %copy.23.up_ref = bf16[1,6144,576]{2,1,0:T(8,128)(2,1)} copy(bf16[1,6144,576]{1,2,0:T(8,128)(2,1)} %param.20) | data formatting | bytes 14155776 | tf_op args[9]
  101.7 92.4 %all-gather.5.cloned.1.call-done.rows_ref = bf16[1280,6144]{1,0:T(8,128)(2,1)} async-done(((bf16[80,6144]{1,0:T(8,128)(2,1)}), bf16[1280,6144]{1,0:T(8,128)(2,1)}) %all-gather.5.cloned.1.call-update) | async-done | bytes 15728656 | tf_op jit(solution)/shard_map/all_gather | solution.py:325
  194.1 33.3 %shard_map.114 = bf16[1280,6144]{1,0:T(8,128)(2,1)} custom-call(bf16[1280,6144]{1,0:T(8,128)(2,1)} %all-gather.5.cloned.1.call-done.rows_ref, bf16[1,6144,576]{2,1,0:T(8,128)(2,1)} %copy.23.up_ref, bf16[1,576,6144]{2,1,0:T(8,128)(2,1)} %down_ref.1), custom_call_target="tpu_custom_call" | custom-call | flops 18119393280 | bytes 45613056 | tf_op jit(solution)/shard_map/pallas_call | solution.py:215
  227.5 0.0 copy-start.1
  227.5 0.0 copy-start.2
  227.5 0.0 reduce-scatter.2.cloned.1.call-update
  227.5 105.2 %reduce-scatter.2.cloned.1.call-done = bf16[80,6144]{1,0:T(8,128)(2,1)} async-done(((bf16[1280,6144]{1,0:T(8,128)(2,1)}), bf16[80,6144]{1,0:T(8,128)(2,1)}) %reduce-scatter.2.cloned.1.call-update) | async-done | bytes 983056 | tf_op jit(solution)/shard_map/reduce_scatter | solution.py:327
  332.7 1.6 reshape.17
  334.2 19.6 %all_to_all.16 = bf16[8,480,128]{2,1,0:T(8,128)(2,1)S(1)} all-to-all(bf16[8,480,128]{2,1,0:T(8,128)(2,1)S(1)} %reshape.17), channel_id=1, replica_groups=mesh['z'=4,'y'=4,'x'=4,'core'=2] {'x','core'}, dimensions={0} | all-to-all | bytes 1966080 | tf_op jit(solution)/shard_map/all_to_all | solution.py:328
  353.8 4.3 %all-to-all-start.2 = ((bf16[8,32,768]{2,1,0:T(8,128)(2,1)}), bf16[8,32,768]{2,1,0:T(8,128)(2,1)S(1)}, u32[]{:S(2)}, u32[]{:S(2)}) async-start(bf16[8,32,768]{2,1,0:T(8,128)(2,1)} %bitcast.7), calls=%async_computation.3 | async-start | bytes 786432 | tf_op jit(solution)/shard_map/all_to_all | solution.py:321
  358.1 0.0 copy-done.1
  358.1 0.7 copy.24.routes_ref
  358.8 0.0 copy-done.2
  358.8 0.7 copy.25.weight_ref
  359.5 1.4 reshape.18.returned_ref
  360.8 5.4 %all-to-all-done.2.mixed_ref = bf16[8,32,768]{2,1,0:T(8,128)(2,1)S(1)} async-done(((bf16[8,32,768]{2,1,0:T(8,128)(2,1)}), bf16[8,32,768]{2,1,0:T(8,128)(2,1)S(1)}, u32[]{:S(2)}, u32[]{:S(2)}) %all-to-all-start.2) | async-done | bytes 393248 | tf_op jit(solution)/shard_map/all_to_all | solution.py:321
  366.2 0.0 copy-start
  366.2 0.8 copy-done
  367.0 2.9 shard_map.115
  (1 shorter events, 0.0 us)
Async XLA Ops:
  6.5 187.6 %all-gather.5.cloned.1.call-start = ((), (), s32[]{:S(2)}) async-start(), calls=%async_computation.4 | async-start | bytes 16711680 | tf_op jit(solution)/shard_map/all_gather | solution.py:325
  91.0 241.6 %reduce-scatter.2.cloned.1.call-start = ((), (), s32[]{:S(2)}) async-start(), calls=%async_computation.5 | async-start | bytes 16711680 | tf_op jit(solution)/shard_map/reduce_scatter | solution.py:327
  227.5 130.6 %copy-start.1 = (s32[32,2]{0,1:T(2,128)S(1)}, s32[32,2]{0,1:T(2,128)}, u32[]{:S(2)}) copy-start(s32[32,2]{0,1:T(2,128)} %param.18) | copy-start | bytes 772
  227.5 131.3 %copy-start.2 = (f32[32,2]{0,1:T(2,128)S(1)}, f32[32,2]{0,1:T(2,128)}, u32[]{:S(2)}) copy-start(f32[32,2]{0,1:T(2,128)} %param.19) | copy-start | bytes 772
  353.8 12.4 %all-to-all-start.2 = ((bf16[8,32,768]{2,1,0:T(8,128)(2,1)}), bf16[8,32,768]{2,1,0:T(8,128)(2,1)S(1)}, u32[]{:S(2)}, u32[]{:S(2)}) async-start(bf16[8,32,768]{2,1,0:T(8,128)(2,1)} %bitcast.7), calls=%async_computation.3 | async-start | bytes 786432 | tf_op jit(solution)/shard_map/all_to_all | solution.py:321
  366.2 0.8 copy-start
Sparse Core Ops, SparseCore 0:
  91.2 102.9 all-gather.4
  227.6 105.0 reduce-scatter.1

commit v2 on v1

v2 whole, which is shorter than its diff:
```python
import jax
import jax.numpy as jnp
from jax import lax
from jax.experimental import pallas as pl
from jax.experimental.pallas import tpu as pltpu
from jax.sharding import Mesh
from jax.sharding import PartitionSpec as P

HEAD_DIM = 128
BLK = 256
EXPERTS = 8
CAP = 10
FIRST = 8
LAST = CAP - FIRST
SIDE = 4
TILE = 256
ROWS = 32
LOG_ROWS = 16
VMEM = 56 * 1024 * 1024
F32 = jnp.float32
BF16 = jnp.bfloat16
HIGH = lax.Precision.HIGHEST
SEQ = ("z", "y")
EXP = ("x", "core")


def params():
    return pltpu.CompilerParams(vmem_limit_bytes=VMEM)


def whole():
    return pl.BlockSpec(memory_space=pltpu.VMEM)


def call(kernel, out, *args):
    many = isinstance(out, (list, tuple))
    return pl.pallas_call(
        kernel,
        out_shape=out,
        in_specs=[whole()] * len(args),
        out_specs=[whole()] * len(out) if many else whole(),
        compiler_params=params(),
    )(*args)


def shape(dims, dtype):
    return jax.ShapeDtypeStruct(dims, dtype)


def split3(value):
    first = value.astype(BF16)
    rest = value - first.astype(F32)
    second = rest.astype(BF16)
    third = (rest - second.astype(F32)).astype(BF16)
    return first, second, third


def cumulated(decay):
    row = lax.broadcasted_iota(jnp.int32, (BLK, BLK), 0)
    col = lax.broadcasted_iota(jnp.int32, (BLK, BLK), 1)
    lower = (col <= row).astype(F32)
    return lax.dot_general(
        lower, decay, (((1,), (1,)), ((), ())), preferred_element_type=F32, precision=HIGH
    )


def log_lines(logs):
    heads = logs.shape[1]
    wide = jnp.concatenate([logs, jnp.zeros((1, HEAD_DIM - heads), F32)], axis=1)
    parts = [p.astype(F32) for p in split3(wide)]
    lines = jnp.concatenate(parts + [jnp.zeros((LOG_ROWS - 3, HEAD_DIM), F32)], axis=0)
    return lines.astype(BF16)


def state_kernel(key_ref, value_ref, decay_ref, out_ref):
    heads = decay_ref.shape[0]
    cumul = cumulated(decay_ref[...])
    total = cumul[BLK - 1 :, :]
    fading = jnp.exp(total - cumul)
    for h in range(heads):
        cols = slice(h * HEAD_DIM, (h + 1) * HEAD_DIM)
        faded = (fading[:, h : h + 1] * key_ref[:, cols].astype(F32)).astype(BF16)
        own = lax.dot_general(
            faded, value_ref[:, cols], (((0,), (0,)), ((), ())), preferred_element_type=F32
        )
        out_ref[cols, :] = own.astype(BF16)
    out_ref[heads * HEAD_DIM :, :] = log_lines(total)


def inner_kernel(query_ref, key_ref, value_ref, decay_ref, out_ref):
    heads = decay_ref.shape[0]
    decay = decay_ref[...]
    cumul = cumulated(decay)
    row = lax.broadcasted_iota(jnp.int32, (BLK, BLK), 0)
    col = lax.broadcasted_iota(jnp.int32, (BLK, BLK), 1)
    upper = (row <= col).astype(F32)
    across = jnp.dot(decay, upper, preferred_element_type=F32, precision=HIGH)
    causal = col <= row
    for h in range(heads):
        cols = slice(h * HEAD_DIM, (h + 1) * HEAD_DIM)
        scores = lax.dot_general(
            query_ref[:, cols],
            key_ref[:, cols],
            (((1,), (1,)), ((), ())),
            preferred_element_type=F32,
        )
        spread = cumul[:, h : h + 1] - across[h : h + 1, :]
        weights = jnp.where(causal, jnp.exp(jnp.where(causal, spread, 0.0)) * scores, 0.0)
        out_ref[:, cols] = jnp.dot(
            weights.astype(BF16), value_ref[:, cols], preferred_element_type=F32
        )


def read_logs(ref, heads):
    rows = ref[heads * HEAD_DIM :, :].astype(F32)
    return rows[0:1] + rows[1:2] + rows[2:3]


def line_kernel(place_ref, *refs):
    states, (line_ref, before_ref, log_ref) = refs[:SIDE], refs[SIDE:]
    heads = line_ref.shape[0] // HEAD_DIM
    mine = place_ref[1]
    spots = [lax.rem(mine - d + SIDE, SIDE) for d in range(SIDE)]
    logs = [read_logs(ref, heads) for ref in states]
    to_end, to_me = [], []
    for i in range(SIDE):
        later = [jnp.where(spots[j] > spots[i], logs[j], 0.0) for j in range(SIDE)]
        between = [jnp.where(spots[j] < mine, later[j], 0.0) for j in range(SIDE)]
        to_end.append(jnp.exp(sum(later)))
        to_me.append(jnp.where(spots[i] < mine, jnp.exp(sum(between)), 0.0))
    for h in range(heads):
        rows = slice(h * HEAD_DIM, (h + 1) * HEAD_DIM)
        end = jnp.zeros((HEAD_DIM, HEAD_DIM), F32)
        me = jnp.zeros((HEAD_DIM, HEAD_DIM), F32)
        for i in range(SIDE):
            state = states[i][rows, :].astype(F32)
            end = end + to_end[i][:, h : h + 1] * state
            me = me + to_me[i][:, h : h + 1] * state
        line_ref[rows, :] = end.astype(BF16)
        before_ref[rows, :] = me
    line_ref[heads * HEAD_DIM :, :] = log_lines(sum(logs)[:, :heads])
    before = [jnp.where(spots[i] < mine, logs[i], 0.0) for i in range(SIDE)]
    log_ref[...] = jnp.broadcast_to(sum(before), log_ref.shape)


def mix_kernel(
    query_ref,
    decay_ref,
    inner_ref,
    residual_ref,
    gain_ref,
    line1_ref,
    line2_ref,
    line3_ref,
    before_ref,
    log_ref,
    routes_ref,
    mixed_ref,
    packed_ref,
):
    heads = decay_ref.shape[0]
    lines = (line1_ref, line2_ref, line3_ref)
    logs = [read_logs(ref, heads) for ref in lines]
    here = log_ref[0:1, :]
    factors = [jnp.exp(sum(logs[:i], here)) for i in range(len(lines))]
    fade = jnp.exp(cumulated(decay_ref[...]))
    for h in range(heads):
        cols = slice(h * HEAD_DIM, (h + 1) * HEAD_DIM)
        state = before_ref[cols, :]
        for factor, ref in zip(factors, lines):
            state = state + factor[:, h : h + 1] * ref[cols, :].astype(F32)
        faded = fade[:, h : h + 1] * query_ref[:, cols].astype(F32)
        attention = inner_ref[:, cols] + jnp.dot(
            faded, state, preferred_element_type=F32, precision=HIGH
        )
        square = jnp.mean(attention * attention, axis=-1, keepdims=True)
        normed = attention * lax.rsqrt(square + 1e-06) * gain_ref[:, cols]
        mixed_ref[:, cols] = (residual_ref[:, cols].astype(F32) + normed).astype(BF16)
    token = lax.broadcasted_iota(jnp.int32, (EXPERTS, BLK), 1)
    expert = lax.broadcasted_iota(jnp.int32, (EXPERTS, BLK), 0)
    names = (expert == routes_ref[0:1, :]) | (expert == routes_ref[1:2, :])
    row = lax.broadcasted_iota(jnp.int32, (BLK, BLK), 0)
    col = lax.broadcasted_iota(jnp.int32, (BLK, BLK), 1)
    earlier = ((row < col) & (row // ROWS == col // ROWS)).astype(BF16)
    rank = jnp.dot(names.astype(BF16), earlier, preferred_element_type=F32).astype(jnp.int32)
    mixed = mixed_ref[...]
    block = token // ROWS
    early = rank < FIRST
    low = block * FIRST + rank
    high = BLK // ROWS * FIRST + block * LAST + rank - FIRST
    slot = jnp.where(names, jnp.where(early, low, high), -1)
    which = lax.broadcasted_iota(jnp.int32, (packed_ref.shape[1], BLK), 0)
    for e in range(EXPERTS):
        placer = (which == slot[e : e + 1, :]).astype(BF16)
        packed_ref[e] = jnp.dot(placer, mixed, preferred_element_type=F32).astype(BF16)


def norm_kernel(parts_ref, gain_ref, first_ref, left_ref, right_ref):
    parts, _, width = parts_ref.shape
    early, half = first_ref.shape[0], parts // 2
    square = 0.0
    for j in range(parts):
        value = parts_ref[j].astype(F32)
        square = square + jnp.sum(value * value, axis=-1, keepdims=True)
    scale = lax.rsqrt(square / (parts * width) + 1e-06)
    for j in range(parts):
        cols = slice(j * width, (j + 1) * width)
        value = (parts_ref[j].astype(F32) * scale * gain_ref[:, cols]).astype(BF16)
        first_ref[:, cols] = value[:early]
        side = left_ref if j < half else right_ref
        side[:, j % half * width : (j % half + 1) * width] = value[early:]


def expert_kernel(plan, counts, refs):
    inputs, outputs, parts = counts
    ins, up, down = refs[:inputs], refs[inputs], refs[inputs + 1]
    outs = refs[inputs + 2 : inputs + 2 + outputs]
    up_here, down_here, rows_here, out_here, weight_sem, in_sem, out_sem = refs[-7:]
    tiles, wide = len(plan), up.shape[1] // parts

    def weight_up(k):
        part = pl.ds(k * wide, wide)
        return pltpu.make_async_copy(up.at[0, part], up_here.at[part], weight_sem.at[k])

    def weight_down(k):
        part = pl.ds(k * wide, wide)
        return pltpu.make_async_copy(
            down.at[0, :, part], down_here.at[:, part], weight_sem.at[parts + k]
        )

    def pieces(t, arrays, here, sems, out):
        for i, (array, index, start, count, row, col) in enumerate(plan[t]):
            far = arrays[array].at[index, pl.ds(start, count)]
            near = here.at[t % 2, pl.ds(row, count), pl.ds(col, far.shape[1])]
            pair = (near, far) if out else (far, near)
            yield pltpu.make_async_copy(*pair, sems.at[t % 2, i])

    def read(t):
        return pieces(t, ins, rows_here, in_sem, False)

    def write(t):
        return pieces(t, outs, out_here, out_sem, True)

    for copy in read(0):
        copy.start()
    for k in range(parts):
        weight_up(k).start()

    def at(t, now, action):
        @pl.when(t == now)
        def _():
            action()

    def wait(copies):
        for copy in copies:
            copy.wait()

    def begin(copies):
        for copy in copies:
            copy.start()

    def step(t, carry):
        slot = lax.rem(t, 2)
        for now in range(tiles):
            at(t, now, lambda now=now: wait(read(now)))
        value = 0.0
        for k in range(parts):
            cols = pl.ds(k * wide, wide)
            at(t, 0, lambda k=k: weight_up(k).wait())
            at(t, 0, lambda k=k: weight_down(k).start())
            value = value + jnp.dot(
                rows_here[slot, :, cols], up_here[cols, :], preferred_element_type=F32
            )
        if tiles > 1:
            at(t, 0, lambda: begin(read(1)))
        hidden = (value / (1.0 + jnp.exp(-value))).astype(BF16)
        for now in range(2, tiles):
            at(t, now, lambda now=now: wait(write(now - 2)))
        for k in range(parts):
            cols = pl.ds(k * wide, wide)
            at(t, 0, lambda k=k: weight_down(k).wait())
            out_here[slot, :, cols] = jnp.dot(
                hidden, down_here[:, cols], preferred_element_type=F32
            ).astype(BF16)
        for now in range(tiles):
            at(t, now, lambda now=now: begin(write(now)))
        for now in range(tiles - 2):
            at(t, now, lambda now=now: begin(read(now + 2)))
        return carry

    lax.fori_loop(0, tiles, step, 0)
    for t in range(max(0, tiles - 2), tiles):
        wait(write(t))


def expert_call(plan, arrays, up_weight, down_weight, tile):
    units, width = down_weight.shape[1:]
    total = len(plan) * tile
    parts = 4
    most = max(len(p) for p in plan)
    counts = (len(arrays), len(arrays), parts)
    anywhere = pl.BlockSpec(memory_space=pl.ANY)

    def kernel(*refs):
        expert_kernel(plan, counts, refs)

    return pl.pallas_call(
        kernel,
        out_shape=[shape(a.shape, BF16) for a in arrays],
        in_specs=[anywhere] * (len(arrays) + 2),
        out_specs=[anywhere] * len(arrays),
        scratch_shapes=[
            pltpu.VMEM((width, units), BF16),
            pltpu.VMEM((units, width), BF16),
            pltpu.VMEM((2, tile, width), BF16),
            pltpu.VMEM((2, tile, width), BF16),
            pltpu.SemaphoreType.DMA((2 * parts,)),
            pltpu.SemaphoreType.DMA((2, most)),
            pltpu.SemaphoreType.DMA((2, most)),
        ],
        compiler_params=params(),
        cost_estimate=pl.CostEstimate(
            flops=6 * total * width * units,
            bytes_accessed=4 * (total + units) * width,
            transcendentals=total * units,
        ),
    )(*arrays, up_weight, down_weight)


def rows_kernel(rows_ref, up_ref, down_ref, out_ref):
    value = jnp.dot(rows_ref[...], up_ref[...], preferred_element_type=F32)
    hidden = (value / (1.0 + jnp.exp(-value))).astype(BF16)
    out_ref[...] = jnp.dot(hidden, down_ref[...], preferred_element_type=F32).astype(BF16)


def expert_rows(rows, up_weight, down_weight):
    total, width = rows.shape
    units = up_weight.shape[-1]
    once = pl.Buffered(1)
    return pl.pallas_call(
        rows_kernel,
        grid=(total // TILE,),
        out_shape=shape((total, width), BF16),
        in_specs=[
            pl.BlockSpec((TILE, width), lambda i: (i, 0)),
            pl.BlockSpec((None, width, units), lambda i: (0, 0, 0), pipeline_mode=once),
            pl.BlockSpec((None, units, width), lambda i: (0, 0, 0), pipeline_mode=once),
        ],
        out_specs=pl.BlockSpec((TILE, width), lambda i: (i, 0)),
        compiler_params=params(),
        cost_estimate=pl.CostEstimate(
            flops=4 * total * width * units,
            bytes_accessed=4 * (total + units) * width,
            transcendentals=total * units,
        ),
    )(rows, up_weight, down_weight)


def expert_halves(left, right, up_weight, down_weight):
    arrays = [a for pair in left + right for a in pair]
    _, rows, half = left[0][0].shape
    plan = [[] for _ in range(SIDE * SIDE * rows // TILE)]
    for z in range(SIDE):
        for y in range(SIDE):
            done = 0
            while done < rows:
                t, row = divmod((z * SIDE + y) * rows + done, TILE)
                count = min(rows - done, TILE - row)
                plan[t].append((2 * z + y // 2, y % 2, done, count, row, 0))
                plan[t].append((2 * (SIDE + y) + z // 2, z % 2, done, count, row, half))
                done += count
    out = expert_call(plan, arrays, up_weight, down_weight, TILE)
    pairs = [(out[2 * i], out[2 * i + 1]) for i in range(2 * SIDE)]
    return pairs[:SIDE], pairs[SIDE:]


def shift(value, axis, step, count=SIDE):
    return lax.ppermute(value, axis, [(i, (i + step) % count) for i in range(count)])


def gather_near(value, axis):
    ring = [value] + [shift(value, axis, d) for d in range(1, SIDE)]
    return jnp.stack(ring[:2]), jnp.stack(ring[2:])


def gather_start(low, high, axis):
    low_after, high_before = shift(low, axis, 1), shift(high, axis, -1)
    return low_after, high_before, shift(high, axis, 1), shift(low, axis, -1)


def gather_end(low, high, started, axis):
    low_after, high_before, high_after, low_before = started
    far = (shift(low_after, axis, 1), shift(high_before, axis, -1))
    return [(low, high), (low_after, high_after), far, (low_before, high_before)]


def total_of(*terms):
    return sum(t.astype(F32) for t in terms).astype(BF16)


def scatter_near(low, high, axis):
    return total_of(
        low[0], shift(low[1], axis, -1), shift(high[0], axis, 2), shift(high[1], axis, 1)
    )


def scatter_start(value, axis):
    to_after = shift(value[2][0], axis, 1)
    to_before = shift(value[2][1], axis, -1)
    return to_after, to_before, shift(value[3][1], axis, 1), shift(value[1][0], axis, -1)


def scatter_end(value, started, axis):
    to_after, to_before, high_after, low_before = started
    low_after = shift(total_of(value[3][0], to_after), axis, 1)
    high_before = shift(total_of(value[1][1], to_before), axis, -1)
    return total_of(value[0][0], low_after, low_before), total_of(
        value[0][1], high_after, high_before
    )


def home_rows(summed):
    lines = summed.reshape(EXPERTS, -1, HEAD_DIM)
    back = lax.all_to_all(lines, EXP, split_axis=0, concat_axis=0, tiled=True)
    return back.reshape(summed.shape)


def gather_routes(routes):
    ours = lax.axis_index("core")
    other = shift(routes, "core", 1, 2)
    pair = jnp.where(ours == 0, jnp.stack([routes, other]), jnp.stack([other, routes]))
    ring = jnp.stack([pair] + [shift(pair, "x", d) for d in range(1, SIDE)])
    distance = (lax.axis_index("x") - jnp.arange(SIDE)) % SIDE
    placed = sum(
        jnp.where((distance == d)[:, None, None, None], ring[d][None], 0) for d in range(SIDE)
    )
    return jnp.transpose(placed, (2, 0, 1, 3)).reshape(2, -1)


def combine_kernel(routes_ref, weight_ref, first_ref, last_ref, mixed_ref, out_ref):
    rows = out_ref.shape[0]
    routes = routes_ref[...]
    expert = lax.broadcasted_iota(jnp.int32, (rows, EXPERTS), 1)
    names = [expert == routes[:, i : i + 1] for i in range(2)]
    row = lax.broadcasted_iota(jnp.int32, (rows, rows), 0)
    col = lax.broadcasted_iota(jnp.int32, (rows, rows), 1)
    earlier = (col < row).astype(BF16)
    ranks = jnp.dot(
        earlier, (names[0] | names[1]).astype(BF16), preferred_element_type=F32
    ).astype(jnp.int32)
    chunks = []
    for ref, low, size in ((first_ref, 0, FIRST), (last_ref, FIRST, LAST)):
        place = lax.broadcasted_iota(jnp.int32, (rows, EXPERTS * size), 1)
        blend = jnp.zeros((rows, EXPERTS * size), F32)
        for i in range(2):
            rank = jnp.sum(jnp.where(names[i], ranks, 0), axis=1, keepdims=True)
            slot = routes[:, i : i + 1] * size + rank - low
            taken = (place == slot) & (rank >= low) & (rank < low + size)
            blend = blend + jnp.where(taken, weight_ref[:, i : i + 1], 0.0)
        chunks.append((ref, split3(blend)))
    width = mixed_ref.shape[2]
    for j in range(mixed_ref.shape[0]):
        cols = slice(j * width, (j + 1) * width)
        value = mixed_ref[j].astype(F32)
        for ref, parts in chunks:
            for p in parts:
                value = value + jnp.dot(p, ref[:, cols], preferred_element_type=F32)
        out_ref[:, cols] = value.astype(BF16)


def per_device(
    queries,
    key_rows,
    value_rows,
    log_decay,
    residual,
    head_gain,
    moe_gain,
    routes,
    route_weight,
    up_weight,
    down_weight,
):
    token_count, width = queries.shape
    heads = log_decay.shape[1]
    half = moe_gain.shape[0] // 2
    model = moe_gain.shape[0]
    exp_count = model // width
    blocks = token_count // ROWS
    place = jnp.stack([lax.axis_index("z"), lax.axis_index("y")]).astype(jnp.int32)
    all_routes = gather_routes(routes.T)
    log_decay = log_decay.T

    state_rows = heads * HEAD_DIM + LOG_ROWS
    sent = call(state_kernel, shape((state_rows, HEAD_DIM), BF16), key_rows, value_rows, log_decay)
    in_line = [sent] + [shift(sent, "y", d) for d in range(1, SIDE)]
    inner = call(
        inner_kernel, shape((token_count, width), F32), queries, key_rows, value_rows, log_decay
    )
    in_line, inner, all_routes = lax.optimization_barrier((in_line, inner, all_routes))
    scalar = pl.BlockSpec(memory_space=pltpu.SMEM)
    line, before, line_log = pl.pallas_call(
        line_kernel,
        out_shape=[
            shape((state_rows, HEAD_DIM), BF16),
            shape((heads * HEAD_DIM, HEAD_DIM), F32),
            shape((8, HEAD_DIM), F32),
        ],
        in_specs=[scalar] + [whole()] * SIDE,
        out_specs=[whole()] * 3,
        compiler_params=params(),
    )(place, *in_line)
    lines = [
        lax.ppermute(line, "z", [(i, i + d) for i in range(SIDE - d)]) for d in range(1, SIDE)
    ]
    mixed, packed = pl.pallas_call(
        mix_kernel,
        out_shape=[
            shape((token_count, width), BF16),
            shape((EXPERTS, blocks * CAP, width), BF16),
        ],
        in_specs=[whole()] * 11,
        out_specs=[whole()] * 2,
        compiler_params=params(),
    )(
        queries,
        log_decay,
        inner,
        residual,
        head_gain.reshape(1, width),
        *lines,
        before,
        line_log,
        all_routes,
    )
    parts = lax.all_to_all(packed, EXP, split_axis=0, concat_axis=0, tiled=True)
    normed, left, right = call(
        norm_kernel,
        [shape((blocks * FIRST, model), BF16)] + [shape((blocks * LAST, half), BF16)] * 2,
        parts,
        moe_gain.reshape(1, model),
    )
    rows = lax.all_gather(normed, SEQ, axis=0, tiled=True)
    left, right = gather_near(left, "y"), gather_near(right, "z")
    left = gather_end(*left, gather_start(*left, "z"), "z")
    right = gather_end(*right, gather_start(*right, "y"), "y")
    left, right = expert_halves(left, right, up_weight, down_weight)
    starts = scatter_start(left, "z"), scatter_start(right, "y")
    rows, starts = lax.optimization_barrier((rows, starts))
    left = scatter_end(left, starts[0], "z")
    right = scatter_end(right, starts[1], "y")

    partial = expert_rows(rows, up_weight, down_weight)
    first = lax.psum_scatter(partial, SEQ, scatter_dimension=0, tiled=True)
    mixed, _ = lax.optimization_barrier((mixed, partial))
    home = lax.all_to_all(
        mixed.reshape(exp_count, ROWS, width), EXP, split_axis=0, concat_axis=0, tiled=True
    )
    left, right = scatter_near(*left, "y"), scatter_near(*right, "z")
    last = home_rows(jnp.concatenate([left, right], axis=1))
    first, last, home = lax.optimization_barrier((first, last, home))
    first = home_rows(first)
    return call(
        combine_kernel, shape((ROWS, model), BF16), routes, route_weight, first, last, home
    )


def solution(mesh):
    fine = Mesh(mesh.devices.reshape(4, 4, 4, 2), ("z", "y", "x", "core"))
    both = ("z", "y", "x", "core")
    return jax.shard_map(
        per_device,
        mesh=fine,
        in_specs=(
            P(SEQ, EXP),
            P(SEQ, EXP),
            P(SEQ, EXP),
            P(SEQ, EXP),
            P(SEQ, EXP),
            P(EXP),
            P(),
            P(both, None),
            P(both, None),
            P(EXP, None, SEQ),
            P(EXP, SEQ, None),
        ),
        out_specs=P(both, None),
        check_vma=False,
    )
```

time: 378 us -> 346 us (0.915)
  starting transfers between devices: 4.35 us -> 88.9 us
  waiting for transfers between devices: 203 us -> 134 us
  blocking collectives: 83.6 us -> 20.1 us
  Pallas kernels: 52.6 us -> 60.4 us
  other arithmetic: 0.61 us -> 5.27 us
  local copies, waits for them, and re-layouts: 19.1 us -> 23 us
    all_gather x1, waiting for transfers between devices: 92.4 us -> 15 us  [per_device(): rows = lax.all_gather(normed, SEQ, axis=0, tiled=True)]
    ppermute x0 -> x46, starting transfers between devices: none -> 68.1 us  [the longest x43 58.1 us: shift(): lax.ppermute(value, axis, [(i, (i + step) % count) for i in range(count)])]
    reduce_scatter x1, waiting for transfers between devices: 105 us -> 46 us  [per_device(): first = lax.psum_scatter(partial, SEQ, scatter_dimension=0, tiled=True)]
    ppermute x0 -> x46, waiting for transfers between devices: none -> 48.6 us  [the longest x43 44.3 us: shift(): lax.ppermute(value, axis, [(i, (i + step) % count) for i in range(count)])]
    all_gather x3 -> x0, blocking collectives: 45.2 us -> none  [the longest x1 16 us: per_device(): all_routes = lax.all_gather(routes, EXP, axis=0, tiled=True).T]
    all_to_all x1 -> x0, blocking collectives: 19.6 us -> none  [per_device(): lax.all_to_all(summed.reshape(exp_count, CAP * model // HEAD_DIM, HEAD_DI...]
    all_to_all x0 -> x2, waiting for transfers between devices: none -> 16.8 us  [home_rows(): back = lax.all_to_all(lines, EXP, split_axis=0, concat_axis=0, tiled=True)]
    all_to_all x0 -> x2, starting transfers between devices: none -> 16.4 us  [home_rows(): back = lax.all_to_all(lines, EXP, split_axis=0, concat_axis=0, tiled=True)]
  transfers between devices with their start and end apart: 3 -> 51, of which waited for: 3 -> 21; matrix products, arithmetic and copies ran while one was open for 4% -> 6% of each run, Pallas kernels for 0% -> 5%
where the time goes in v2:
time: 346 us; the launch traced here: 345 us
  waiting for transfers between devices  134 us (39%)
  starting transfers between devices  88.9 us (26%)
  Pallas kernels  60.4 us (17%)
  local copies, waits for them, and re-layouts  23 us (7%)
  blocking collectives  20.1 us (6%)
  between operations  13.9 us (4%)
  other arithmetic  5.27 us (2%)
    ppermute x43, starting transfers between devices, shift(): lax.ppermute(value, axis, [(i, (i + step) % count) for i in range(count)])  58.1 us
    reduce_scatter x1, waiting for transfers between devices, per_device(): first = lax.psum_scatter(partial, SEQ, scatter_dimension=0, tiled=True)  46 us
    ppermute x43, waiting for transfers between devices, shift(): lax.ppermute(value, axis, [(i, (i + step) % count) for i in range(count)])  44.3 us
    pallas_call x1, Pallas kernels, expert_rows(): pl.pallas_call(rows_kernel, grid=(total // TILE,), out_shape=shape((total...  28.2 us
    all_to_all x1, blocking collectives, per_device(): parts = lax.all_to_all(packed, EXP, split_axis=0, concat_axis=0, tiled=True)  20.1 us
    all_to_all x2, waiting for transfers between devices, home_rows(): back = lax.all_to_all(lines, EXP, split_axis=0, concat_axis=0, tiled=True)  16.8 us
    all_to_all x2, starting transfers between devices, home_rows(): back = lax.all_to_all(lines, EXP, split_axis=0, concat_axis=0, tiled=True)  16.4 us
    unnamed x69, local copies, waits for them, and re-layouts  15.7 us
  transfers between devices with their start and end apart: 51, of which 21 were waited for; matrix products, arithmetic and copies ran while one was open for 6% of the time, Pallas kernels for 5%

profile of v2, /device:TPU:1, one launch (start us, length us, event | category | flops | bytes accessed | tf_op | source)
XLA Modules:
  0.0 345.3 jit_solution(8898629538584666839)
XLA Ops:
  6.5 2.8 shard_map.109.refs_0_
  9.4 2.1 collective-permute-start
  11.5 2.6 collective-permute-start.1
  14.1 1.2 collective-permute-start.3
  16.7 3.3 shard_map.110.inner_ref
  20.8 1.2 collective-permute-start.4
  22.0 2.5 collective-permute-start.5
  24.4 1.2 collective-permute-start.6
  28.4 3.9 %collective-permute-done.2.refs_3_ = bf16[784,128]{1,0:T(8,128)(2,1)S(1)} collective-permute-done((bf16[784,128]{1,0:T(8,128)(2,1)}, bf16[784,128]{1,0:T(8,128)(2,1)S(1)}, u32[]{:S(2)}, u32[]{:S(2)}) %collective-permute-start.2) | collective-permute-done | bytes 200736 | tf_op jit(solution)/shard_map/ppermute | solution.py:378
  33.0 2.4 shard_map.111
  35.5 3.5 %collective-permute-start.7 = (bf16[784,128]{1,0:T(8,128)(2,1)}, bf16[784,128]{1,0:T(8,128)(2,1)S(1)}, u32[]{:S(2)}, u32[]{:S(2)}) collective-permute-start(bf16[784,128]{1,0:T(8,128)(2,1)} %get-tuple-element.53), channel_id=1, source_target_pairs={{0,32},{32,64},{64,96},{1,33},{33,65},{65,97},{2,34},{34,66},{66,9... | collective-permute-start | bytes 602120 | tf_op jit(solution)/shard_map/ppermute | solution.py:514
  39.0 5.2 %collective-permute-start.8 = (bf16[784,128]{1,0:T(8,128)(2,1)}, bf16[784,128]{1,0:T(8,128)(2,1)S(1)}, u32[]{:S(2)}, u32[]{:S(2)}) collective-permute-start(bf16[784,128]{1,0:T(8,128)(2,1)} %get-tuple-element.53), channel_id=1, source_target_pairs={{0,64},{32,96},{1,65},{33,97},{2,66},{34,98},{3,67},{35,99},{4,68}... | collective-permute-start | bytes 602120 | tf_op jit(solution)/shard_map/ppermute | solution.py:514
  44.2 1.3 collective-permute-start.9
  45.5 1.3 reshape.95.gain_ref
  47.2 4.0 %collective-permute-done.9.line3_ref = bf16[784,128]{1,0:T(8,128)(2,1)S(1)} collective-permute-done((bf16[784,128]{1,0:T(8,128)(2,1)}, bf16[784,128]{1,0:T(8,128)(2,1)S(1)}, u32[]{:S(2)}, u32[]{:S(2)}) %collective-permute-start.9) | collective-permute-done | bytes 200736 | tf_op jit(solution)/shard_map/ppermute | solution.py:514
  51.8 4.9 %shard_map.112 = (bf16[256,768]{1,0:T(8,128)(2,1)}, bf16[8,80,768]{2,1,0:T(8,128)(2,1)}) custom-call(bf16[256,768]{1,0:T(8,128)(2,1)} %query_ref.3, f32[6,256]{1,0:T(8,128)} %bitcast.54, f32[256,768]{1,0:T(8,128)} %shard_map.110.inner_ref, bf16[256,768]{1,0:T(8,128)(2,1)} %residual_ref.1, f32[1,768]{1,0:T(1,128)} %reshape.95.gain_ref, ...), custom_call_target="tpu_custom_call" | custom-call | tf_op jit(solution)/shard_map/pallas_call | solution.py:516
  56.8 20.1 %all_to_all.20.parts_ref = bf16[8,80,768]{2,1,0:T(8,128)(2,1)} all-to-all(bf16[8,80,768]{2,1,0:T(8,128)(2,1)} %get-tuple-element.57), channel_id=1, replica_groups=mesh['z'=4,'y'=4,'x'=4,'core'=2] {'x','core'}, dimensions={0} | all-to-all | bytes 1966080 | tf_op jit(solution)/shard_map/all_to_all | solution.py:536
  76.8 2.6 shard_map.113
  79.5 1.2 collective-permute-start.20
  80.7 2.2 collective-permute-start.21
  84.5 1.2 collective-permute-start.12
  86.3 1.1 collective-permute-done.21
  87.5 2.3 collective-permute-start.25
  90.9 2.7 collective-permute-start.27
  93.6 3.7 %collective-permute-start.16 = (bf16[2,16,3072]{2,1,0:T(8,128)(2,1)S(1)}, bf16[2,16,3072]{2,1,0:T(8,128)(2,1)S(1)}, u32[]{:S(2)}, u32[]{:S(2)}) collective-permute-start(bf16[2,16,3072]{2,1,0:T(8,128)(2,1)S(1)} %pad_maximum_fusion.1.refs_1_), channel_id=1, source_target_pairs={{0,96},{32,0},{64,32},{96,64},{1,97},{33,1},{65,33},{97,65},{2,98}... | collective-permute-start | bytes 589832 | tf_op jit(solution)/shard_map/ppermute | solution.py:378
  98.3 1.7 collective-permute-start.14
  101.1 1.4 collective-permute-start.13
  102.5 7.1 %collective-permute-done.22.refs_10_ = bf16[2,16,3072]{2,1,0:T(8,128)(2,1)S(1)} collective-permute-done((bf16[2,16,3072]{2,1,0:T(8,128)(2,1)S(1)}, bf16[2,16,3072]{2,1,0:T(8,128)(2,1)S(1)}, u32[]{:S(2)}, u32[]{:S(2)}) %collective-permute-start.22) | collective-permute-done | bytes 196640 | tf_op jit(solution)/shard_map/ppermute | solution.py:378
  109.6 3.6 %collective-permute-start.18 = (bf16[2,16,3072]{2,1,0:T(8,128)(2,1)S(1)}, bf16[2,16,3072]{2,1,0:T(8,128)(2,1)S(1)}, u32[]{:S(2)}, u32[]{:S(2)}) collective-permute-start(bf16[2,16,3072]{2,1,0:T(8,128)(2,1)S(1)} %pad_maximum_fusion.refs_0_), channel_id=1, source_target_pairs={{0,96},{32,0},{64,32},{96,64},{1,97},{33,1},{65,33},{97,65},{2,98}... | collective-permute-start | bytes 589832 | tf_op jit(solution)/shard_map/ppermute | solution.py:378
  113.2 1.4 collective-permute-start.24
  114.7 1.4 collective-permute-start.15
  116.1 10.6 %copy.24.refs_16_.up_ref = bf16[1,6144,576]{2,1,0:T(8,128)(2,1)} copy(bf16[1,6144,576]{1,2,0:T(8,128)(2,1)} %param.20) | data formatting | bytes 14155776 | tf_op args[9]
  128.3 12.8 %shard_map.114 = (bf16[2,16,3072]{2,1,0:T(8,128)(2,1)}, bf16[2,16,3072]{2,1,0:T(8,128)(2,1)}, bf16[2,16,3072]{2,1,0:T(8,128)(2,1)}, bf16[2,16,3072]{2,1,0:T(8,12...) custom-call(bf16[2,16,3072]{2,1,0:T(8,128)(2,1)} %copy-done.10, ...), custom_call_target="tpu_custom_call" | custom-call | flops 5435817984 | bytes 20447232 | tf_op jit(solution)/shard_map/pallas_call | solution.py:307
  141.2 2.7 collective-permute-start.29
  143.9 2.7 collective-permute-start.31
  146.6 5.9 %collective-permute-done.28 = bf16[2,16,3072]{2,1,0:T(8,128)(2,1)S(1)} collective-permute-done((bf16[2,16,3072]{2,1,0:T(8,128)(2,1)}, bf16[2,16,3072]{2,1,0:T(8,128)(2,1)S(1)}, u32[]{:S(2)}, u32[]{:S(2)}) %collective-permute-start.28) | collective-permute-done | bytes 196640 | tf_op jit(solution)/shard_map/ppermute | solution.py:378
  152.5 2.1 collective-permute-start.33
  154.6 6.3 %collective-permute-done.30 = bf16[2,16,3072]{2,1,0:T(8,128)(2,1)S(1)} collective-permute-done((bf16[2,16,3072]{2,1,0:T(8,128)(2,1)}, bf16[2,16,3072]{2,1,0:T(8,128)(2,1)S(1)}, u32[]{:S(2)}, u32[]{:S(2)}) %collective-permute-start.30) | collective-permute-done | bytes 196640 | tf_op jit(solution)/shard_map/ppermute | solution.py:378
  160.9 2.1 collective-permute-start.35
  163.0 3.8 %collective-permute-done.34 = bf16[2,16,3072]{2,1,0:T(8,128)(2,1)S(1)} collective-permute-done((bf16[2,16,3072]{2,1,0:T(8,128)(2,1)}, bf16[2,16,3072]{2,1,0:T(8,128)(2,1)S(1)}, u32[]{:S(2)}, u32[]{:S(2)}) %collective-permute-start.34) | collective-permute-done | bytes 196640 | tf_op jit(solution)/shard_map/ppermute | solution.py:378
  166.8 5.5 %collective-permute-done.35 = bf16[2,16,3072]{2,1,0:T(8,128)(2,1)S(1)} collective-permute-done((bf16[2,16,3072]{2,1,0:T(8,128)(2,1)}, bf16[2,16,3072]{2,1,0:T(8,128)(2,1)S(1)}, u32[]{:S(2)}, u32[]{:S(2)}) %collective-permute-start.35) | collective-permute-done | bytes 196640 | tf_op jit(solution)/shard_map/ppermute | solution.py:378
  172.3 15.0 %all-gather.2.cloned.1.call-done.rows_ref = bf16[1024,6144]{1,0:T(8,128)(2,1)} async-done(((bf16[64,6144]{1,0:T(8,128)(2,1)}), bf16[1024,6144]{1,0:T(8,128)(2,1)}) %all-gather.2.cloned.1.call-update) | async-done | bytes 12582928 | tf_op jit(solution)/shard_map/all_gather | solution.py:543
  187.3 28.2 %shard_map.115 = bf16[1024,6144]{1,0:T(8,128)(2,1)} custom-call(bf16[1024,6144]{1,0:T(8,128)(2,1)} %all-gather.2.cloned.1.call-done.rows_ref, bf16[1,6144,576]{2,1,0:T(8,128)(2,1)} %copy.24.refs_16_.up_ref, bf16[1,576,6144]{2,1,0:T(8,128)(2,1)} %down_ref.1), custom_call_target="tpu_custom_call" | custom-call | flops 14495514624 | bytes 39321600 | tf_op jit(solution)/shard_map/pallas_call | solution.py:340
  216.5 1.2 collective-permute-start.36
  217.7 1.6 collective-permute-start.38
  219.4 1.3 collective-permute-start.41
  220.7 1.5 collective-permute-start.43
  222.3 1.3 collective-permute-done.36
  223.6 2.5 collective-permute-start.37
  227.6 1.8 collective-permute-start.42
  229.6 1.5 collective-permute-done.37
  231.1 2.9 collective-permute-done.39
  233.9 2.4 collective-permute-done.40
  236.5 1.4 collective-permute-done.45
  238.8 11.2 %all-to-all-start.1 = ((bf16[8,96,128]{2,1,0:T(8,128)(2,1)}), bf16[8,96,128]{2,1,0:T(8,128)(2,1)S(1)}, u32[]{:S(2)}, u32[]{:S(2)}) async-start(bf16[8,96,128]{2,1,0:T(8,128)(2,1)} %reshape.97), calls=%async_computation.2 | async-start | bytes 393216 | tf_op jit(solution)/shard_map/all_to_all | solution.py:424
  250.0 5.9 %all-to-all-done.1 = bf16[8,96,128]{2,1,0:T(8,128)(2,1)S(1)} async-done(((bf16[8,96,128]{2,1,0:T(8,128)(2,1)}), bf16[8,96,128]{2,1,0:T(8,128)(2,1)S(1)}, u32[]{:S(2)}, u32[]{:S(2)}) %all-to-all-start.1) | async-done | bytes 196640 | tf_op jit(solution)/shard_map/all_to_all | solution.py:424
  255.9 4.3 %all-to-all-start.2 = ((bf16[8,32,768]{2,1,0:T(8,128)(2,1)}), bf16[8,32,768]{2,1,0:T(8,128)(2,1)S(1)}, u32[]{:S(2)}, u32[]{:S(2)}) async-start(bf16[8,32,768]{2,1,0:T(8,128)(2,1)} %bitcast.28), calls=%async_computation.3 | async-start | bytes 786432 | tf_op jit(solution)/shard_map/all_to_all | solution.py:556
  261.0 7.3 %all-to-all-done.2.mixed_ref = bf16[8,32,768]{2,1,0:T(8,128)(2,1)S(1)} async-done(((bf16[8,32,768]{2,1,0:T(8,128)(2,1)}), bf16[8,32,768]{2,1,0:T(8,128)(2,1)S(1)}, u32[]{:S(2)}, u32[]{:S(2)}) %all-to-all-start.2) | async-done | bytes 393248 | tf_op jit(solution)/shard_map/all_to_all | solution.py:556
  268.3 46.0 %reduce-scatter.2.cloned.1.call-done = bf16[64,6144]{1,0:T(8,128)(2,1)} async-done(((bf16[1024,6144]{1,0:T(8,128)(2,1)}), bf16[64,6144]{1,0:T(8,128)(2,1)}) %reduce-scatter.2.cloned.1.call-update) | async-done | bytes 786448 | tf_op jit(solution)/shard_map/reduce_scatter | solution.py:554
  314.3 2.2 reshape.100
  316.5 5.2 %all-to-all-start.3 = ((bf16[8,384,128]{2,1,0:T(8,128)(2,1)}), bf16[8,384,128]{2,1,0:T(8,128)(2,1)S(1)}, u32[]{:S(2)}, u32[]{:S(2)}) async-start(bf16[8,384,128]{2,1,0:T(8,128)(2,1)} %reshape.100), calls=%async_computation.4 | async-start | bytes 1572864 | tf_op jit(solution)/shard_map/all_to_all | solution.py:424
  323.1 10.9 %all-to-all-done.3 = bf16[8,384,128]{2,1,0:T(8,128)(2,1)S(1)} async-done(((bf16[8,384,128]{2,1,0:T(8,128)(2,1)}), bf16[8,384,128]{2,1,0:T(8,128)(2,1)S(1)}, u32[]{:S(2)}, u32[]{:S(2)}) %all-to-all-start.3) | async-done | bytes 786464 | tf_op jit(solution)/shard_map/all_to_all | solution.py:424
  334.0 1.2 reshape.101.first_ref
  335.2 3.2 shard_map.116
  (168 shorter events, 19.4 us)
Async XLA Ops:
  6.5 180.7 %all-gather.2.cloned.1.call-start = ((), (), s32[]{:S(2)}) async-start(), calls=%async_computation.5 | async-start | bytes 13369344 | tf_op jit(solution)/shard_map/all_gather | solution.py:543
  9.4 19.0 %collective-permute-start = (bf16[784,128]{1,0:T(8,128)(2,1)}, bf16[784,128]{1,0:T(8,128)(2,1)S(1)}, u32[]{:S(2)}, u32[]{:S(2)}) collective-permute-start(bf16[784,128]{1,0:T(8,128)(2,1)} %shard_map.109.refs_0_), channel_id=1, source_target_pairs={{0,8},{8,16},{16,24},{24,0},{1,9},{9,17},{17,25},{25,1},{2,10},{10... | collective-permute-start | bytes 602120 | tf_op jit(solution)/shard_map/ppermute | solution.py:378
  11.5 16.9 %collective-permute-start.1 = (bf16[784,128]{1,0:T(8,128)(2,1)}, bf16[784,128]{1,0:T(8,128)(2,1)S(1)}, u32[]{:S(2)}, u32[]{:S(2)}) collective-permute-start(bf16[784,128]{1,0:T(8,128)(2,1)} %shard_map.109.refs_0_), channel_id=1, source_target_pairs={{0,16},{8,24},{16,0},{24,8},{1,17},{9,25},{17,1},{25,9},{2,18},{10... | collective-permute-start | bytes 602120 | tf_op jit(solution)/shard_map/ppermute | solution.py:378
  14.1 5.9 %collective-permute-start.3 = (s32[2,32]{1,0:T(2,128)}, s32[2,32]{1,0:T(2,128)S(1)}, u32[]{:S(2)}, u32[]{:S(2)}) collective-permute-start(s32[2,32]{1,0:T(2,128)} %bitcast.56), channel_id=1, source_target_pairs={{0,1},{1,0},{2,3},{3,2},{4,5},{5,4},{6,7},{7,6},{8,9},{9,8},{10,11... | collective-permute-start | bytes 776 | tf_op jit(solution)/shard_map/ppermute | solution.py:378
  20.8 5.7 %collective-permute-start.4 = (s32[2,2,32]{2,1,0:T(2,128)S(1)}, s32[2,2,32]{2,1,0:T(2,128)S(1)}, u32[]{:S(2)}, u32[]{:S(2)}) collective-permute-start(s32[2,2,32]{2,1,0:T(2,128)S(1)} %add_select_fusion), channel_id=1, source_target_pairs={{0,2},{2,4},{4,6},{6,0},{1,3},{3,5},{5,7},{7,1},{8,10},{10,12},{12... | collective-permute-start | bytes 1544 | tf_op jit(solution)/shard_map/ppermute | solution.py:378
  22.0 5.6 %collective-permute-start.5 = (s32[2,2,32]{2,1,0:T(2,128)S(1)}, s32[2,2,32]{2,1,0:T(2,128)S(1)}, u32[]{:S(2)}, u32[]{:S(2)}) collective-permute-start(s32[2,2,32]{2,1,0:T(2,128)S(1)} %add_select_fusion), channel_id=1, source_target_pairs={{0,4},{2,6},{4,0},{6,2},{1,5},{3,7},{5,1},{7,3},{8,12},{10,14},{12... | collective-permute-start | bytes 1544 | tf_op jit(solution)/shard_map/ppermute | solution.py:378
  24.4 3.3 collective-permute-start.6
  26.4 5.9 %collective-permute-start.2 = (bf16[784,128]{1,0:T(8,128)(2,1)}, bf16[784,128]{1,0:T(8,128)(2,1)S(1)}, u32[]{:S(2)}, u32[]{:S(2)}) collective-permute-start(bf16[784,128]{1,0:T(8,128)(2,1)} %shard_map.109.refs_0_), channel_id=1, source_target_pairs={{0,24},{8,0},{16,8},{24,16},{1,25},{9,1},{17,9},{25,17},{2,26},{10... | collective-permute-start | bytes 602120 | tf_op jit(solution)/shard_map/ppermute | solution.py:378
  35.5 11.4 %collective-permute-start.7 = (bf16[784,128]{1,0:T(8,128)(2,1)}, bf16[784,128]{1,0:T(8,128)(2,1)S(1)}, u32[]{:S(2)}, u32[]{:S(2)}) collective-permute-start(bf16[784,128]{1,0:T(8,128)(2,1)} %get-tuple-element.53), channel_id=1, source_target_pairs={{0,32},{32,64},{64,96},{1,33},{33,65},{65,97},{2,34},{34,66},{66,9... | collective-permute-start | bytes 602120 | tf_op jit(solution)/shard_map/ppermute | solution.py:514
  39.0 8.2 %collective-permute-start.8 = (bf16[784,128]{1,0:T(8,128)(2,1)}, bf16[784,128]{1,0:T(8,128)(2,1)S(1)}, u32[]{:S(2)}, u32[]{:S(2)}) collective-permute-start(bf16[784,128]{1,0:T(8,128)(2,1)} %get-tuple-element.53), channel_id=1, source_target_pairs={{0,64},{32,96},{1,65},{33,97},{2,66},{34,98},{3,67},{35,99},{4,68}... | collective-permute-start | bytes 602120 | tf_op jit(solution)/shard_map/ppermute | solution.py:514
  44.2 6.9 %collective-permute-start.9 = (bf16[784,128]{1,0:T(8,128)(2,1)}, bf16[784,128]{1,0:T(8,128)(2,1)S(1)}, u32[]{:S(2)}, u32[]{:S(2)}) collective-permute-start(bf16[784,128]{1,0:T(8,128)(2,1)} %get-tuple-element.53), channel_id=1, source_target_pairs={{0,96},{1,97},{2,98},{3,99},{4,100},{5,101},{6,102},{7,103},{8,104... | collective-permute-start | bytes 602120 | tf_op jit(solution)/shard_map/ppermute | solution.py:514
  79.4 234.9 %reduce-scatter.2.cloned.1.call-start = ((), (), s32[]{:S(2)}) async-start(), calls=%async_computation.6 | async-start | bytes 13369344 | tf_op jit(solution)/shard_map/reduce_scatter | solution.py:554
  79.5 6.3 %collective-permute-start.20 = (bf16[16,3072]{1,0:T(8,128)(2,1)}, bf16[16,3072]{1,0:T(8,128)(2,1)S(1)}, u32[]{:S(2)}, u32[]{:S(2)}) collective-permute-start(bf16[16,3072]{1,0:T(8,128)(2,1)} %get-tuple-element.60), channel_id=1, source_target_pairs={{0,64},{32,96},{64,0},{96,32},{1,65},{33,97},{65,1},{97,33},{2,66}... | collective-permute-start | bytes 294920 | tf_op jit(solution)/shard_map/ppermute | solution.py:378
  80.7 6.7 %collective-permute-start.21 = (bf16[16,3072]{1,0:T(8,128)(2,1)}, bf16[16,3072]{1,0:T(8,128)(2,1)S(1)}, u32[]{:S(2)}, u32[]{:S(2)}) collective-permute-start(bf16[16,3072]{1,0:T(8,128)(2,1)} %get-tuple-element.60), channel_id=1, source_target_pairs={{0,96},{32,0},{64,32},{96,64},{1,97},{33,1},{65,33},{97,65},{2,98}... | collective-permute-start | bytes 294920 | tf_op jit(solution)/shard_map/ppermute | solution.py:378
  82.9 6.9 %collective-permute-start.19 = (bf16[16,3072]{1,0:T(8,128)(2,1)}, bf16[16,3072]{1,0:T(8,128)(2,1)S(1)}, u32[]{:S(2)}, u32[]{:S(2)}) collective-permute-start(bf16[16,3072]{1,0:T(8,128)(2,1)} %get-tuple-element.60), channel_id=1, source_target_pairs={{0,32},{32,64},{64,96},{96,0},{1,33},{33,65},{65,97},{97,1},{2,34}... | collective-permute-start | bytes 294920 | tf_op jit(solution)/shard_map/ppermute | solution.py:378
  83.4 7.3 %collective-permute-start.11 = (bf16[16,3072]{1,0:T(8,128)(2,1)}, bf16[16,3072]{1,0:T(8,128)(2,1)S(1)}, u32[]{:S(2)}, u32[]{:S(2)}) collective-permute-start(bf16[16,3072]{1,0:T(8,128)(2,1)} %get-tuple-element.59), channel_id=1, source_target_pairs={{0,16},{8,24},{16,0},{24,8},{1,17},{9,25},{17,1},{25,9},{2,18},{10... | collective-permute-start | bytes 294920 | tf_op jit(solution)/shard_map/ppermute | solution.py:378
  84.5 6.3 %collective-permute-start.12 = (bf16[16,3072]{1,0:T(8,128)(2,1)}, bf16[16,3072]{1,0:T(8,128)(2,1)S(1)}, u32[]{:S(2)}, u32[]{:S(2)}) collective-permute-start(bf16[16,3072]{1,0:T(8,128)(2,1)} %get-tuple-element.59), channel_id=1, source_target_pairs={{0,24},{8,0},{16,8},{24,16},{1,25},{9,1},{17,9},{25,17},{2,26},{10... | collective-permute-start | bytes 294920 | tf_op jit(solution)/shard_map/ppermute | solution.py:378
  85.7 7.9 %collective-permute-start.10 = (bf16[16,3072]{1,0:T(8,128)(2,1)}, bf16[16,3072]{1,0:T(8,128)(2,1)S(1)}, u32[]{:S(2)}, u32[]{:S(2)}) collective-permute-start(bf16[16,3072]{1,0:T(8,128)(2,1)} %get-tuple-element.59), channel_id=1, source_target_pairs={{0,8},{8,16},{16,24},{24,0},{1,9},{9,17},{17,25},{25,1},{2,10},{10... | collective-permute-start | bytes 294920 | tf_op jit(solution)/shard_map/ppermute | solution.py:378
  87.5 39.3 %copy-start.7 = (bf16[2,16,3072]{2,1,0:T(8,128)(2,1)}, bf16[2,16,3072]{2,1,0:T(8,128)(2,1)S(1)}, u32[]{:S(2)}) copy-start(bf16[2,16,3072]{2,1,0:T(8,128)(2,1)S(1)} %pad_maximum_fusion.3.refs_9_) | copy-start | bytes 589828
  87.5 10.9 %collective-permute-start.25 = (bf16[2,16,3072]{2,1,0:T(8,128)(2,1)S(1)}, bf16[2,16,3072]{2,1,0:T(8,128)(2,1)S(1)}, u32[]{:S(2)}, u32[]{:S(2)}) collective-permute-start(bf16[2,16,3072]{2,1,0:T(8,128)(2,1)S(1)} %pad_maximum_fusion.3.refs_9_), channel_id=1, source_target_pairs={{0,24},{8,0},{16,8},{24,16},{1,25},{9,1},{17,9},{25,17},{2,26},{10... | collective-permute-start | bytes 589832 | tf_op jit(solution)/shard_map/ppermute | solution.py:378
  89.8 11.3 %collective-permute-start.23 = (bf16[2,16,3072]{2,1,0:T(8,128)(2,1)S(1)}, bf16[2,16,3072]{2,1,0:T(8,128)(2,1)S(1)}, u32[]{:S(2)}, u32[]{:S(2)}) collective-permute-start(bf16[2,16,3072]{2,1,0:T(8,128)(2,1)S(1)} %pad_maximum_fusion.3.refs_9_), channel_id=1, source_target_pairs={{0,8},{8,16},{16,24},{24,0},{1,9},{9,17},{17,25},{25,1},{2,10},{10... | collective-permute-start | bytes 589832 | tf_op jit(solution)/shard_map/ppermute | solution.py:378
  90.7 36.0 %copy-start.8 = (bf16[2,16,3072]{2,1,0:T(8,128)(2,1)}, bf16[2,16,3072]{2,1,0:T(8,128)(2,1)S(1)}, u32[]{:S(2)}) copy-start(bf16[2,16,3072]{2,1,0:T(8,128)(2,1)S(1)} %pad_maximum_fusion.2.refs_8_) | copy-start | bytes 589828
  90.8 18.8 %collective-permute-start.22 = (bf16[2,16,3072]{2,1,0:T(8,128)(2,1)S(1)}, bf16[2,16,3072]{2,1,0:T(8,128)(2,1)S(1)}, u32[]{:S(2)}, u32[]{:S(2)}) collective-permute-start(bf16[2,16,3072]{2,1,0:T(8,128)(2,1)S(1)} %pad_maximum_fusion.2.refs_8_), channel_id=1, source_target_pairs={{0,8},{8,16},{16,24},{24,0},{1,9},{9,17},{17,25},{25,1},{2,10},{10... | collective-permute-start | bytes 589832 | tf_op jit(solution)/shard_map/ppermute | solution.py:378
  90.9 22.3 %collective-permute-start.27 = (bf16[2,16,3072]{2,1,0:T(8,128)(2,1)S(1)}, bf16[2,16,3072]{2,1,0:T(8,128)(2,1)S(1)}, u32[]{:S(2)}, u32[]{:S(2)}) collective-permute-start(bf16[2,16,3072]{2,1,0:T(8,128)(2,1)S(1)} %pad_maximum_fusion.2.refs_8_), channel_id=1, source_target_pairs={{0,24},{8,0},{16,8},{24,16},{1,25},{9,1},{17,9},{25,17},{2,26},{10... | collective-permute-start | bytes 589832 | tf_op jit(solution)/shard_map/ppermute | solution.py:378
  93.6 33.2 %copy-start.9 = (bf16[2,16,3072]{2,1,0:T(8,128)(2,1)}, bf16[2,16,3072]{2,1,0:T(8,128)(2,1)S(1)}, u32[]{:S(2)}) copy-start(bf16[2,16,3072]{2,1,0:T(8,128)(2,1)S(1)} %pad_maximum_fusion.1.refs_1_) | copy-start | bytes 589828
  93.6 19.5 %collective-permute-start.16 = (bf16[2,16,3072]{2,1,0:T(8,128)(2,1)S(1)}, bf16[2,16,3072]{2,1,0:T(8,128)(2,1)S(1)}, u32[]{:S(2)}, u32[]{:S(2)}) collective-permute-start(bf16[2,16,3072]{2,1,0:T(8,128)(2,1)S(1)} %pad_maximum_fusion.1.refs_1_), channel_id=1, source_target_pairs={{0,96},{32,0},{64,32},{96,64},{1,97},{33,1},{65,33},{97,65},{2,98}... | collective-permute-start | bytes 589832 | tf_op jit(solution)/shard_map/ppermute | solution.py:378
  98.3 28.6 %copy-start.10 = (bf16[2,16,3072]{2,1,0:T(8,128)(2,1)}, bf16[2,16,3072]{2,1,0:T(8,128)(2,1)S(1)}, u32[]{:S(2)}) copy-start(bf16[2,16,3072]{2,1,0:T(8,128)(2,1)S(1)} %pad_maximum_fusion.refs_0_) | copy-start | bytes 589828
  98.3 28.5 %copy-start.21 = (bf16[2,16,3072]{2,1,0:T(8,128)(2,1)}, bf16[2,16,3072]{2,1,0:T(8,128)(2,1)S(1)}, u32[]{:S(2)}) copy-start(bf16[2,16,3072]{2,1,0:T(8,128)(2,1)S(1)} %collective-permute-done.25.refs_15_) | copy-start | bytes 589828
  98.3 16.3 %collective-permute-start.14 = (bf16[2,16,3072]{2,1,0:T(8,128)(2,1)S(1)}, bf16[2,16,3072]{2,1,0:T(8,128)(2,1)S(1)}, u32[]{:S(2)}, u32[]{:S(2)}) collective-permute-start(bf16[2,16,3072]{2,1,0:T(8,128)(2,1)S(1)} %pad_maximum_fusion.1.refs_1_), channel_id=1, source_target_pairs={{0,32},{32,64},{64,96},{96,0},{1,33},{33,65},{65,97},{97,1},{2,34}... | collective-permute-start | bytes 589832 | tf_op jit(solution)/shard_map/ppermute | solution.py:378
  101.1 25.7 %copy-start.22 = (bf16[2,16,3072]{2,1,0:T(8,128)(2,1)}, bf16[2,16,3072]{2,1,0:T(8,128)(2,1)S(1)}, u32[]{:S(2)}) copy-start(bf16[2,16,3072]{2,1,0:T(8,128)(2,1)S(1)} %collective-permute-done.23.refs_11_) | copy-start | bytes 589828
  101.1 13.6 %collective-permute-start.13 = (bf16[2,16,3072]{2,1,0:T(8,128)(2,1)S(1)}, bf16[2,16,3072]{2,1,0:T(8,128)(2,1)S(1)}, u32[]{:S(2)}, u32[]{:S(2)}) collective-permute-start(bf16[2,16,3072]{2,1,0:T(8,128)(2,1)S(1)} %pad_maximum_fusion.refs_0_), channel_id=1, source_target_pairs={{0,32},{32,64},{64,96},{96,0},{1,33},{33,65},{65,97},{97,1},{2,34}... | collective-permute-start | bytes 589832 | tf_op jit(solution)/shard_map/ppermute | solution.py:378
  109.6 17.3 %copy-start.23 = (bf16[2,16,3072]{2,1,0:T(8,128)(2,1)}, bf16[2,16,3072]{2,1,0:T(8,128)(2,1)S(1)}, u32[]{:S(2)}) copy-start(bf16[2,16,3072]{2,1,0:T(8,128)(2,1)S(1)} %collective-permute-done.22.refs_10_) | copy-start | bytes 589828
  109.6 17.2 %collective-permute-start.18 = (bf16[2,16,3072]{2,1,0:T(8,128)(2,1)S(1)}, bf16[2,16,3072]{2,1,0:T(8,128)(2,1)S(1)}, u32[]{:S(2)}, u32[]{:S(2)}) collective-permute-start(bf16[2,16,3072]{2,1,0:T(8,128)(2,1)S(1)} %pad_maximum_fusion.refs_0_), channel_id=1, source_target_pairs={{0,96},{32,0},{64,32},{96,64},{1,97},{33,1},{65,33},{97,65},{2,98}... | collective-permute-start | bytes 589832 | tf_op jit(solution)/shard_map/ppermute | solution.py:378
  113.2 13.7 %copy-start.24 = (bf16[2,16,3072]{2,1,0:T(8,128)(2,1)}, bf16[2,16,3072]{2,1,0:T(8,128)(2,1)S(1)}, u32[]{:S(2)}) copy-start(bf16[2,16,3072]{2,1,0:T(8,128)(2,1)S(1)} %collective-permute-done.27.refs_14_) | copy-start | bytes 589828
  113.2 13.6 %collective-permute-start.26 = (bf16[2,16,3072]{2,1,0:T(8,128)(2,1)S(1)}, bf16[2,16,3072]{2,1,0:T(8,128)(2,1)S(1)}, u32[]{:S(2)}, u32[]{:S(2)}) collective-permute-start(bf16[2,16,3072]{2,1,0:T(8,128)(2,1)S(1)} %collective-permute-done.25.refs_15_), channel_id=1, source_target_pairs={{0,24},{8,0},{16,8},{24,16},{1,25},{9,1},{17,9},{25,17},{2,26},{10... | collective-permute-start | bytes 589832 | tf_op jit(solution)/shard_map/ppermute | solution.py:378
  113.2 13.7 %copy-start.25 = (bf16[2,16,3072]{2,1,0:T(8,128)(2,1)}, bf16[2,16,3072]{2,1,0:T(8,128)(2,1)S(1)}, u32[]{:S(2)}) copy-start(bf16[2,16,3072]{2,1,0:T(8,128)(2,1)S(1)} %collective-permute-done.16.refs_7_) | copy-start | bytes 589828
  113.2 13.6 %collective-permute-start.24 = (bf16[2,16,3072]{2,1,0:T(8,128)(2,1)S(1)}, bf16[2,16,3072]{2,1,0:T(8,128)(2,1)S(1)}, u32[]{:S(2)}, u32[]{:S(2)}) collective-permute-start(bf16[2,16,3072]{2,1,0:T(8,128)(2,1)S(1)} %collective-permute-done.22.refs_10_), channel_id=1, source_target_pairs={{0,8},{8,16},{16,24},{24,0},{1,9},{9,17},{17,25},{25,1},{2,10},{10... | collective-permute-start | bytes 589832 | tf_op jit(solution)/shard_map/ppermute | solution.py:378
  114.6 12.2 %collective-permute-start.17 = (bf16[2,16,3072]{2,1,0:T(8,128)(2,1)S(1)}, bf16[2,16,3072]{2,1,0:T(8,128)(2,1)S(1)}, u32[]{:S(2)}, u32[]{:S(2)}) collective-permute-start(bf16[2,16,3072]{2,1,0:T(8,128)(2,1)S(1)} %collective-permute-done.16.refs_7_), channel_id=1, source_target_pairs={{0,96},{32,0},{64,32},{96,64},{1,97},{33,1},{65,33},{97,65},{2,98}... | collective-permute-start | bytes 589832 | tf_op jit(solution)/shard_map/ppermute | solution.py:378
  114.7 12.1 %collective-permute-start.15 = (bf16[2,16,3072]{2,1,0:T(8,128)(2,1)S(1)}, bf16[2,16,3072]{2,1,0:T(8,128)(2,1)S(1)}, u32[]{:S(2)}, u32[]{:S(2)}) collective-permute-start(bf16[2,16,3072]{2,1,0:T(8,128)(2,1)S(1)} %collective-permute-done.13.refs_2_), channel_id=1, source_target_pairs={{0,32},{32,64},{64,96},{96,0},{1,33},{33,65},{65,97},{97,1},{2,34}... | collective-permute-start | bytes 589832 | tf_op jit(solution)/shard_map/ppermute | solution.py:378
  141.1 11.3 %collective-permute-start.28 = (bf16[2,16,3072]{2,1,0:T(8,128)(2,1)}, bf16[2,16,3072]{2,1,0:T(8,128)(2,1)S(1)}, u32[]{:S(2)}, u32[]{:S(2)}) collective-permute-start(bf16[2,16,3072]{2,1,0:T(8,128)(2,1)} %get-tuple-element.61), channel_id=1, source_target_pairs={{0,32},{32,64},{64,96},{96,0},{1,33},{33,65},{65,97},{97,1},{2,34}... | collective-permute-start | bytes 589832 | tf_op jit(solution)/shard_map/ppermute | solution.py:378
  141.2 13.3 %collective-permute-start.29 = (bf16[2,16,3072]{2,1,0:T(8,128)(2,1)}, bf16[2,16,3072]{2,1,0:T(8,128)(2,1)S(1)}, u32[]{:S(2)}, u32[]{:S(2)}) collective-permute-start(bf16[2,16,3072]{2,1,0:T(8,128)(2,1)} %get-tuple-element.62), channel_id=1, source_target_pairs={{0,96},{32,0},{64,32},{96,64},{1,97},{33,1},{65,33},{97,65},{2,98}... | collective-permute-start | bytes 589832 | tf_op jit(solution)/shard_map/ppermute | solution.py:378
  143.9 17.0 %collective-permute-start.30 = (bf16[2,16,3072]{2,1,0:T(8,128)(2,1)}, bf16[2,16,3072]{2,1,0:T(8,128)(2,1)S(1)}, u32[]{:S(2)}, u32[]{:S(2)}) collective-permute-start(bf16[2,16,3072]{2,1,0:T(8,128)(2,1)} %get-tuple-element.63), channel_id=1, source_target_pairs={{0,32},{32,64},{64,96},{96,0},{1,33},{33,65},{65,97},{97,1},{2,34}... | collective-permute-start | bytes 589832 | tf_op jit(solution)/shard_map/ppermute | solution.py:378
  143.9 19.1 %collective-permute-start.31 = (bf16[2,16,3072]{2,1,0:T(8,128)(2,1)}, bf16[2,16,3072]{2,1,0:T(8,128)(2,1)S(1)}, u32[]{:S(2)}, u32[]{:S(2)}) collective-permute-start(bf16[2,16,3072]{2,1,0:T(8,128)(2,1)} %get-tuple-element.64), channel_id=1, source_target_pairs={{0,96},{32,0},{64,32},{96,64},{1,97},{33,1},{65,33},{97,65},{2,98}... | collective-permute-start | bytes 589832 | tf_op jit(solution)/shard_map/ppermute | solution.py:378
  146.6 16.4 %collective-permute-start.32 = (bf16[2,16,3072]{2,1,0:T(8,128)(2,1)}, bf16[2,16,3072]{2,1,0:T(8,128)(2,1)S(1)}, u32[]{:S(2)}, u32[]{:S(2)}) collective-permute-start(bf16[2,16,3072]{2,1,0:T(8,128)(2,1)} %get-tuple-element.65), channel_id=1, source_target_pairs={{0,8},{8,16},{16,24},{24,0},{1,9},{9,17},{17,25},{25,1},{2,10},{10... | collective-permute-start | bytes 589832 | tf_op jit(solution)/shard_map/ppermute | solution.py:378
  152.5 10.5 %collective-permute-start.33 = (bf16[2,16,3072]{2,1,0:T(8,128)(2,1)}, bf16[2,16,3072]{2,1,0:T(8,128)(2,1)S(1)}, u32[]{:S(2)}, u32[]{:S(2)}) collective-permute-start(bf16[2,16,3072]{2,1,0:T(8,128)(2,1)} %get-tuple-element.66), channel_id=1, source_target_pairs={{0,24},{8,0},{16,8},{24,16},{1,25},{9,1},{17,9},{25,17},{2,26},{10... | collective-permute-start | bytes 589832 | tf_op jit(solution)/shard_map/ppermute | solution.py:378
  154.6 12.2 %collective-permute-start.34 = (bf16[2,16,3072]{2,1,0:T(8,128)(2,1)}, bf16[2,16,3072]{2,1,0:T(8,128)(2,1)S(1)}, u32[]{:S(2)}, u32[]{:S(2)}) collective-permute-start(bf16[2,16,3072]{2,1,0:T(8,128)(2,1)} %get-tuple-element.67), channel_id=1, source_target_pairs={{0,8},{8,16},{16,24},{24,0},{1,9},{9,17},{17,25},{25,1},{2,10},{10... | collective-permute-start | bytes 589832 | tf_op jit(solution)/shard_map/ppermute | solution.py:378
  160.9 11.4 %collective-permute-start.35 = (bf16[2,16,3072]{2,1,0:T(8,128)(2,1)}, bf16[2,16,3072]{2,1,0:T(8,128)(2,1)S(1)}, u32[]{:S(2)}, u32[]{:S(2)}) collective-permute-start(bf16[2,16,3072]{2,1,0:T(8,128)(2,1)} %get-tuple-element.68), channel_id=1, source_target_pairs={{0,24},{8,0},{16,8},{24,16},{1,25},{9,1},{17,9},{25,17},{2,26},{10... | collective-permute-start | bytes 589832 | tf_op jit(solution)/shard_map/ppermute | solution.py:378
  215.5 13.9 %copy-start.11 = (bf16[2,16,3072]{2,1,0:T(8,128)(2,1)S(1)}, bf16[2,16,3072]{2,1,0:T(8,128)(2,1)}, u32[]{:S(2)}) copy-start(bf16[2,16,3072]{2,1,0:T(8,128)(2,1)} %get-tuple-element.82) | copy-start | bytes 589828
  215.6 106.2 %copy-start.19 = (s32[32,2]{0,1:T(2,128)S(1)}, s32[32,2]{0,1:T(2,128)}, u32[]{:S(2)}) copy-start(s32[32,2]{0,1:T(2,128)} %param.18) | copy-start | bytes 772
  215.6 106.8 %copy-start.20 = (f32[32,2]{0,1:T(2,128)S(1)}, f32[32,2]{0,1:T(2,128)}, u32[]{:S(2)}) copy-start(f32[32,2]{0,1:T(2,128)} %param.19) | copy-start | bytes 772
  216.5 7.0 %collective-permute-start.36 = (bf16[2,16,3072]{2,1,0:T(8,128)(2,1)S(1)}, bf16[2,16,3072]{2,1,0:T(8,128)(2,1)S(1)}, u32[]{:S(2)}, u32[]{:S(2)}) collective-permute-start(bf16[2,16,3072]{2,1,0:T(8,128)(2,1)S(1)} %add_convert_fusion.7), channel_id=1, source_target_pairs={{0,32},{32,64},{64,96},{96,0},{1,33},{33,65},{65,97},{97,1},{2,34}... | collective-permute-start | bytes 589832 | tf_op jit(solution)/shard_map/ppermute | solution.py:378
  217.7 8.4 %collective-permute-start.38 = (bf16[2,16,3072]{2,1,0:T(8,128)(2,1)S(1)}, bf16[2,16,3072]{2,1,0:T(8,128)(2,1)S(1)}, u32[]{:S(2)}, u32[]{:S(2)}) collective-permute-start(bf16[2,16,3072]{2,1,0:T(8,128)(2,1)S(1)} %add_convert_fusion.5), channel_id=1, source_target_pairs={{0,96},{32,0},{64,32},{96,64},{1,97},{33,1},{65,33},{97,65},{2,98}... | collective-permute-start | bytes 589832 | tf_op jit(solution)/shard_map/ppermute | solution.py:378
  219.4 8.1 %collective-permute-start.41 = (bf16[2,16,3072]{2,1,0:T(8,128)(2,1)S(1)}, bf16[2,16,3072]{2,1,0:T(8,128)(2,1)S(1)}, u32[]{:S(2)}, u32[]{:S(2)}) collective-permute-start(bf16[2,16,3072]{2,1,0:T(8,128)(2,1)S(1)} %add_convert_fusion.3), channel_id=1, source_target_pairs={{0,8},{8,16},{16,24},{24,0},{1,9},{9,17},{17,25},{25,1},{2,10},{10... | collective-permute-start | bytes 589832 | tf_op jit(solution)/shard_map/ppermute | solution.py:378
  220.7 8.7 %collective-permute-start.43 = (bf16[2,16,3072]{2,1,0:T(8,128)(2,1)S(1)}, bf16[2,16,3072]{2,1,0:T(8,128)(2,1)S(1)}, u32[]{:S(2)}, u32[]{:S(2)}) collective-permute-start(bf16[2,16,3072]{2,1,0:T(8,128)(2,1)S(1)} %add_convert_fusion.1), channel_id=1, source_target_pairs={{0,24},{8,0},{16,8},{24,16},{1,25},{9,1},{17,9},{25,17},{2,26},{10... | collective-permute-start | bytes 589832 | tf_op jit(solution)/shard_map/ppermute | solution.py:378
  223.6 7.4 %collective-permute-start.37 = (bf16[16,3072]{1,0:T(8,128)(2,1)S(1)}, bf16[16,3072]{1,0:T(8,128)(2,1)S(1)}, u32[]{:S(2)}, u32[]{:S(2)}) collective-permute-start(bf16[16,3072]{1,0:T(8,128)(2,1)S(1)} %slice_bitcast_fusion.6), channel_id=1, source_target_pairs={{0,24},{8,0},{16,8},{24,16},{1,25},{9,1},{17,9},{25,17},{2,26},{10... | collective-permute-start | bytes 294920 | tf_op jit(solution)/shard_map/ppermute | solution.py:378
  226.2 7.7 %collective-permute-start.39 = (bf16[16,3072]{1,0:T(8,128)(2,1)S(1)}, bf16[16,3072]{1,0:T(8,128)(2,1)S(1)}, u32[]{:S(2)}, u32[]{:S(2)}) collective-permute-start(bf16[16,3072]{1,0:T(8,128)(2,1)S(1)} %get-tuple-element.91), channel_id=1, source_target_pairs={{0,16},{8,24},{16,0},{24,8},{1,17},{9,25},{17,1},{25,9},{2,18},{10... | collective-permute-start | bytes 294920 | tf_op jit(solution)/shard_map/ppermute | solution.py:378
  226.9 9.5 %collective-permute-start.40 = (bf16[16,3072]{1,0:T(8,128)(2,1)S(1)}, bf16[16,3072]{1,0:T(8,128)(2,1)S(1)}, u32[]{:S(2)}, u32[]{:S(2)}) collective-permute-start(bf16[16,3072]{1,0:T(8,128)(2,1)S(1)} %get-tuple-element.92), channel_id=1, source_target_pairs={{0,8},{8,16},{16,24},{24,0},{1,9},{9,17},{17,25},{25,1},{2,10},{10... | collective-permute-start | bytes 294920 | tf_op jit(solution)/shard_map/ppermute | solution.py:378
  227.6 8.9 %collective-permute-start.42 = (bf16[16,3072]{1,0:T(8,128)(2,1)S(1)}, bf16[16,3072]{1,0:T(8,128)(2,1)S(1)}, u32[]{:S(2)}, u32[]{:S(2)}) collective-permute-start(bf16[16,3072]{1,0:T(8,128)(2,1)S(1)} %slice_bitcast_fusion.2), channel_id=1, source_target_pairs={{0,96},{32,0},{64,32},{96,64},{1,97},{33,1},{65,33},{97,65},{2,98}... | collective-permute-start | bytes 294920 | tf_op jit(solution)/shard_map/ppermute | solution.py:378
  229.5 7.0 %collective-permute-start.44 = (bf16[16,3072]{1,0:T(8,128)(2,1)S(1)}, bf16[16,3072]{1,0:T(8,128)(2,1)S(1)}, u32[]{:S(2)}, u32[]{:S(2)}) collective-permute-start(bf16[16,3072]{1,0:T(8,128)(2,1)S(1)} %get-tuple-element.93), channel_id=1, source_target_pairs={{0,64},{32,96},{64,0},{96,32},{1,65},{33,97},{65,1},{97,33},{2,66}... | collective-permute-start | bytes 294920 | tf_op jit(solution)/shard_map/ppermute | solution.py:378
  231.0 6.9 %collective-permute-start.45 = (bf16[16,3072]{1,0:T(8,128)(2,1)S(1)}, bf16[16,3072]{1,0:T(8,128)(2,1)S(1)}, u32[]{:S(2)}, u32[]{:S(2)}) collective-permute-start(bf16[16,3072]{1,0:T(8,128)(2,1)S(1)} %get-tuple-element.94), channel_id=1, source_target_pairs={{0,32},{32,64},{64,96},{96,0},{1,33},{33,65},{65,97},{97,1},{2,34}... | collective-permute-start | bytes 294920 | tf_op jit(solution)/shard_map/ppermute | solution.py:378
  238.8 17.1 %all-to-all-start.1 = ((bf16[8,96,128]{2,1,0:T(8,128)(2,1)}), bf16[8,96,128]{2,1,0:T(8,128)(2,1)S(1)}, u32[]{:S(2)}, u32[]{:S(2)}) async-start(bf16[8,96,128]{2,1,0:T(8,128)(2,1)} %reshape.97), calls=%async_computation.2 | async-start | bytes 393216 | tf_op jit(solution)/shard_map/all_to_all | solution.py:424
  255.9 12.4 %all-to-all-start.2 = ((bf16[8,32,768]{2,1,0:T(8,128)(2,1)}), bf16[8,32,768]{2,1,0:T(8,128)(2,1)S(1)}, u32[]{:S(2)}, u32[]{:S(2)}) async-start(bf16[8,32,768]{2,1,0:T(8,128)(2,1)} %bitcast.28), calls=%async_computation.3 | async-start | bytes 786432 | tf_op jit(solution)/shard_map/all_to_all | solution.py:556
  268.3 66.9 %copy-start = (bf16[8,32,768]{2,1,0:T(8,128)(2,1)}, bf16[8,32,768]{2,1,0:T(8,128)(2,1)S(1)}, u32[]{:S(2)}) copy-start(bf16[8,32,768]{2,1,0:T(8,128)(2,1)S(1)} %all-to-all-done.2.mixed_ref) | copy-start | bytes 1179652
  316.5 17.5 %all-to-all-start.3 = ((bf16[8,384,128]{2,1,0:T(8,128)(2,1)}), bf16[8,384,128]{2,1,0:T(8,128)(2,1)S(1)}, u32[]{:S(2)}, u32[]{:S(2)}) async-start(bf16[8,384,128]{2,1,0:T(8,128)(2,1)} %reshape.100), calls=%async_computation.4 | async-start | bytes 1572864 | tf_op jit(solution)/shard_map/all_to_all | solution.py:424
  (20 other events, 88.3 us)
Sparse Core Ops, SparseCore 0:
  79.6 107.6 all-gather.1
  215.7 98.5 reduce-scatter.1

commit v3 on v2

--- a/solution.py
+++ b/solution.py
@@ -425,10 +425,13 @@
     return back.reshape(summed.shape)
 
 
-def gather_routes(routes):
+def chip_routes(routes):
     ours = lax.axis_index("core")
     other = shift(routes, "core", 1, 2)
-    pair = jnp.where(ours == 0, jnp.stack([routes, other]), jnp.stack([other, routes]))
+    return jnp.where(ours == 0, jnp.stack([routes, other]), jnp.stack([other, routes]))
+
+
+def gather_routes(pair):
     ring = jnp.stack([pair] + [shift(pair, "x", d) for d in range(1, SIDE)])
     distance = (lax.axis_index("x") - jnp.arange(SIDE)) % SIDE
     placed = sum(
@@ -488,7 +491,7 @@
     exp_count = model // width
     blocks = token_count // ROWS
     place = jnp.stack([lax.axis_index("z"), lax.axis_index("y")]).astype(jnp.int32)
-    all_routes = gather_routes(routes.T)
+    chip = chip_routes(routes.T)
     log_decay = log_decay.T
 
     state_rows = heads * HEAD_DIM + LOG_ROWS
@@ -497,7 +500,8 @@
     inner = call(
         inner_kernel, shape((token_count, width), F32), queries, key_rows, value_rows, log_decay
     )
-    in_line, inner, all_routes = lax.optimization_barrier((in_line, inner, all_routes))
+    in_line, inner, chip = lax.optimization_barrier((in_line, inner, chip))
+    all_routes = gather_routes(chip)
     scalar = pl.BlockSpec(memory_space=pltpu.SMEM)
     line, before, line_log = pl.pallas_call(
         line_kernel,

time: 346 us -> 340 us (0.983)
  transfers between devices with their start and end apart: 51 -> 51, of which waited for: 21 -> 20; matrix products, arithmetic and copies ran while one was open for 6% -> 6% of each run, Pallas kernels for 5% -> 5%
where the time goes in v3:
time: 340 us; the launch traced here: 339 us
  waiting for transfers between devices  131 us (39%)
  starting transfers between devices  86.9 us (26%)
  Pallas kernels  60.4 us (18%)
  local copies, waits for them, and re-layouts  22.3 us (7%)
  blocking collectives  20.2 us (6%)
  between operations  14 us (4%)
  other arithmetic  4.45 us (1%)
    ppermute x43, starting transfers between devices, shift(): lax.ppermute(value, axis, [(i, (i + step) % count) for i in range(count)])  56 us
    reduce_scatter x1, waiting for transfers between devices, per_device(): first = lax.psum_scatter(partial, SEQ, scatter_dimension=0, tiled=True)  45.6 us
    ppermute x43, waiting for transfers between devices, shift(): lax.ppermute(value, axis, [(i, (i + step) % count) for i in range(count)])  42.6 us
    pallas_call x1, Pallas kernels, expert_rows(): pl.pallas_call(rows_kernel, grid=(total // TILE,), out_shape=shape((total...  28.2 us
    all_to_all x1, blocking collectives, per_device(): parts = lax.all_to_all(packed, EXP, split_axis=0, concat_axis=0, tiled=True)  20.2 us
    all_to_all x2, waiting for transfers between devices, home_rows(): back = lax.all_to_all(lines, EXP, split_axis=0, concat_axis=0, tiled=True)  16.8 us
    all_to_all x2, starting transfers between devices, home_rows(): back = lax.all_to_all(lines, EXP, split_axis=0, concat_axis=0, tiled=True)  16.5 us
    unnamed x69, local copies, waits for them, and re-layouts  15 us
  transfers between devices with their start and end apart: 51, of which 20 were waited for; matrix products, arithmetic and copies ran while one was open for 6% of the time, Pallas kernels for 5%

profile of v3, /device:TPU:1, one launch (start us, length us, event | category | flops | bytes accessed | tf_op | source)
XLA Modules:
  0.0 338.8 jit_solution(2309027338537577230)
XLA Ops:
  6.5 2.8 shard_map.109.refs_0_
  9.4 2.1 collective-permute-start
  11.5 2.6 collective-permute-start.1
  15.2 1.5 collective-permute-start.3
  16.7 3.3 shard_map.110.inner_ref
  21.3 1.3 reshape.63.gain_ref
  23.4 1.3 collective-permute-start.7
  24.7 2.5 collective-permute-start.8
  27.1 1.2 collective-permute-start.9
  28.3 2.4 shard_map.111
  30.7 3.5 %collective-permute-start.4 = (bf16[784,128]{1,0:T(8,128)(2,1)}, bf16[784,128]{1,0:T(8,128)(2,1)S(1)}, u32[]{:S(2)}, u32[]{:S(2)}) collective-permute-start(bf16[784,128]{1,0:T(8,128)(2,1)} %get-tuple-element.53), channel_id=1, source_target_pairs={{0,32},{32,64},{64,96},{1,33},{33,65},{65,97},{2,34},{34,66},{66,9... | collective-permute-start | bytes 602120 | tf_op jit(solution)/shard_map/ppermute | solution.py:518
  34.3 5.2 %collective-permute-start.5 = (bf16[784,128]{1,0:T(8,128)(2,1)}, bf16[784,128]{1,0:T(8,128)(2,1)S(1)}, u32[]{:S(2)}, u32[]{:S(2)}) collective-permute-start(bf16[784,128]{1,0:T(8,128)(2,1)} %get-tuple-element.53), channel_id=1, source_target_pairs={{0,64},{32,96},{1,65},{33,97},{2,66},{34,98},{3,67},{35,99},{4,68}... | collective-permute-start | bytes 602120 | tf_op jit(solution)/shard_map/ppermute | solution.py:518
  39.6 1.3 collective-permute-start.6
  42.4 4.2 %collective-permute-done.6.line3_ref = bf16[784,128]{1,0:T(8,128)(2,1)S(1)} collective-permute-done((bf16[784,128]{1,0:T(8,128)(2,1)}, bf16[784,128]{1,0:T(8,128)(2,1)S(1)}, u32[]{:S(2)}, u32[]{:S(2)}) %collective-permute-start.6) | collective-permute-done | bytes 200736 | tf_op jit(solution)/shard_map/ppermute | solution.py:518
  47.3 4.9 %shard_map.112 = (bf16[256,768]{1,0:T(8,128)(2,1)}, bf16[8,80,768]{2,1,0:T(8,128)(2,1)}) custom-call(bf16[256,768]{1,0:T(8,128)(2,1)} %query_ref.3, f32[6,256]{1,0:T(8,128)} %bitcast.53, f32[256,768]{1,0:T(8,128)} %shard_map.110.inner_ref, bf16[256,768]{1,0:T(8,128)(2,1)} %residual_ref.1, f32[1,768]{1,0:T(1,128)} %reshape.63.gain_ref, ...), custom_call_target="tpu_custom_call" | custom-call | tf_op jit(solution)/shard_map/pallas_call | solution.py:520
  52.2 20.2 %all_to_all.20.parts_ref = bf16[8,80,768]{2,1,0:T(8,128)(2,1)} all-to-all(bf16[8,80,768]{2,1,0:T(8,128)(2,1)} %get-tuple-element.57), channel_id=1, replica_groups=mesh['z'=4,'y'=4,'x'=4,'core'=2] {'x','core'}, dimensions={0} | all-to-all | bytes 1966080 | tf_op jit(solution)/shard_map/all_to_all | solution.py:540
  72.4 2.6 shard_map.113
  75.0 1.2 collective-permute-start.20
  76.3 2.2 collective-permute-start.21
  79.0 2.0 collective-permute-start.11
  81.0 1.2 collective-permute-start.12
  83.0 2.0 collective-permute-start.25
  86.4 2.4 collective-permute-start.27
  88.8 3.5 %collective-permute-start.16 = (bf16[2,16,3072]{2,1,0:T(8,128)(2,1)S(1)}, bf16[2,16,3072]{2,1,0:T(8,128)(2,1)S(1)}, u32[]{:S(2)}, u32[]{:S(2)}) collective-permute-start(bf16[2,16,3072]{2,1,0:T(8,128)(2,1)S(1)} %pad_maximum_fusion.1.refs_1_), channel_id=1, source_target_pairs={{0,96},{32,0},{64,32},{96,64},{1,97},{33,1},{65,33},{97,65},{2,98}... | collective-permute-start | bytes 589832 | tf_op jit(solution)/shard_map/ppermute | solution.py:378
  93.8 1.6 collective-permute-start.14
  95.4 2.0 collective-permute-done.23.refs_11_
  97.4 1.3 collective-permute-start.13
  98.7 7.1 %collective-permute-done.22.refs_10_ = bf16[2,16,3072]{2,1,0:T(8,128)(2,1)S(1)} collective-permute-done((bf16[2,16,3072]{2,1,0:T(8,128)(2,1)S(1)}, bf16[2,16,3072]{2,1,0:T(8,128)(2,1)S(1)}, u32[]{:S(2)}, u32[]{:S(2)}) %collective-permute-start.22) | collective-permute-done | bytes 196640 | tf_op jit(solution)/shard_map/ppermute | solution.py:378
  105.8 2.7 collective-permute-start.18
  108.5 1.4 collective-permute-start.24
  110.0 1.4 collective-permute-start.15
  111.4 10.6 %copy.24.refs_16_.up_ref = bf16[1,6144,576]{2,1,0:T(8,128)(2,1)} copy(bf16[1,6144,576]{1,2,0:T(8,128)(2,1)} %param.20) | data formatting | bytes 14155776 | tf_op args[9]
  123.6 12.9 %shard_map.114 = (bf16[2,16,3072]{2,1,0:T(8,128)(2,1)}, bf16[2,16,3072]{2,1,0:T(8,128)(2,1)}, bf16[2,16,3072]{2,1,0:T(8,128)(2,1)}, bf16[2,16,3072]{2,1,0:T(8,12...) custom-call(bf16[2,16,3072]{2,1,0:T(8,128)(2,1)} %copy-done.10, ...), custom_call_target="tpu_custom_call" | custom-call | flops 5435817984 | bytes 20447232 | tf_op jit(solution)/shard_map/pallas_call | solution.py:307
  136.7 2.5 collective-permute-start.29
  139.2 2.7 collective-permute-start.31
  142.0 5.8 %collective-permute-done.28 = bf16[2,16,3072]{2,1,0:T(8,128)(2,1)S(1)} collective-permute-done((bf16[2,16,3072]{2,1,0:T(8,128)(2,1)}, bf16[2,16,3072]{2,1,0:T(8,128)(2,1)S(1)}, u32[]{:S(2)}, u32[]{:S(2)}) %collective-permute-start.28) | collective-permute-done | bytes 196640 | tf_op jit(solution)/shard_map/ppermute | solution.py:378
  147.8 1.3 collective-permute-start.33
  149.3 7.0 %collective-permute-done.30 = bf16[2,16,3072]{2,1,0:T(8,128)(2,1)S(1)} collective-permute-done((bf16[2,16,3072]{2,1,0:T(8,128)(2,1)}, bf16[2,16,3072]{2,1,0:T(8,128)(2,1)S(1)}, u32[]{:S(2)}, u32[]{:S(2)}) %collective-permute-start.30) | collective-permute-done | bytes 196640 | tf_op jit(solution)/shard_map/ppermute | solution.py:378
  156.2 1.3 collective-permute-start.35
  157.6 3.9 %collective-permute-done.34 = bf16[2,16,3072]{2,1,0:T(8,128)(2,1)S(1)} collective-permute-done((bf16[2,16,3072]{2,1,0:T(8,128)(2,1)}, bf16[2,16,3072]{2,1,0:T(8,128)(2,1)S(1)}, u32[]{:S(2)}, u32[]{:S(2)}) %collective-permute-start.34) | collective-permute-done | bytes 196640 | tf_op jit(solution)/shard_map/ppermute | solution.py:378
  161.4 6.2 %collective-permute-done.35 = bf16[2,16,3072]{2,1,0:T(8,128)(2,1)S(1)} collective-permute-done((bf16[2,16,3072]{2,1,0:T(8,128)(2,1)}, bf16[2,16,3072]{2,1,0:T(8,128)(2,1)S(1)}, u32[]{:S(2)}, u32[]{:S(2)}) %collective-permute-start.35) | collective-permute-done | bytes 196640 | tf_op jit(solution)/shard_map/ppermute | solution.py:378
  167.6 13.4 %all-gather.2.cloned.1.call-done.rows_ref = bf16[1024,6144]{1,0:T(8,128)(2,1)} async-done(((bf16[64,6144]{1,0:T(8,128)(2,1)}), bf16[1024,6144]{1,0:T(8,128)(2,1)}) %all-gather.2.cloned.1.call-update) | async-done | bytes 12582928 | tf_op jit(solution)/shard_map/all_gather | solution.py:547
  181.0 28.2 %shard_map.115 = bf16[1024,6144]{1,0:T(8,128)(2,1)} custom-call(bf16[1024,6144]{1,0:T(8,128)(2,1)} %all-gather.2.cloned.1.call-done.rows_ref, bf16[1,6144,576]{2,1,0:T(8,128)(2,1)} %copy.24.refs_16_.up_ref, bf16[1,576,6144]{2,1,0:T(8,128)(2,1)} %down_ref.1), custom_call_target="tpu_custom_call" | custom-call | flops 14495514624 | bytes 39321600 | tf_op jit(solution)/shard_map/pallas_call | solution.py:340
  210.2 1.2 collective-permute-start.36
  211.5 1.6 collective-permute-start.38
  213.2 1.3 collective-permute-start.41
  214.5 1.5 collective-permute-start.43
  216.0 1.3 collective-permute-done.36
  217.4 2.5 collective-permute-start.37
  221.3 1.8 collective-permute-start.42
  223.4 1.5 collective-permute-done.37
  224.8 2.9 collective-permute-done.39
  227.7 2.4 collective-permute-done.40
  230.2 1.4 collective-permute-done.45
  232.5 11.3 %all-to-all-start.1 = ((bf16[8,96,128]{2,1,0:T(8,128)(2,1)}), bf16[8,96,128]{2,1,0:T(8,128)(2,1)S(1)}, u32[]{:S(2)}, u32[]{:S(2)}) async-start(bf16[8,96,128]{2,1,0:T(8,128)(2,1)} %reshape.65), calls=%async_computation.2 | async-start | bytes 393216 | tf_op jit(solution)/shard_map/all_to_all | solution.py:424
  243.9 5.9 %all-to-all-done.1 = bf16[8,96,128]{2,1,0:T(8,128)(2,1)S(1)} async-done(((bf16[8,96,128]{2,1,0:T(8,128)(2,1)}), bf16[8,96,128]{2,1,0:T(8,128)(2,1)S(1)}, u32[]{:S(2)}, u32[]{:S(2)}) %all-to-all-start.1) | async-done | bytes 196640 | tf_op jit(solution)/shard_map/all_to_all | solution.py:424
  249.8 4.3 %all-to-all-start.2 = ((bf16[8,32,768]{2,1,0:T(8,128)(2,1)}), bf16[8,32,768]{2,1,0:T(8,128)(2,1)S(1)}, u32[]{:S(2)}, u32[]{:S(2)}) async-start(bf16[8,32,768]{2,1,0:T(8,128)(2,1)} %bitcast.28), calls=%async_computation.3 | async-start | bytes 786432 | tf_op jit(solution)/shard_map/all_to_all | solution.py:560
  254.8 7.3 %all-to-all-done.2.mixed_ref = bf16[8,32,768]{2,1,0:T(8,128)(2,1)S(1)} async-done(((bf16[8,32,768]{2,1,0:T(8,128)(2,1)}), bf16[8,32,768]{2,1,0:T(8,128)(2,1)S(1)}, u32[]{:S(2)}, u32[]{:S(2)}) %all-to-all-start.2) | async-done | bytes 393248 | tf_op jit(solution)/shard_map/all_to_all | solution.py:560
  262.2 45.6 %reduce-scatter.2.cloned.1.call-done = bf16[64,6144]{1,0:T(8,128)(2,1)} async-done(((bf16[1024,6144]{1,0:T(8,128)(2,1)}), bf16[64,6144]{1,0:T(8,128)(2,1)}) %reduce-scatter.2.cloned.1.call-update) | async-done | bytes 786448 | tf_op jit(solution)/shard_map/reduce_scatter | solution.py:558
  307.8 2.2 reshape.68
  310.0 5.2 %all-to-all-start.3 = ((bf16[8,384,128]{2,1,0:T(8,128)(2,1)}), bf16[8,384,128]{2,1,0:T(8,128)(2,1)S(1)}, u32[]{:S(2)}, u32[]{:S(2)}) async-start(bf16[8,384,128]{2,1,0:T(8,128)(2,1)} %reshape.68), calls=%async_computation.4 | async-start | bytes 1572864 | tf_op jit(solution)/shard_map/all_to_all | solution.py:424
  316.5 10.9 %all-to-all-done.3 = bf16[8,384,128]{2,1,0:T(8,128)(2,1)S(1)} async-done(((bf16[8,384,128]{2,1,0:T(8,128)(2,1)}), bf16[8,384,128]{2,1,0:T(8,128)(2,1)S(1)}, u32[]{:S(2)}, u32[]{:S(2)}) %all-to-all-start.3) | async-done | bytes 786464 | tf_op jit(solution)/shard_map/all_to_all | solution.py:424
  327.5 1.2 reshape.69.first_ref
  328.7 3.2 shard_map.116
  (167 shorter events, 17.3 us)
Async XLA Ops:
  6.5 174.5 %all-gather.2.cloned.1.call-start = ((), (), s32[]{:S(2)}) async-start(), calls=%async_computation.5 | async-start | bytes 13369344 | tf_op jit(solution)/shard_map/all_gather | solution.py:547
  9.4 14.0 %collective-permute-start = (bf16[784,128]{1,0:T(8,128)(2,1)}, bf16[784,128]{1,0:T(8,128)(2,1)S(1)}, u32[]{:S(2)}, u32[]{:S(2)}) collective-permute-start(bf16[784,128]{1,0:T(8,128)(2,1)} %shard_map.109.refs_0_), channel_id=1, source_target_pairs={{0,8},{8,16},{16,24},{24,0},{1,9},{9,17},{17,25},{25,1},{2,10},{10... | collective-permute-start | bytes 602120 | tf_op jit(solution)/shard_map/ppermute | solution.py:378
  11.5 11.8 %collective-permute-start.1 = (bf16[784,128]{1,0:T(8,128)(2,1)}, bf16[784,128]{1,0:T(8,128)(2,1)S(1)}, u32[]{:S(2)}, u32[]{:S(2)}) collective-permute-start(bf16[784,128]{1,0:T(8,128)(2,1)} %shard_map.109.refs_0_), channel_id=1, source_target_pairs={{0,16},{8,24},{16,0},{24,8},{1,17},{9,25},{17,1},{25,9},{2,18},{10... | collective-permute-start | bytes 602120 | tf_op jit(solution)/shard_map/ppermute | solution.py:378
  14.1 9.2 %collective-permute-start.2 = (bf16[784,128]{1,0:T(8,128)(2,1)}, bf16[784,128]{1,0:T(8,128)(2,1)S(1)}, u32[]{:S(2)}, u32[]{:S(2)}) collective-permute-start(bf16[784,128]{1,0:T(8,128)(2,1)} %shard_map.109.refs_0_), channel_id=1, source_target_pairs={{0,24},{8,0},{16,8},{24,16},{1,25},{9,1},{17,9},{25,17},{2,26},{10... | collective-permute-start | bytes 602120 | tf_op jit(solution)/shard_map/ppermute | solution.py:378
  15.2 7.4 %collective-permute-start.3 = (s32[2,32]{1,0:T(2,128)}, s32[2,32]{1,0:T(2,128)S(1)}, u32[]{:S(2)}, u32[]{:S(2)}) collective-permute-start(s32[2,32]{1,0:T(2,128)} %bitcast.56), channel_id=1, source_target_pairs={{0,1},{1,0},{2,3},{3,2},{4,5},{5,4},{6,7},{7,6},{8,9},{9,8},{10,11... | collective-permute-start | bytes 776 | tf_op jit(solution)/shard_map/ppermute | solution.py:378
  23.4 16.2 %collective-permute-start.7 = (s32[2,2,32]{2,1,0:T(2,128)S(1)}, s32[2,2,32]{2,1,0:T(2,128)S(1)}, u32[]{:S(2)}, u32[]{:S(2)}) collective-permute-start(s32[2,2,32]{2,1,0:T(2,128)S(1)} %add_select_fusion), channel_id=1, source_target_pairs={{0,2},{2,4},{4,6},{6,0},{1,3},{3,5},{5,7},{7,1},{8,10},{10,12},{12... | collective-permute-start | bytes 1544 | tf_op jit(solution)/shard_map/ppermute | solution.py:378
  24.7 16.3 %collective-permute-start.8 = (s32[2,2,32]{2,1,0:T(2,128)S(1)}, s32[2,2,32]{2,1,0:T(2,128)S(1)}, u32[]{:S(2)}, u32[]{:S(2)}) collective-permute-start(s32[2,2,32]{2,1,0:T(2,128)S(1)} %add_select_fusion), channel_id=1, source_target_pairs={{0,4},{2,6},{4,0},{6,2},{1,5},{3,7},{5,1},{7,3},{8,12},{10,14},{12... | collective-permute-start | bytes 1544 | tf_op jit(solution)/shard_map/ppermute | solution.py:378
  27.1 14.0 %collective-permute-start.9 = (s32[2,2,32]{2,1,0:T(2,128)S(1)}, s32[2,2,32]{2,1,0:T(2,128)S(1)}, u32[]{:S(2)}, u32[]{:S(2)}) collective-permute-start(s32[2,2,32]{2,1,0:T(2,128)S(1)} %add_select_fusion), channel_id=1, source_target_pairs={{0,6},{2,0},{4,2},{6,4},{1,7},{3,1},{5,3},{7,5},{8,14},{10,8},{12,... | collective-permute-start | bytes 1544 | tf_op jit(solution)/shard_map/ppermute | solution.py:378
  30.7 11.1 %collective-permute-start.4 = (bf16[784,128]{1,0:T(8,128)(2,1)}, bf16[784,128]{1,0:T(8,128)(2,1)S(1)}, u32[]{:S(2)}, u32[]{:S(2)}) collective-permute-start(bf16[784,128]{1,0:T(8,128)(2,1)} %get-tuple-element.53), channel_id=1, source_target_pairs={{0,32},{32,64},{64,96},{1,33},{33,65},{65,97},{2,34},{34,66},{66,9... | collective-permute-start | bytes 602120 | tf_op jit(solution)/shard_map/ppermute | solution.py:518
  34.3 8.2 %collective-permute-start.5 = (bf16[784,128]{1,0:T(8,128)(2,1)}, bf16[784,128]{1,0:T(8,128)(2,1)S(1)}, u32[]{:S(2)}, u32[]{:S(2)}) collective-permute-start(bf16[784,128]{1,0:T(8,128)(2,1)} %get-tuple-element.53), channel_id=1, source_target_pairs={{0,64},{32,96},{1,65},{33,97},{2,66},{34,98},{3,67},{35,99},{4,68}... | collective-permute-start | bytes 602120 | tf_op jit(solution)/shard_map/ppermute | solution.py:518
  39.6 7.0 %collective-permute-start.6 = (bf16[784,128]{1,0:T(8,128)(2,1)}, bf16[784,128]{1,0:T(8,128)(2,1)S(1)}, u32[]{:S(2)}, u32[]{:S(2)}) collective-permute-start(bf16[784,128]{1,0:T(8,128)(2,1)} %get-tuple-element.53), channel_id=1, source_target_pairs={{0,96},{1,97},{2,98},{3,99},{4,100},{5,101},{6,102},{7,103},{8,104... | collective-permute-start | bytes 602120 | tf_op jit(solution)/shard_map/ppermute | solution.py:518
  75.0 232.8 %reduce-scatter.2.cloned.1.call-start = ((), (), s32[]{:S(2)}) async-start(), calls=%async_computation.6 | async-start | bytes 13369344 | tf_op jit(solution)/shard_map/reduce_scatter | solution.py:558
  75.0 7.2 %collective-permute-start.20 = (bf16[16,3072]{1,0:T(8,128)(2,1)}, bf16[16,3072]{1,0:T(8,128)(2,1)S(1)}, u32[]{:S(2)}, u32[]{:S(2)}) collective-permute-start(bf16[16,3072]{1,0:T(8,128)(2,1)} %get-tuple-element.60), channel_id=1, source_target_pairs={{0,64},{32,96},{64,0},{96,32},{1,65},{33,97},{65,1},{97,33},{2,66}... | collective-permute-start | bytes 294920 | tf_op jit(solution)/shard_map/ppermute | solution.py:378
  76.3 6.7 %collective-permute-start.21 = (bf16[16,3072]{1,0:T(8,128)(2,1)}, bf16[16,3072]{1,0:T(8,128)(2,1)S(1)}, u32[]{:S(2)}, u32[]{:S(2)}) collective-permute-start(bf16[16,3072]{1,0:T(8,128)(2,1)} %get-tuple-element.60), channel_id=1, source_target_pairs={{0,96},{32,0},{64,32},{96,64},{1,97},{33,1},{65,33},{97,65},{2,98}... | collective-permute-start | bytes 294920 | tf_op jit(solution)/shard_map/ppermute | solution.py:378
  78.5 6.5 %collective-permute-start.19 = (bf16[16,3072]{1,0:T(8,128)(2,1)}, bf16[16,3072]{1,0:T(8,128)(2,1)S(1)}, u32[]{:S(2)}, u32[]{:S(2)}) collective-permute-start(bf16[16,3072]{1,0:T(8,128)(2,1)} %get-tuple-element.60), channel_id=1, source_target_pairs={{0,32},{32,64},{64,96},{96,0},{1,33},{33,65},{65,97},{97,1},{2,34}... | collective-permute-start | bytes 294920 | tf_op jit(solution)/shard_map/ppermute | solution.py:378
  79.0 6.9 %collective-permute-start.11 = (bf16[16,3072]{1,0:T(8,128)(2,1)}, bf16[16,3072]{1,0:T(8,128)(2,1)S(1)}, u32[]{:S(2)}, u32[]{:S(2)}) collective-permute-start(bf16[16,3072]{1,0:T(8,128)(2,1)} %get-tuple-element.59), channel_id=1, source_target_pairs={{0,16},{8,24},{16,0},{24,8},{1,17},{9,25},{17,1},{25,9},{2,18},{10... | collective-permute-start | bytes 294920 | tf_op jit(solution)/shard_map/ppermute | solution.py:378
  81.0 5.4 %collective-permute-start.12 = (bf16[16,3072]{1,0:T(8,128)(2,1)}, bf16[16,3072]{1,0:T(8,128)(2,1)S(1)}, u32[]{:S(2)}, u32[]{:S(2)}) collective-permute-start(bf16[16,3072]{1,0:T(8,128)(2,1)} %get-tuple-element.59), channel_id=1, source_target_pairs={{0,24},{8,0},{16,8},{24,16},{1,25},{9,1},{17,9},{25,17},{2,26},{10... | collective-permute-start | bytes 294920 | tf_op jit(solution)/shard_map/ppermute | solution.py:378
  82.2 6.6 %collective-permute-start.10 = (bf16[16,3072]{1,0:T(8,128)(2,1)}, bf16[16,3072]{1,0:T(8,128)(2,1)S(1)}, u32[]{:S(2)}, u32[]{:S(2)}) collective-permute-start(bf16[16,3072]{1,0:T(8,128)(2,1)} %get-tuple-element.59), channel_id=1, source_target_pairs={{0,8},{8,16},{16,24},{24,0},{1,9},{9,17},{17,25},{25,1},{2,10},{10... | collective-permute-start | bytes 294920 | tf_op jit(solution)/shard_map/ppermute | solution.py:378
  83.0 39.1 %copy-start.7 = (bf16[2,16,3072]{2,1,0:T(8,128)(2,1)}, bf16[2,16,3072]{2,1,0:T(8,128)(2,1)S(1)}, u32[]{:S(2)}) copy-start(bf16[2,16,3072]{2,1,0:T(8,128)(2,1)S(1)} %pad_maximum_fusion.3.refs_9_) | copy-start | bytes 589828
  83.0 10.8 %collective-permute-start.25 = (bf16[2,16,3072]{2,1,0:T(8,128)(2,1)S(1)}, bf16[2,16,3072]{2,1,0:T(8,128)(2,1)S(1)}, u32[]{:S(2)}, u32[]{:S(2)}) collective-permute-start(bf16[2,16,3072]{2,1,0:T(8,128)(2,1)S(1)} %pad_maximum_fusion.3.refs_9_), channel_id=1, source_target_pairs={{0,24},{8,0},{16,8},{24,16},{1,25},{9,1},{17,9},{25,17},{2,26},{10... | collective-permute-start | bytes 589832 | tf_op jit(solution)/shard_map/ppermute | solution.py:378
  85.0 12.4 %collective-permute-start.23 = (bf16[2,16,3072]{2,1,0:T(8,128)(2,1)S(1)}, bf16[2,16,3072]{2,1,0:T(8,128)(2,1)S(1)}, u32[]{:S(2)}, u32[]{:S(2)}) collective-permute-start(bf16[2,16,3072]{2,1,0:T(8,128)(2,1)S(1)} %pad_maximum_fusion.3.refs_9_), channel_id=1, source_target_pairs={{0,8},{8,16},{16,24},{24,0},{1,9},{9,17},{17,25},{25,1},{2,10},{10... | collective-permute-start | bytes 589832 | tf_op jit(solution)/shard_map/ppermute | solution.py:378
  85.9 36.2 %copy-start.8 = (bf16[2,16,3072]{2,1,0:T(8,128)(2,1)}, bf16[2,16,3072]{2,1,0:T(8,128)(2,1)S(1)}, u32[]{:S(2)}) copy-start(bf16[2,16,3072]{2,1,0:T(8,128)(2,1)S(1)} %pad_maximum_fusion.2.refs_8_) | copy-start | bytes 589828
  85.9 19.9 %collective-permute-start.22 = (bf16[2,16,3072]{2,1,0:T(8,128)(2,1)S(1)}, bf16[2,16,3072]{2,1,0:T(8,128)(2,1)S(1)}, u32[]{:S(2)}, u32[]{:S(2)}) collective-permute-start(bf16[2,16,3072]{2,1,0:T(8,128)(2,1)S(1)} %pad_maximum_fusion.2.refs_8_), channel_id=1, source_target_pairs={{0,8},{8,16},{16,24},{24,0},{1,9},{9,17},{17,25},{25,1},{2,10},{10... | collective-permute-start | bytes 589832 | tf_op jit(solution)/shard_map/ppermute | solution.py:378
  86.4 22.1 %collective-permute-start.27 = (bf16[2,16,3072]{2,1,0:T(8,128)(2,1)S(1)}, bf16[2,16,3072]{2,1,0:T(8,128)(2,1)S(1)}, u32[]{:S(2)}, u32[]{:S(2)}) collective-permute-start(bf16[2,16,3072]{2,1,0:T(8,128)(2,1)S(1)} %pad_maximum_fusion.2.refs_8_), channel_id=1, source_target_pairs={{0,24},{8,0},{16,8},{24,16},{1,25},{9,1},{17,9},{25,17},{2,26},{10... | collective-permute-start | bytes 589832 | tf_op jit(solution)/shard_map/ppermute | solution.py:378
  88.8 33.4 %copy-start.9 = (bf16[2,16,3072]{2,1,0:T(8,128)(2,1)}, bf16[2,16,3072]{2,1,0:T(8,128)(2,1)S(1)}, u32[]{:S(2)}) copy-start(bf16[2,16,3072]{2,1,0:T(8,128)(2,1)S(1)} %pad_maximum_fusion.1.refs_1_) | copy-start | bytes 589828
  88.8 19.7 %collective-permute-start.16 = (bf16[2,16,3072]{2,1,0:T(8,128)(2,1)S(1)}, bf16[2,16,3072]{2,1,0:T(8,128)(2,1)S(1)}, u32[]{:S(2)}, u32[]{:S(2)}) collective-permute-start(bf16[2,16,3072]{2,1,0:T(8,128)(2,1)S(1)} %pad_maximum_fusion.1.refs_1_), channel_id=1, source_target_pairs={{0,96},{32,0},{64,32},{96,64},{1,97},{33,1},{65,33},{97,65},{2,98}... | collective-permute-start | bytes 589832 | tf_op jit(solution)/shard_map/ppermute | solution.py:378
  93.2 28.9 %copy-start.10 = (bf16[2,16,3072]{2,1,0:T(8,128)(2,1)}, bf16[2,16,3072]{2,1,0:T(8,128)(2,1)S(1)}, u32[]{:S(2)}) copy-start(bf16[2,16,3072]{2,1,0:T(8,128)(2,1)S(1)} %pad_maximum_fusion.refs_0_) | copy-start | bytes 589828
  93.8 28.4 %copy-start.21 = (bf16[2,16,3072]{2,1,0:T(8,128)(2,1)}, bf16[2,16,3072]{2,1,0:T(8,128)(2,1)S(1)}, u32[]{:S(2)}) copy-start(bf16[2,16,3072]{2,1,0:T(8,128)(2,1)S(1)} %collective-permute-done.25.refs_15_) | copy-start | bytes 589828
  93.8 16.2 %collective-permute-start.14 = (bf16[2,16,3072]{2,1,0:T(8,128)(2,1)S(1)}, bf16[2,16,3072]{2,1,0:T(8,128)(2,1)S(1)}, u32[]{:S(2)}, u32[]{:S(2)}) collective-permute-start(bf16[2,16,3072]{2,1,0:T(8,128)(2,1)S(1)} %pad_maximum_fusion.1.refs_1_), channel_id=1, source_target_pairs={{0,32},{32,64},{64,96},{96,0},{1,33},{33,65},{65,97},{97,1},{2,34}... | collective-permute-start | bytes 589832 | tf_op jit(solution)/shard_map/ppermute | solution.py:378
  97.4 24.8 %copy-start.22 = (bf16[2,16,3072]{2,1,0:T(8,128)(2,1)}, bf16[2,16,3072]{2,1,0:T(8,128)(2,1)S(1)}, u32[]{:S(2)}) copy-start(bf16[2,16,3072]{2,1,0:T(8,128)(2,1)S(1)} %collective-permute-done.23.refs_11_) | copy-start | bytes 589828
  97.4 12.6 %collective-permute-start.13 = (bf16[2,16,3072]{2,1,0:T(8,128)(2,1)S(1)}, bf16[2,16,3072]{2,1,0:T(8,128)(2,1)S(1)}, u32[]{:S(2)}, u32[]{:S(2)}) collective-permute-start(bf16[2,16,3072]{2,1,0:T(8,128)(2,1)S(1)} %pad_maximum_fusion.refs_0_), channel_id=1, source_target_pairs={{0,32},{32,64},{64,96},{96,0},{1,33},{33,65},{65,97},{97,1},{2,34}... | collective-permute-start | bytes 589832 | tf_op jit(solution)/shard_map/ppermute | solution.py:378
  105.8 16.4 %copy-start.23 = (bf16[2,16,3072]{2,1,0:T(8,128)(2,1)}, bf16[2,16,3072]{2,1,0:T(8,128)(2,1)S(1)}, u32[]{:S(2)}) copy-start(bf16[2,16,3072]{2,1,0:T(8,128)(2,1)S(1)} %collective-permute-done.22.refs_10_) | copy-start | bytes 589828
  105.8 16.2 %collective-permute-start.18 = (bf16[2,16,3072]{2,1,0:T(8,128)(2,1)S(1)}, bf16[2,16,3072]{2,1,0:T(8,128)(2,1)S(1)}, u32[]{:S(2)}, u32[]{:S(2)}) collective-permute-start(bf16[2,16,3072]{2,1,0:T(8,128)(2,1)S(1)} %pad_maximum_fusion.refs_0_), channel_id=1, source_target_pairs={{0,96},{32,0},{64,32},{96,64},{1,97},{33,1},{65,33},{97,65},{2,98}... | collective-permute-start | bytes 589832 | tf_op jit(solution)/shard_map/ppermute | solution.py:378
  108.5 13.7 %copy-start.24 = (bf16[2,16,3072]{2,1,0:T(8,128)(2,1)}, bf16[2,16,3072]{2,1,0:T(8,128)(2,1)S(1)}, u32[]{:S(2)}) copy-start(bf16[2,16,3072]{2,1,0:T(8,128)(2,1)S(1)} %collective-permute-done.27.refs_14_) | copy-start | bytes 589828
  108.5 13.6 %collective-permute-start.26 = (bf16[2,16,3072]{2,1,0:T(8,128)(2,1)S(1)}, bf16[2,16,3072]{2,1,0:T(8,128)(2,1)S(1)}, u32[]{:S(2)}, u32[]{:S(2)}) collective-permute-start(bf16[2,16,3072]{2,1,0:T(8,128)(2,1)S(1)} %collective-permute-done.25.refs_15_), channel_id=1, source_target_pairs={{0,24},{8,0},{16,8},{24,16},{1,25},{9,1},{17,9},{25,17},{2,26},{10... | collective-permute-start | bytes 589832 | tf_op jit(solution)/shard_map/ppermute | solution.py:378
  108.5 13.7 %copy-start.25 = (bf16[2,16,3072]{2,1,0:T(8,128)(2,1)}, bf16[2,16,3072]{2,1,0:T(8,128)(2,1)S(1)}, u32[]{:S(2)}) copy-start(bf16[2,16,3072]{2,1,0:T(8,128)(2,1)S(1)} %collective-permute-done.16.refs_7_) | copy-start | bytes 589828
  108.5 13.6 %collective-permute-start.24 = (bf16[2,16,3072]{2,1,0:T(8,128)(2,1)S(1)}, bf16[2,16,3072]{2,1,0:T(8,128)(2,1)S(1)}, u32[]{:S(2)}, u32[]{:S(2)}) collective-permute-start(bf16[2,16,3072]{2,1,0:T(8,128)(2,1)S(1)} %collective-permute-done.22.refs_10_), channel_id=1, source_target_pairs={{0,8},{8,16},{16,24},{24,0},{1,9},{9,17},{17,25},{25,1},{2,10},{10... | collective-permute-start | bytes 589832 | tf_op jit(solution)/shard_map/ppermute | solution.py:378
  109.9 12.2 %collective-permute-start.17 = (bf16[2,16,3072]{2,1,0:T(8,128)(2,1)S(1)}, bf16[2,16,3072]{2,1,0:T(8,128)(2,1)S(1)}, u32[]{:S(2)}, u32[]{:S(2)}) collective-permute-start(bf16[2,16,3072]{2,1,0:T(8,128)(2,1)S(1)} %collective-permute-done.16.refs_7_), channel_id=1, source_target_pairs={{0,96},{32,0},{64,32},{96,64},{1,97},{33,1},{65,33},{97,65},{2,98}... | collective-permute-start | bytes 589832 | tf_op jit(solution)/shard_map/ppermute | solution.py:378
  110.0 12.1 %collective-permute-start.15 = (bf16[2,16,3072]{2,1,0:T(8,128)(2,1)S(1)}, bf16[2,16,3072]{2,1,0:T(8,128)(2,1)S(1)}, u32[]{:S(2)}, u32[]{:S(2)}) collective-permute-start(bf16[2,16,3072]{2,1,0:T(8,128)(2,1)S(1)} %collective-permute-done.13.refs_2_), channel_id=1, source_target_pairs={{0,32},{32,64},{64,96},{96,0},{1,33},{33,65},{65,97},{97,1},{2,34}... | collective-permute-start | bytes 589832 | tf_op jit(solution)/shard_map/ppermute | solution.py:378
  136.5 11.3 %collective-permute-start.28 = (bf16[2,16,3072]{2,1,0:T(8,128)(2,1)}, bf16[2,16,3072]{2,1,0:T(8,128)(2,1)S(1)}, u32[]{:S(2)}, u32[]{:S(2)}) collective-permute-start(bf16[2,16,3072]{2,1,0:T(8,128)(2,1)} %get-tuple-element.61), channel_id=1, source_target_pairs={{0,32},{32,64},{64,96},{96,0},{1,33},{33,65},{65,97},{97,1},{2,34}... | collective-permute-start | bytes 589832 | tf_op jit(solution)/shard_map/ppermute | solution.py:378
  136.7 12.5 %collective-permute-start.29 = (bf16[2,16,3072]{2,1,0:T(8,128)(2,1)}, bf16[2,16,3072]{2,1,0:T(8,128)(2,1)S(1)}, u32[]{:S(2)}, u32[]{:S(2)}) collective-permute-start(bf16[2,16,3072]{2,1,0:T(8,128)(2,1)} %get-tuple-element.62), channel_id=1, source_target_pairs={{0,96},{32,0},{64,32},{96,64},{1,97},{33,1},{65,33},{97,65},{2,98}... | collective-permute-start | bytes 589832 | tf_op jit(solution)/shard_map/ppermute | solution.py:378
  139.2 17.0 %collective-permute-start.30 = (bf16[2,16,3072]{2,1,0:T(8,128)(2,1)}, bf16[2,16,3072]{2,1,0:T(8,128)(2,1)S(1)}, u32[]{:S(2)}, u32[]{:S(2)}) collective-permute-start(bf16[2,16,3072]{2,1,0:T(8,128)(2,1)} %get-tuple-element.63), channel_id=1, source_target_pairs={{0,32},{32,64},{64,96},{96,0},{1,33},{33,65},{65,97},{97,1},{2,34}... | collective-permute-start | bytes 589832 | tf_op jit(solution)/shard_map/ppermute | solution.py:378
  139.2 18.3 %collective-permute-start.31 = (bf16[2,16,3072]{2,1,0:T(8,128)(2,1)}, bf16[2,16,3072]{2,1,0:T(8,128)(2,1)S(1)}, u32[]{:S(2)}, u32[]{:S(2)}) collective-permute-start(bf16[2,16,3072]{2,1,0:T(8,128)(2,1)} %get-tuple-element.64), channel_id=1, source_target_pairs={{0,96},{32,0},{64,32},{96,64},{1,97},{33,1},{65,33},{97,65},{2,98}... | collective-permute-start | bytes 589832 | tf_op jit(solution)/shard_map/ppermute | solution.py:378
  141.9 15.7 %collective-permute-start.32 = (bf16[2,16,3072]{2,1,0:T(8,128)(2,1)}, bf16[2,16,3072]{2,1,0:T(8,128)(2,1)S(1)}, u32[]{:S(2)}, u32[]{:S(2)}) collective-permute-start(bf16[2,16,3072]{2,1,0:T(8,128)(2,1)} %get-tuple-element.65), channel_id=1, source_target_pairs={{0,8},{8,16},{16,24},{24,0},{1,9},{9,17},{17,25},{25,1},{2,10},{10... | collective-permute-start | bytes 589832 | tf_op jit(solution)/shard_map/ppermute | solution.py:378
  147.8 9.8 %collective-permute-start.33 = (bf16[2,16,3072]{2,1,0:T(8,128)(2,1)}, bf16[2,16,3072]{2,1,0:T(8,128)(2,1)S(1)}, u32[]{:S(2)}, u32[]{:S(2)}) collective-permute-start(bf16[2,16,3072]{2,1,0:T(8,128)(2,1)} %get-tuple-element.66), channel_id=1, source_target_pairs={{0,24},{8,0},{16,8},{24,16},{1,25},{9,1},{17,9},{25,17},{2,26},{10... | collective-permute-start | bytes 589832 | tf_op jit(solution)/shard_map/ppermute | solution.py:378
  149.1 12.3 %collective-permute-start.34 = (bf16[2,16,3072]{2,1,0:T(8,128)(2,1)}, bf16[2,16,3072]{2,1,0:T(8,128)(2,1)S(1)}, u32[]{:S(2)}, u32[]{:S(2)}) collective-permute-start(bf16[2,16,3072]{2,1,0:T(8,128)(2,1)} %get-tuple-element.67), channel_id=1, source_target_pairs={{0,8},{8,16},{16,24},{24,0},{1,9},{9,17},{17,25},{25,1},{2,10},{10... | collective-permute-start | bytes 589832 | tf_op jit(solution)/shard_map/ppermute | solution.py:378
  156.2 11.4 %collective-permute-start.35 = (bf16[2,16,3072]{2,1,0:T(8,128)(2,1)}, bf16[2,16,3072]{2,1,0:T(8,128)(2,1)S(1)}, u32[]{:S(2)}, u32[]{:S(2)}) collective-permute-start(bf16[2,16,3072]{2,1,0:T(8,128)(2,1)} %get-tuple-element.68), channel_id=1, source_target_pairs={{0,24},{8,0},{16,8},{24,16},{1,25},{9,1},{17,9},{25,17},{2,26},{10... | collective-permute-start | bytes 589832 | tf_op jit(solution)/shard_map/ppermute | solution.py:378
  209.3 13.9 %copy-start.11 = (bf16[2,16,3072]{2,1,0:T(8,128)(2,1)S(1)}, bf16[2,16,3072]{2,1,0:T(8,128)(2,1)}, u32[]{:S(2)}) copy-start(bf16[2,16,3072]{2,1,0:T(8,128)(2,1)} %get-tuple-element.82) | copy-start | bytes 589828
  209.3 105.8 %copy-start.19 = (s32[32,2]{0,1:T(2,128)S(1)}, s32[32,2]{0,1:T(2,128)}, u32[]{:S(2)}) copy-start(s32[32,2]{0,1:T(2,128)} %param.18) | copy-start | bytes 772
  209.3 106.5 %copy-start.20 = (f32[32,2]{0,1:T(2,128)S(1)}, f32[32,2]{0,1:T(2,128)}, u32[]{:S(2)}) copy-start(f32[32,2]{0,1:T(2,128)} %param.19) | copy-start | bytes 772
  210.2 7.0 %collective-permute-start.36 = (bf16[2,16,3072]{2,1,0:T(8,128)(2,1)S(1)}, bf16[2,16,3072]{2,1,0:T(8,128)(2,1)S(1)}, u32[]{:S(2)}, u32[]{:S(2)}) collective-permute-start(bf16[2,16,3072]{2,1,0:T(8,128)(2,1)S(1)} %add_convert_fusion.7), channel_id=1, source_target_pairs={{0,32},{32,64},{64,96},{96,0},{1,33},{33,65},{65,97},{97,1},{2,34}... | collective-permute-start | bytes 589832 | tf_op jit(solution)/shard_map/ppermute | solution.py:378
  211.5 8.5 %collective-permute-start.38 = (bf16[2,16,3072]{2,1,0:T(8,128)(2,1)S(1)}, bf16[2,16,3072]{2,1,0:T(8,128)(2,1)S(1)}, u32[]{:S(2)}, u32[]{:S(2)}) collective-permute-start(bf16[2,16,3072]{2,1,0:T(8,128)(2,1)S(1)} %add_convert_fusion.5), channel_id=1, source_target_pairs={{0,96},{32,0},{64,32},{96,64},{1,97},{33,1},{65,33},{97,65},{2,98}... | collective-permute-start | bytes 589832 | tf_op jit(solution)/shard_map/ppermute | solution.py:378
  213.2 8.1 %collective-permute-start.41 = (bf16[2,16,3072]{2,1,0:T(8,128)(2,1)S(1)}, bf16[2,16,3072]{2,1,0:T(8,128)(2,1)S(1)}, u32[]{:S(2)}, u32[]{:S(2)}) collective-permute-start(bf16[2,16,3072]{2,1,0:T(8,128)(2,1)S(1)} %add_convert_fusion.3), channel_id=1, source_target_pairs={{0,8},{8,16},{16,24},{24,0},{1,9},{9,17},{17,25},{25,1},{2,10},{10... | collective-permute-start | bytes 589832 | tf_op jit(solution)/shard_map/ppermute | solution.py:378
  214.5 8.7 %collective-permute-start.43 = (bf16[2,16,3072]{2,1,0:T(8,128)(2,1)S(1)}, bf16[2,16,3072]{2,1,0:T(8,128)(2,1)S(1)}, u32[]{:S(2)}, u32[]{:S(2)}) collective-permute-start(bf16[2,16,3072]{2,1,0:T(8,128)(2,1)S(1)} %add_convert_fusion.1), channel_id=1, source_target_pairs={{0,24},{8,0},{16,8},{24,16},{1,25},{9,1},{17,9},{25,17},{2,26},{10... | collective-permute-start | bytes 589832 | tf_op jit(solution)/shard_map/ppermute | solution.py:378
  217.4 7.5 %collective-permute-start.37 = (bf16[16,3072]{1,0:T(8,128)(2,1)S(1)}, bf16[16,3072]{1,0:T(8,128)(2,1)S(1)}, u32[]{:S(2)}, u32[]{:S(2)}) collective-permute-start(bf16[16,3072]{1,0:T(8,128)(2,1)S(1)} %slice_bitcast_fusion.6), channel_id=1, source_target_pairs={{0,24},{8,0},{16,8},{24,16},{1,25},{9,1},{17,9},{25,17},{2,26},{10... | collective-permute-start | bytes 294920 | tf_op jit(solution)/shard_map/ppermute | solution.py:378
  220.0 7.7 %collective-permute-start.39 = (bf16[16,3072]{1,0:T(8,128)(2,1)S(1)}, bf16[16,3072]{1,0:T(8,128)(2,1)S(1)}, u32[]{:S(2)}, u32[]{:S(2)}) collective-permute-start(bf16[16,3072]{1,0:T(8,128)(2,1)S(1)} %get-tuple-element.91), channel_id=1, source_target_pairs={{0,16},{8,24},{16,0},{24,8},{1,17},{9,25},{17,1},{25,9},{2,18},{10... | collective-permute-start | bytes 294920 | tf_op jit(solution)/shard_map/ppermute | solution.py:378
  220.6 9.5 %collective-permute-start.40 = (bf16[16,3072]{1,0:T(8,128)(2,1)S(1)}, bf16[16,3072]{1,0:T(8,128)(2,1)S(1)}, u32[]{:S(2)}, u32[]{:S(2)}) collective-permute-start(bf16[16,3072]{1,0:T(8,128)(2,1)S(1)} %get-tuple-element.92), channel_id=1, source_target_pairs={{0,8},{8,16},{16,24},{24,0},{1,9},{9,17},{17,25},{25,1},{2,10},{10... | collective-permute-start | bytes 294920 | tf_op jit(solution)/shard_map/ppermute | solution.py:378
  221.3 8.9 %collective-permute-start.42 = (bf16[16,3072]{1,0:T(8,128)(2,1)S(1)}, bf16[16,3072]{1,0:T(8,128)(2,1)S(1)}, u32[]{:S(2)}, u32[]{:S(2)}) collective-permute-start(bf16[16,3072]{1,0:T(8,128)(2,1)S(1)} %slice_bitcast_fusion.2), channel_id=1, source_target_pairs={{0,96},{32,0},{64,32},{96,64},{1,97},{33,1},{65,33},{97,65},{2,98}... | collective-permute-start | bytes 294920 | tf_op jit(solution)/shard_map/ppermute | solution.py:378
  223.3 7.0 %collective-permute-start.44 = (bf16[16,3072]{1,0:T(8,128)(2,1)S(1)}, bf16[16,3072]{1,0:T(8,128)(2,1)S(1)}, u32[]{:S(2)}, u32[]{:S(2)}) collective-permute-start(bf16[16,3072]{1,0:T(8,128)(2,1)S(1)} %get-tuple-element.93), channel_id=1, source_target_pairs={{0,64},{32,96},{64,0},{96,32},{1,65},{33,97},{65,1},{97,33},{2,66}... | collective-permute-start | bytes 294920 | tf_op jit(solution)/shard_map/ppermute | solution.py:378
  224.8 6.9 %collective-permute-start.45 = (bf16[16,3072]{1,0:T(8,128)(2,1)S(1)}, bf16[16,3072]{1,0:T(8,128)(2,1)S(1)}, u32[]{:S(2)}, u32[]{:S(2)}) collective-permute-start(bf16[16,3072]{1,0:T(8,128)(2,1)S(1)} %get-tuple-element.94), channel_id=1, source_target_pairs={{0,32},{32,64},{64,96},{96,0},{1,33},{33,65},{65,97},{97,1},{2,34}... | collective-permute-start | bytes 294920 | tf_op jit(solution)/shard_map/ppermute | solution.py:378
  232.5 17.2 %all-to-all-start.1 = ((bf16[8,96,128]{2,1,0:T(8,128)(2,1)}), bf16[8,96,128]{2,1,0:T(8,128)(2,1)S(1)}, u32[]{:S(2)}, u32[]{:S(2)}) async-start(bf16[8,96,128]{2,1,0:T(8,128)(2,1)} %reshape.65), calls=%async_computation.2 | async-start | bytes 393216 | tf_op jit(solution)/shard_map/all_to_all | solution.py:424
  249.8 12.4 %all-to-all-start.2 = ((bf16[8,32,768]{2,1,0:T(8,128)(2,1)}), bf16[8,32,768]{2,1,0:T(8,128)(2,1)S(1)}, u32[]{:S(2)}, u32[]{:S(2)}) async-start(bf16[8,32,768]{2,1,0:T(8,128)(2,1)} %bitcast.28), calls=%async_computation.3 | async-start | bytes 786432 | tf_op jit(solution)/shard_map/all_to_all | solution.py:560
  262.2 66.5 %copy-start = (bf16[8,32,768]{2,1,0:T(8,128)(2,1)}, bf16[8,32,768]{2,1,0:T(8,128)(2,1)S(1)}, u32[]{:S(2)}) copy-start(bf16[8,32,768]{2,1,0:T(8,128)(2,1)S(1)} %all-to-all-done.2.mixed_ref) | copy-start | bytes 1179652
  310.0 17.5 %all-to-all-start.3 = ((bf16[8,384,128]{2,1,0:T(8,128)(2,1)}), bf16[8,384,128]{2,1,0:T(8,128)(2,1)S(1)}, u32[]{:S(2)}, u32[]{:S(2)}) async-start(bf16[8,384,128]{2,1,0:T(8,128)(2,1)} %reshape.68), calls=%async_computation.4 | async-start | bytes 1572864 | tf_op jit(solution)/shard_map/all_to_all | solution.py:424
  (20 other events, 95.2 us)
Sparse Core Ops, SparseCore 0:
  75.1 105.9 all-gather.1
  209.5 98.2 reduce-scatter.1

commit v4 on v3

--- a/solution.py
+++ b/solution.py
@@ -420,7 +420,10 @@
 
 
 def home_rows(summed):
-    lines = summed.reshape(EXPERTS, -1, HEAD_DIM)
+    rows, model = summed.shape
+    each = rows // EXPERTS
+    whole_tiles = each % 8 == 0
+    lines = summed.reshape((EXPERTS, each, model) if whole_tiles else (EXPERTS, -1, HEAD_DIM))
     back = lax.all_to_all(lines, EXP, split_axis=0, concat_axis=0, tiled=True)
     return back.reshape(summed.shape)
 

time: 340 us -> 337 us (level)
    unnamed x69 -> x71, local copies, waits for them, and re-layouts: 15 us -> 15.9 us
  transfers between devices with their start and end apart: 51 -> 51, of which waited for: 20 -> 20; matrix products, arithmetic and copies ran while one was open for 6% -> 6% of each run, Pallas kernels for 5% -> 6%
where the time goes in v4:
time: 337 us; the launch traced here: 336 us
  waiting for transfers between devices  131 us (39%)
  starting transfers between devices  86.9 us (26%)
  Pallas kernels  60.4 us (18%)
  blocking collectives  20.2 us (6%)
  local copies, waits for them, and re-layouts  19.8 us (6%)
  between operations  14 us (4%)
  other arithmetic  4.52 us (1%)
    ppermute x43, starting transfers between devices, shift(): lax.ppermute(value, axis, [(i, (i + step) % count) for i in range(count)])  56 us
    reduce_scatter x1, waiting for transfers between devices, per_device(): first = lax.psum_scatter(partial, SEQ, scatter_dimension=0, tiled=True)  45.7 us
    ppermute x43, waiting for transfers between devices, shift(): lax.ppermute(value, axis, [(i, (i + step) % count) for i in range(count)])  42.6 us
    pallas_call x1, Pallas kernels, expert_rows(): pl.pallas_call(rows_kernel, grid=(total // TILE,), out_shape=shape((total...  28.2 us
    all_to_all x1, blocking collectives, per_device(): parts = lax.all_to_all(packed, EXP, split_axis=0, concat_axis=0, tiled=True)  20.2 us
    all_to_all x2, waiting for transfers between devices, home_rows(): back = lax.all_to_all(lines, EXP, split_axis=0, concat_axis=0, tiled=True)  16.8 us
    all_to_all x2, starting transfers between devices, home_rows(): back = lax.all_to_all(lines, EXP, split_axis=0, concat_axis=0, tiled=True)  16.5 us
    unnamed x71, local copies, waits for them, and re-layouts  15.9 us
  transfers between devices with their start and end apart: 51, of which 20 were waited for; matrix products, arithmetic and copies ran while one was open for 6% of the time, Pallas kernels for 6%

profile of v4, /device:TPU:1, one launch (start us, length us, event | category | flops | bytes accessed | tf_op | source)
XLA Modules:
  0.0 336.2 jit_solution(456034052939505850)
XLA Ops:
  6.5 2.8 shard_map.109.refs_0_
  9.4 2.1 collective-permute-start
  11.5 2.6 collective-permute-start.1
  14.1 1.1 collective-permute-start.2
  15.2 1.5 collective-permute-start.3
  16.7 3.3 shard_map.110.inner_ref
  21.4 1.3 reshape.63.gain_ref
  23.5 1.3 collective-permute-start.7
  24.7 2.5 collective-permute-start.8
  27.2 1.2 collective-permute-start.9
  28.4 2.4 shard_map.111
  30.8 3.5 %collective-permute-start.4 = (bf16[784,128]{1,0:T(8,128)(2,1)}, bf16[784,128]{1,0:T(8,128)(2,1)S(1)}, u32[]{:S(2)}, u32[]{:S(2)}) collective-permute-start(bf16[784,128]{1,0:T(8,128)(2,1)} %get-tuple-element.53), channel_id=1, source_target_pairs={{0,32},{32,64},{64,96},{1,33},{33,65},{65,97},{2,34},{34,66},{66,9... | collective-permute-start | bytes 602120 | tf_op jit(solution)/shard_map/ppermute | solution.py:521
  34.3 5.2 %collective-permute-start.5 = (bf16[784,128]{1,0:T(8,128)(2,1)}, bf16[784,128]{1,0:T(8,128)(2,1)S(1)}, u32[]{:S(2)}, u32[]{:S(2)}) collective-permute-start(bf16[784,128]{1,0:T(8,128)(2,1)} %get-tuple-element.53), channel_id=1, source_target_pairs={{0,64},{32,96},{1,65},{33,97},{2,66},{34,98},{3,67},{35,99},{4,68}... | collective-permute-start | bytes 602120 | tf_op jit(solution)/shard_map/ppermute | solution.py:521
  39.7 1.3 collective-permute-start.6
  42.5 4.1 %collective-permute-done.6.line3_ref = bf16[784,128]{1,0:T(8,128)(2,1)S(1)} collective-permute-done((bf16[784,128]{1,0:T(8,128)(2,1)}, bf16[784,128]{1,0:T(8,128)(2,1)S(1)}, u32[]{:S(2)}, u32[]{:S(2)}) %collective-permute-start.6) | collective-permute-done | bytes 200736 | tf_op jit(solution)/shard_map/ppermute | solution.py:521
  47.3 4.9 %shard_map.112 = (bf16[256,768]{1,0:T(8,128)(2,1)}, bf16[8,80,768]{2,1,0:T(8,128)(2,1)}) custom-call(bf16[256,768]{1,0:T(8,128)(2,1)} %query_ref.3, f32[6,256]{1,0:T(8,128)} %bitcast.57, f32[256,768]{1,0:T(8,128)} %shard_map.110.inner_ref, bf16[256,768]{1,0:T(8,128)(2,1)} %residual_ref.1, f32[1,768]{1,0:T(1,128)} %reshape.63.gain_ref, ...), custom_call_target="tpu_custom_call" | custom-call | tf_op jit(solution)/shard_map/pallas_call | solution.py:523
  52.2 20.2 %all_to_all.20.parts_ref = bf16[8,80,768]{2,1,0:T(8,128)(2,1)} all-to-all(bf16[8,80,768]{2,1,0:T(8,128)(2,1)} %get-tuple-element.57), channel_id=1, replica_groups=mesh['z'=4,'y'=4,'x'=4,'core'=2] {'x','core'}, dimensions={0} | all-to-all | bytes 1966080 | tf_op jit(solution)/shard_map/all_to_all | solution.py:543
  72.4 2.6 shard_map.113
  75.0 1.2 collective-permute-start.20
  76.2 2.2 collective-permute-start.21
  79.0 2.0 collective-permute-start.11
  81.0 1.2 collective-permute-start.12
  83.0 2.0 collective-permute-start.25
  84.9 0.9 pad_maximum_fusion.2.refs_8_
  86.3 2.4 collective-permute-start.27
  88.8 3.5 %collective-permute-start.16 = (bf16[2,16,3072]{2,1,0:T(8,128)(2,1)S(1)}, bf16[2,16,3072]{2,1,0:T(8,128)(2,1)S(1)}, u32[]{:S(2)}, u32[]{:S(2)}) collective-permute-start(bf16[2,16,3072]{2,1,0:T(8,128)(2,1)S(1)} %pad_maximum_fusion.1.refs_1_), channel_id=1, source_target_pairs={{0,96},{32,0},{64,32},{96,64},{1,97},{33,1},{65,33},{97,65},{2,98}... | collective-permute-start | bytes 589832 | tf_op jit(solution)/shard_map/ppermute | solution.py:378
  93.7 1.6 collective-permute-start.14
  95.4 2.0 collective-permute-done.23.refs_11_
  97.4 1.3 collective-permute-start.13
  98.6 7.1 %collective-permute-done.22.refs_10_ = bf16[2,16,3072]{2,1,0:T(8,128)(2,1)S(1)} collective-permute-done((bf16[2,16,3072]{2,1,0:T(8,128)(2,1)S(1)}, bf16[2,16,3072]{2,1,0:T(8,128)(2,1)S(1)}, u32[]{:S(2)}, u32[]{:S(2)}) %collective-permute-start.22) | collective-permute-done | bytes 196640 | tf_op jit(solution)/shard_map/ppermute | solution.py:378
  105.8 2.6 collective-permute-start.18
  108.5 1.4 collective-permute-start.24
  110.0 1.4 collective-permute-start.15
  111.4 10.6 %copy.24.refs_16_.up_ref = bf16[1,6144,576]{2,1,0:T(8,128)(2,1)} copy(bf16[1,6144,576]{1,2,0:T(8,128)(2,1)} %param.20) | data formatting | bytes 14155776 | tf_op args[9]
  123.6 12.9 %shard_map.114 = (bf16[2,16,3072]{2,1,0:T(8,128)(2,1)}, bf16[2,16,3072]{2,1,0:T(8,128)(2,1)}, bf16[2,16,3072]{2,1,0:T(8,128)(2,1)}, bf16[2,16,3072]{2,1,0:T(8,12...) custom-call(bf16[2,16,3072]{2,1,0:T(8,128)(2,1)} %copy-done.11, ...), custom_call_target="tpu_custom_call" | custom-call | flops 5435817984 | bytes 20447232 | tf_op jit(solution)/shard_map/pallas_call | solution.py:307
  136.7 2.5 collective-permute-start.29
  139.2 2.7 collective-permute-start.31
  141.9 5.8 %collective-permute-done.28 = bf16[2,16,3072]{2,1,0:T(8,128)(2,1)S(1)} collective-permute-done((bf16[2,16,3072]{2,1,0:T(8,128)(2,1)}, bf16[2,16,3072]{2,1,0:T(8,128)(2,1)S(1)}, u32[]{:S(2)}, u32[]{:S(2)}) %collective-permute-start.28) | collective-permute-done | bytes 196640 | tf_op jit(solution)/shard_map/ppermute | solution.py:378
  147.8 1.3 collective-permute-start.33
  149.2 7.0 %collective-permute-done.30 = bf16[2,16,3072]{2,1,0:T(8,128)(2,1)S(1)} collective-permute-done((bf16[2,16,3072]{2,1,0:T(8,128)(2,1)}, bf16[2,16,3072]{2,1,0:T(8,128)(2,1)S(1)}, u32[]{:S(2)}, u32[]{:S(2)}) %collective-permute-start.30) | collective-permute-done | bytes 196640 | tf_op jit(solution)/shard_map/ppermute | solution.py:378
  156.2 1.3 collective-permute-start.35
  157.5 3.9 %collective-permute-done.34 = bf16[2,16,3072]{2,1,0:T(8,128)(2,1)S(1)} collective-permute-done((bf16[2,16,3072]{2,1,0:T(8,128)(2,1)}, bf16[2,16,3072]{2,1,0:T(8,128)(2,1)S(1)}, u32[]{:S(2)}, u32[]{:S(2)}) %collective-permute-start.34) | collective-permute-done | bytes 196640 | tf_op jit(solution)/shard_map/ppermute | solution.py:378
  161.4 6.2 %collective-permute-done.35 = bf16[2,16,3072]{2,1,0:T(8,128)(2,1)S(1)} collective-permute-done((bf16[2,16,3072]{2,1,0:T(8,128)(2,1)}, bf16[2,16,3072]{2,1,0:T(8,128)(2,1)S(1)}, u32[]{:S(2)}, u32[]{:S(2)}) %collective-permute-start.35) | collective-permute-done | bytes 196640 | tf_op jit(solution)/shard_map/ppermute | solution.py:378
  167.6 13.4 %all-gather.2.cloned.1.call-done.rows_ref = bf16[1024,6144]{1,0:T(8,128)(2,1)} async-done(((bf16[64,6144]{1,0:T(8,128)(2,1)}), bf16[1024,6144]{1,0:T(8,128)(2,1)}) %all-gather.2.cloned.1.call-update) | async-done | bytes 12582928 | tf_op jit(solution)/shard_map/all_gather | solution.py:550
  181.0 28.2 %shard_map.115 = bf16[1024,6144]{1,0:T(8,128)(2,1)} custom-call(bf16[1024,6144]{1,0:T(8,128)(2,1)} %all-gather.2.cloned.1.call-done.rows_ref, bf16[1,6144,576]{2,1,0:T(8,128)(2,1)} %copy.24.refs_16_.up_ref, bf16[1,576,6144]{2,1,0:T(8,128)(2,1)} %down_ref.1), custom_call_target="tpu_custom_call" | custom-call | flops 14495514624 | bytes 39321600 | tf_op jit(solution)/shard_map/pallas_call | solution.py:340
  210.2 1.2 collective-permute-start.36
  211.4 1.6 collective-permute-start.38
  213.1 1.3 collective-permute-start.41
  214.5 1.5 collective-permute-start.43
  216.0 1.3 collective-permute-done.36
  217.4 2.5 collective-permute-start.37
  221.3 1.8 collective-permute-start.42
  223.3 1.5 collective-permute-done.37
  224.8 2.9 collective-permute-done.39
  227.7 2.4 collective-permute-done.40
  230.2 1.4 collective-permute-done.45
  232.5 11.3 %all-to-all-start.1 = ((bf16[8,96,128]{2,1,0:T(8,128)(2,1)}), bf16[8,96,128]{2,1,0:T(8,128)(2,1)S(1)}, u32[]{:S(2)}, u32[]{:S(2)}) async-start(bf16[8,96,128]{2,1,0:T(8,128)(2,1)} %reshape.65), calls=%async_computation.2 | async-start | bytes 393216 | tf_op jit(solution)/shard_map/all_to_all | solution.py:427
  243.8 5.9 %all-to-all-done.1 = bf16[8,96,128]{2,1,0:T(8,128)(2,1)S(1)} async-done(((bf16[8,96,128]{2,1,0:T(8,128)(2,1)}), bf16[8,96,128]{2,1,0:T(8,128)(2,1)S(1)}, u32[]{:S(2)}, u32[]{:S(2)}) %all-to-all-start.1) | async-done | bytes 196640 | tf_op jit(solution)/shard_map/all_to_all | solution.py:427
  249.7 4.3 %all-to-all-start.2 = ((bf16[8,32,768]{2,1,0:T(8,128)(2,1)}), bf16[8,32,768]{2,1,0:T(8,128)(2,1)S(1)}, u32[]{:S(2)}, u32[]{:S(2)}) async-start(bf16[8,32,768]{2,1,0:T(8,128)(2,1)} %bitcast.28), calls=%async_computation.3 | async-start | bytes 786432 | tf_op jit(solution)/shard_map/all_to_all | solution.py:563
  254.8 7.3 %all-to-all-done.2.mixed_ref = bf16[8,32,768]{2,1,0:T(8,128)(2,1)S(1)} async-done(((bf16[8,32,768]{2,1,0:T(8,128)(2,1)}), bf16[8,32,768]{2,1,0:T(8,128)(2,1)S(1)}, u32[]{:S(2)}, u32[]{:S(2)}) %all-to-all-start.2) | async-done | bytes 393248 | tf_op jit(solution)/shard_map/all_to_all | solution.py:563
  262.1 45.7 %reduce-scatter.2.cloned.1.call-done = bf16[64,6144]{1,0:T(8,128)(2,1)} async-done(((bf16[1024,6144]{1,0:T(8,128)(2,1)}), bf16[64,6144]{1,0:T(8,128)(2,1)}) %reduce-scatter.2.cloned.1.call-update) | async-done | bytes 786448 | tf_op jit(solution)/shard_map/reduce_scatter | solution.py:561
  307.8 5.2 %all-to-all-start.3 = ((bf16[8,8,6144]{2,1,0:T(8,128)(2,1)}), bf16[8,8,6144]{2,1,0:T(8,128)(2,1)S(1)}, u32[]{:S(2)}, u32[]{:S(2)}) async-start(bf16[8,8,6144]{2,1,0:T(8,128)(2,1)} %bitcast.46), calls=%async_computation.4 | async-start | bytes 1572864 | tf_op jit(solution)/shard_map/all_to_all | solution.py:427
  314.3 10.9 %all-to-all-done.3 = bf16[8,8,6144]{2,1,0:T(8,128)(2,1)S(1)} async-done(((bf16[8,8,6144]{2,1,0:T(8,128)(2,1)}), bf16[8,8,6144]{2,1,0:T(8,128)(2,1)S(1)}, u32[]{:S(2)}, u32[]{:S(2)}) %all-to-all-start.3) | async-done | bytes 786464 | tf_op jit(solution)/shard_map/all_to_all | solution.py:427
  326.1 3.2 shard_map.116
  (167 shorter events, 16.3 us)
Async XLA Ops:
  6.5 174.5 %all-gather.2.cloned.1.call-start = ((), (), s32[]{:S(2)}) async-start(), calls=%async_computation.5 | async-start | bytes 13369344 | tf_op jit(solution)/shard_map/all_gather | solution.py:550
  9.4 14.0 %collective-permute-start = (bf16[784,128]{1,0:T(8,128)(2,1)}, bf16[784,128]{1,0:T(8,128)(2,1)S(1)}, u32[]{:S(2)}, u32[]{:S(2)}) collective-permute-start(bf16[784,128]{1,0:T(8,128)(2,1)} %shard_map.109.refs_0_), channel_id=1, source_target_pairs={{0,8},{8,16},{16,24},{24,0},{1,9},{9,17},{17,25},{25,1},{2,10},{10... | collective-permute-start | bytes 602120 | tf_op jit(solution)/shard_map/ppermute | solution.py:378
  11.5 11.9 %collective-permute-start.1 = (bf16[784,128]{1,0:T(8,128)(2,1)}, bf16[784,128]{1,0:T(8,128)(2,1)S(1)}, u32[]{:S(2)}, u32[]{:S(2)}) collective-permute-start(bf16[784,128]{1,0:T(8,128)(2,1)} %shard_map.109.refs_0_), channel_id=1, source_target_pairs={{0,16},{8,24},{16,0},{24,8},{1,17},{9,25},{17,1},{25,9},{2,18},{10... | collective-permute-start | bytes 602120 | tf_op jit(solution)/shard_map/ppermute | solution.py:378
  14.1 9.3 %collective-permute-start.2 = (bf16[784,128]{1,0:T(8,128)(2,1)}, bf16[784,128]{1,0:T(8,128)(2,1)S(1)}, u32[]{:S(2)}, u32[]{:S(2)}) collective-permute-start(bf16[784,128]{1,0:T(8,128)(2,1)} %shard_map.109.refs_0_), channel_id=1, source_target_pairs={{0,24},{8,0},{16,8},{24,16},{1,25},{9,1},{17,9},{25,17},{2,26},{10... | collective-permute-start | bytes 602120 | tf_op jit(solution)/shard_map/ppermute | solution.py:378
  15.2 7.5 %collective-permute-start.3 = (s32[2,32]{1,0:T(2,128)}, s32[2,32]{1,0:T(2,128)S(1)}, u32[]{:S(2)}, u32[]{:S(2)}) collective-permute-start(s32[2,32]{1,0:T(2,128)} %bitcast.60), channel_id=1, source_target_pairs={{0,1},{1,0},{2,3},{3,2},{4,5},{5,4},{6,7},{7,6},{8,9},{9,8},{10,11... | collective-permute-start | bytes 776 | tf_op jit(solution)/shard_map/ppermute | solution.py:378
  23.5 16.2 %collective-permute-start.7 = (s32[2,2,32]{2,1,0:T(2,128)S(1)}, s32[2,2,32]{2,1,0:T(2,128)S(1)}, u32[]{:S(2)}, u32[]{:S(2)}) collective-permute-start(s32[2,2,32]{2,1,0:T(2,128)S(1)} %add_select_fusion), channel_id=1, source_target_pairs={{0,2},{2,4},{4,6},{6,0},{1,3},{3,5},{5,7},{7,1},{8,10},{10,12},{12... | collective-permute-start | bytes 1544 | tf_op jit(solution)/shard_map/ppermute | solution.py:378
  24.7 16.3 %collective-permute-start.8 = (s32[2,2,32]{2,1,0:T(2,128)S(1)}, s32[2,2,32]{2,1,0:T(2,128)S(1)}, u32[]{:S(2)}, u32[]{:S(2)}) collective-permute-start(s32[2,2,32]{2,1,0:T(2,128)S(1)} %add_select_fusion), channel_id=1, source_target_pairs={{0,4},{2,6},{4,0},{6,2},{1,5},{3,7},{5,1},{7,3},{8,12},{10,14},{12... | collective-permute-start | bytes 1544 | tf_op jit(solution)/shard_map/ppermute | solution.py:378
  27.2 14.0 %collective-permute-start.9 = (s32[2,2,32]{2,1,0:T(2,128)S(1)}, s32[2,2,32]{2,1,0:T(2,128)S(1)}, u32[]{:S(2)}, u32[]{:S(2)}) collective-permute-start(s32[2,2,32]{2,1,0:T(2,128)S(1)} %add_select_fusion), channel_id=1, source_target_pairs={{0,6},{2,0},{4,2},{6,4},{1,7},{3,1},{5,3},{7,5},{8,14},{10,8},{12,... | collective-permute-start | bytes 1544 | tf_op jit(solution)/shard_map/ppermute | solution.py:378
  30.8 11.1 %collective-permute-start.4 = (bf16[784,128]{1,0:T(8,128)(2,1)}, bf16[784,128]{1,0:T(8,128)(2,1)S(1)}, u32[]{:S(2)}, u32[]{:S(2)}) collective-permute-start(bf16[784,128]{1,0:T(8,128)(2,1)} %get-tuple-element.53), channel_id=1, source_target_pairs={{0,32},{32,64},{64,96},{1,33},{33,65},{65,97},{2,34},{34,66},{66,9... | collective-permute-start | bytes 602120 | tf_op jit(solution)/shard_map/ppermute | solution.py:521
  34.3 8.2 %collective-permute-start.5 = (bf16[784,128]{1,0:T(8,128)(2,1)}, bf16[784,128]{1,0:T(8,128)(2,1)S(1)}, u32[]{:S(2)}, u32[]{:S(2)}) collective-permute-start(bf16[784,128]{1,0:T(8,128)(2,1)} %get-tuple-element.53), channel_id=1, source_target_pairs={{0,64},{32,96},{1,65},{33,97},{2,66},{34,98},{3,67},{35,99},{4,68}... | collective-permute-start | bytes 602120 | tf_op jit(solution)/shard_map/ppermute | solution.py:521
  39.7 6.9 %collective-permute-start.6 = (bf16[784,128]{1,0:T(8,128)(2,1)}, bf16[784,128]{1,0:T(8,128)(2,1)S(1)}, u32[]{:S(2)}, u32[]{:S(2)}) collective-permute-start(bf16[784,128]{1,0:T(8,128)(2,1)} %get-tuple-element.53), channel_id=1, source_target_pairs={{0,96},{1,97},{2,98},{3,99},{4,100},{5,101},{6,102},{7,103},{8,104... | collective-permute-start | bytes 602120 | tf_op jit(solution)/shard_map/ppermute | solution.py:521
  74.9 232.8 %reduce-scatter.2.cloned.1.call-start = ((), (), s32[]{:S(2)}) async-start(), calls=%async_computation.6 | async-start | bytes 13369344 | tf_op jit(solution)/shard_map/reduce_scatter | solution.py:561
  75.0 7.2 %collective-permute-start.20 = (bf16[16,3072]{1,0:T(8,128)(2,1)}, bf16[16,3072]{1,0:T(8,128)(2,1)S(1)}, u32[]{:S(2)}, u32[]{:S(2)}) collective-permute-start(bf16[16,3072]{1,0:T(8,128)(2,1)} %get-tuple-element.60), channel_id=1, source_target_pairs={{0,64},{32,96},{64,0},{96,32},{1,65},{33,97},{65,1},{97,33},{2,66}... | collective-permute-start | bytes 294920 | tf_op jit(solution)/shard_map/ppermute | solution.py:378
  76.2 6.7 %collective-permute-start.21 = (bf16[16,3072]{1,0:T(8,128)(2,1)}, bf16[16,3072]{1,0:T(8,128)(2,1)S(1)}, u32[]{:S(2)}, u32[]{:S(2)}) collective-permute-start(bf16[16,3072]{1,0:T(8,128)(2,1)} %get-tuple-element.60), channel_id=1, source_target_pairs={{0,96},{32,0},{64,32},{96,64},{1,97},{33,1},{65,33},{97,65},{2,98}... | collective-permute-start | bytes 294920 | tf_op jit(solution)/shard_map/ppermute | solution.py:378
  78.5 6.5 %collective-permute-start.19 = (bf16[16,3072]{1,0:T(8,128)(2,1)}, bf16[16,3072]{1,0:T(8,128)(2,1)S(1)}, u32[]{:S(2)}, u32[]{:S(2)}) collective-permute-start(bf16[16,3072]{1,0:T(8,128)(2,1)} %get-tuple-element.60), channel_id=1, source_target_pairs={{0,32},{32,64},{64,96},{96,0},{1,33},{33,65},{65,97},{97,1},{2,34}... | collective-permute-start | bytes 294920 | tf_op jit(solution)/shard_map/ppermute | solution.py:378
  79.0 6.9 %collective-permute-start.11 = (bf16[16,3072]{1,0:T(8,128)(2,1)}, bf16[16,3072]{1,0:T(8,128)(2,1)S(1)}, u32[]{:S(2)}, u32[]{:S(2)}) collective-permute-start(bf16[16,3072]{1,0:T(8,128)(2,1)} %get-tuple-element.59), channel_id=1, source_target_pairs={{0,16},{8,24},{16,0},{24,8},{1,17},{9,25},{17,1},{25,9},{2,18},{10... | collective-permute-start | bytes 294920 | tf_op jit(solution)/shard_map/ppermute | solution.py:378
  81.0 5.3 %collective-permute-start.12 = (bf16[16,3072]{1,0:T(8,128)(2,1)}, bf16[16,3072]{1,0:T(8,128)(2,1)S(1)}, u32[]{:S(2)}, u32[]{:S(2)}) collective-permute-start(bf16[16,3072]{1,0:T(8,128)(2,1)} %get-tuple-element.59), channel_id=1, source_target_pairs={{0,24},{8,0},{16,8},{24,16},{1,25},{9,1},{17,9},{25,17},{2,26},{10... | collective-permute-start | bytes 294920 | tf_op jit(solution)/shard_map/ppermute | solution.py:378
  82.2 6.6 %collective-permute-start.10 = (bf16[16,3072]{1,0:T(8,128)(2,1)}, bf16[16,3072]{1,0:T(8,128)(2,1)S(1)}, u32[]{:S(2)}, u32[]{:S(2)}) collective-permute-start(bf16[16,3072]{1,0:T(8,128)(2,1)} %get-tuple-element.59), channel_id=1, source_target_pairs={{0,8},{8,16},{16,24},{24,0},{1,9},{9,17},{17,25},{25,1},{2,10},{10... | collective-permute-start | bytes 294920 | tf_op jit(solution)/shard_map/ppermute | solution.py:378
  83.0 39.0 %copy-start.8 = (bf16[2,16,3072]{2,1,0:T(8,128)(2,1)}, bf16[2,16,3072]{2,1,0:T(8,128)(2,1)S(1)}, u32[]{:S(2)}) copy-start(bf16[2,16,3072]{2,1,0:T(8,128)(2,1)S(1)} %pad_maximum_fusion.3.refs_9_) | copy-start | bytes 589828
  83.0 10.8 %collective-permute-start.25 = (bf16[2,16,3072]{2,1,0:T(8,128)(2,1)S(1)}, bf16[2,16,3072]{2,1,0:T(8,128)(2,1)S(1)}, u32[]{:S(2)}, u32[]{:S(2)}) collective-permute-start(bf16[2,16,3072]{2,1,0:T(8,128)(2,1)S(1)} %pad_maximum_fusion.3.refs_9_), channel_id=1, source_target_pairs={{0,24},{8,0},{16,8},{24,16},{1,25},{9,1},{17,9},{25,17},{2,26},{10... | collective-permute-start | bytes 589832 | tf_op jit(solution)/shard_map/ppermute | solution.py:378
  84.9 12.4 %collective-permute-start.23 = (bf16[2,16,3072]{2,1,0:T(8,128)(2,1)S(1)}, bf16[2,16,3072]{2,1,0:T(8,128)(2,1)S(1)}, u32[]{:S(2)}, u32[]{:S(2)}) collective-permute-start(bf16[2,16,3072]{2,1,0:T(8,128)(2,1)S(1)} %pad_maximum_fusion.3.refs_9_), channel_id=1, source_target_pairs={{0,8},{8,16},{16,24},{24,0},{1,9},{9,17},{17,25},{25,1},{2,10},{10... | collective-permute-start | bytes 589832 | tf_op jit(solution)/shard_map/ppermute | solution.py:378
  85.9 36.1 %copy-start.9 = (bf16[2,16,3072]{2,1,0:T(8,128)(2,1)}, bf16[2,16,3072]{2,1,0:T(8,128)(2,1)S(1)}, u32[]{:S(2)}) copy-start(bf16[2,16,3072]{2,1,0:T(8,128)(2,1)S(1)} %pad_maximum_fusion.2.refs_8_) | copy-start | bytes 589828
  85.9 19.9 %collective-permute-start.22 = (bf16[2,16,3072]{2,1,0:T(8,128)(2,1)S(1)}, bf16[2,16,3072]{2,1,0:T(8,128)(2,1)S(1)}, u32[]{:S(2)}, u32[]{:S(2)}) collective-permute-start(bf16[2,16,3072]{2,1,0:T(8,128)(2,1)S(1)} %pad_maximum_fusion.2.refs_8_), channel_id=1, source_target_pairs={{0,8},{8,16},{16,24},{24,0},{1,9},{9,17},{17,25},{25,1},{2,10},{10... | collective-permute-start | bytes 589832 | tf_op jit(solution)/shard_map/ppermute | solution.py:378
  86.3 22.1 %collective-permute-start.27 = (bf16[2,16,3072]{2,1,0:T(8,128)(2,1)S(1)}, bf16[2,16,3072]{2,1,0:T(8,128)(2,1)S(1)}, u32[]{:S(2)}, u32[]{:S(2)}) collective-permute-start(bf16[2,16,3072]{2,1,0:T(8,128)(2,1)S(1)} %pad_maximum_fusion.2.refs_8_), channel_id=1, source_target_pairs={{0,24},{8,0},{16,8},{24,16},{1,25},{9,1},{17,9},{25,17},{2,26},{10... | collective-permute-start | bytes 589832 | tf_op jit(solution)/shard_map/ppermute | solution.py:378
  88.7 33.4 %copy-start.10 = (bf16[2,16,3072]{2,1,0:T(8,128)(2,1)}, bf16[2,16,3072]{2,1,0:T(8,128)(2,1)S(1)}, u32[]{:S(2)}) copy-start(bf16[2,16,3072]{2,1,0:T(8,128)(2,1)S(1)} %pad_maximum_fusion.1.refs_1_) | copy-start | bytes 589828
  88.8 19.7 %collective-permute-start.16 = (bf16[2,16,3072]{2,1,0:T(8,128)(2,1)S(1)}, bf16[2,16,3072]{2,1,0:T(8,128)(2,1)S(1)}, u32[]{:S(2)}, u32[]{:S(2)}) collective-permute-start(bf16[2,16,3072]{2,1,0:T(8,128)(2,1)S(1)} %pad_maximum_fusion.1.refs_1_), channel_id=1, source_target_pairs={{0,96},{32,0},{64,32},{96,64},{1,97},{33,1},{65,33},{97,65},{2,98}... | collective-permute-start | bytes 589832 | tf_op jit(solution)/shard_map/ppermute | solution.py:378
  93.2 28.9 %copy-start.11 = (bf16[2,16,3072]{2,1,0:T(8,128)(2,1)}, bf16[2,16,3072]{2,1,0:T(8,128)(2,1)S(1)}, u32[]{:S(2)}) copy-start(bf16[2,16,3072]{2,1,0:T(8,128)(2,1)S(1)} %pad_maximum_fusion.refs_0_) | copy-start | bytes 589828
  93.7 28.4 %copy-start.22 = (bf16[2,16,3072]{2,1,0:T(8,128)(2,1)}, bf16[2,16,3072]{2,1,0:T(8,128)(2,1)S(1)}, u32[]{:S(2)}) copy-start(bf16[2,16,3072]{2,1,0:T(8,128)(2,1)S(1)} %collective-permute-done.25.refs_15_) | copy-start | bytes 589828
  93.7 16.2 %collective-permute-start.14 = (bf16[2,16,3072]{2,1,0:T(8,128)(2,1)S(1)}, bf16[2,16,3072]{2,1,0:T(8,128)(2,1)S(1)}, u32[]{:S(2)}, u32[]{:S(2)}) collective-permute-start(bf16[2,16,3072]{2,1,0:T(8,128)(2,1)S(1)} %pad_maximum_fusion.1.refs_1_), channel_id=1, source_target_pairs={{0,32},{32,64},{64,96},{96,0},{1,33},{33,65},{65,97},{97,1},{2,34}... | collective-permute-start | bytes 589832 | tf_op jit(solution)/shard_map/ppermute | solution.py:378
  97.4 24.8 %copy-start.23 = (bf16[2,16,3072]{2,1,0:T(8,128)(2,1)}, bf16[2,16,3072]{2,1,0:T(8,128)(2,1)S(1)}, u32[]{:S(2)}) copy-start(bf16[2,16,3072]{2,1,0:T(8,128)(2,1)S(1)} %collective-permute-done.23.refs_11_) | copy-start | bytes 589828
  97.4 12.6 %collective-permute-start.13 = (bf16[2,16,3072]{2,1,0:T(8,128)(2,1)S(1)}, bf16[2,16,3072]{2,1,0:T(8,128)(2,1)S(1)}, u32[]{:S(2)}, u32[]{:S(2)}) collective-permute-start(bf16[2,16,3072]{2,1,0:T(8,128)(2,1)S(1)} %pad_maximum_fusion.refs_0_), channel_id=1, source_target_pairs={{0,32},{32,64},{64,96},{96,0},{1,33},{33,65},{65,97},{97,1},{2,34}... | collective-permute-start | bytes 589832 | tf_op jit(solution)/shard_map/ppermute | solution.py:378
  105.8 16.4 %copy-start.24 = (bf16[2,16,3072]{2,1,0:T(8,128)(2,1)}, bf16[2,16,3072]{2,1,0:T(8,128)(2,1)S(1)}, u32[]{:S(2)}) copy-start(bf16[2,16,3072]{2,1,0:T(8,128)(2,1)S(1)} %collective-permute-done.22.refs_10_) | copy-start | bytes 589828
  105.8 16.2 %collective-permute-start.18 = (bf16[2,16,3072]{2,1,0:T(8,128)(2,1)S(1)}, bf16[2,16,3072]{2,1,0:T(8,128)(2,1)S(1)}, u32[]{:S(2)}, u32[]{:S(2)}) collective-permute-start(bf16[2,16,3072]{2,1,0:T(8,128)(2,1)S(1)} %pad_maximum_fusion.refs_0_), channel_id=1, source_target_pairs={{0,96},{32,0},{64,32},{96,64},{1,97},{33,1},{65,33},{97,65},{2,98}... | collective-permute-start | bytes 589832 | tf_op jit(solution)/shard_map/ppermute | solution.py:378
  108.4 13.7 %copy-start.25 = (bf16[2,16,3072]{2,1,0:T(8,128)(2,1)}, bf16[2,16,3072]{2,1,0:T(8,128)(2,1)S(1)}, u32[]{:S(2)}) copy-start(bf16[2,16,3072]{2,1,0:T(8,128)(2,1)S(1)} %collective-permute-done.27.refs_14_) | copy-start | bytes 589828
  108.4 13.6 %collective-permute-start.26 = (bf16[2,16,3072]{2,1,0:T(8,128)(2,1)S(1)}, bf16[2,16,3072]{2,1,0:T(8,128)(2,1)S(1)}, u32[]{:S(2)}, u32[]{:S(2)}) collective-permute-start(bf16[2,16,3072]{2,1,0:T(8,128)(2,1)S(1)} %collective-permute-done.25.refs_15_), channel_id=1, source_target_pairs={{0,24},{8,0},{16,8},{24,16},{1,25},{9,1},{17,9},{25,17},{2,26},{10... | collective-permute-start | bytes 589832 | tf_op jit(solution)/shard_map/ppermute | solution.py:378
  108.4 13.7 %copy-start.26 = (bf16[2,16,3072]{2,1,0:T(8,128)(2,1)}, bf16[2,16,3072]{2,1,0:T(8,128)(2,1)S(1)}, u32[]{:S(2)}) copy-start(bf16[2,16,3072]{2,1,0:T(8,128)(2,1)S(1)} %collective-permute-done.16.refs_7_) | copy-start | bytes 589828
  108.5 13.6 %collective-permute-start.24 = (bf16[2,16,3072]{2,1,0:T(8,128)(2,1)S(1)}, bf16[2,16,3072]{2,1,0:T(8,128)(2,1)S(1)}, u32[]{:S(2)}, u32[]{:S(2)}) collective-permute-start(bf16[2,16,3072]{2,1,0:T(8,128)(2,1)S(1)} %collective-permute-done.22.refs_10_), channel_id=1, source_target_pairs={{0,8},{8,16},{16,24},{24,0},{1,9},{9,17},{17,25},{25,1},{2,10},{10... | collective-permute-start | bytes 589832 | tf_op jit(solution)/shard_map/ppermute | solution.py:378
  109.9 12.2 %collective-permute-start.17 = (bf16[2,16,3072]{2,1,0:T(8,128)(2,1)S(1)}, bf16[2,16,3072]{2,1,0:T(8,128)(2,1)S(1)}, u32[]{:S(2)}, u32[]{:S(2)}) collective-permute-start(bf16[2,16,3072]{2,1,0:T(8,128)(2,1)S(1)} %collective-permute-done.16.refs_7_), channel_id=1, source_target_pairs={{0,96},{32,0},{64,32},{96,64},{1,97},{33,1},{65,33},{97,65},{2,98}... | collective-permute-start | bytes 589832 | tf_op jit(solution)/shard_map/ppermute | solution.py:378
  110.0 12.1 %collective-permute-start.15 = (bf16[2,16,3072]{2,1,0:T(8,128)(2,1)S(1)}, bf16[2,16,3072]{2,1,0:T(8,128)(2,1)S(1)}, u32[]{:S(2)}, u32[]{:S(2)}) collective-permute-start(bf16[2,16,3072]{2,1,0:T(8,128)(2,1)S(1)} %collective-permute-done.13.refs_2_), channel_id=1, source_target_pairs={{0,32},{32,64},{64,96},{96,0},{1,33},{33,65},{65,97},{97,1},{2,34}... | collective-permute-start | bytes 589832 | tf_op jit(solution)/shard_map/ppermute | solution.py:378
  136.4 11.3 %collective-permute-start.28 = (bf16[2,16,3072]{2,1,0:T(8,128)(2,1)}, bf16[2,16,3072]{2,1,0:T(8,128)(2,1)S(1)}, u32[]{:S(2)}, u32[]{:S(2)}) collective-permute-start(bf16[2,16,3072]{2,1,0:T(8,128)(2,1)} %get-tuple-element.61), channel_id=1, source_target_pairs={{0,32},{32,64},{64,96},{96,0},{1,33},{33,65},{65,97},{97,1},{2,34}... | collective-permute-start | bytes 589832 | tf_op jit(solution)/shard_map/ppermute | solution.py:378
  136.7 12.4 %collective-permute-start.29 = (bf16[2,16,3072]{2,1,0:T(8,128)(2,1)}, bf16[2,16,3072]{2,1,0:T(8,128)(2,1)S(1)}, u32[]{:S(2)}, u32[]{:S(2)}) collective-permute-start(bf16[2,16,3072]{2,1,0:T(8,128)(2,1)} %get-tuple-element.62), channel_id=1, source_target_pairs={{0,96},{32,0},{64,32},{96,64},{1,97},{33,1},{65,33},{97,65},{2,98}... | collective-permute-start | bytes 589832 | tf_op jit(solution)/shard_map/ppermute | solution.py:378
  139.2 17.0 %collective-permute-start.30 = (bf16[2,16,3072]{2,1,0:T(8,128)(2,1)}, bf16[2,16,3072]{2,1,0:T(8,128)(2,1)S(1)}, u32[]{:S(2)}, u32[]{:S(2)}) collective-permute-start(bf16[2,16,3072]{2,1,0:T(8,128)(2,1)} %get-tuple-element.63), channel_id=1, source_target_pairs={{0,32},{32,64},{64,96},{96,0},{1,33},{33,65},{65,97},{97,1},{2,34}... | collective-permute-start | bytes 589832 | tf_op jit(solution)/shard_map/ppermute | solution.py:378
  139.2 18.3 %collective-permute-start.31 = (bf16[2,16,3072]{2,1,0:T(8,128)(2,1)}, bf16[2,16,3072]{2,1,0:T(8,128)(2,1)S(1)}, u32[]{:S(2)}, u32[]{:S(2)}) collective-permute-start(bf16[2,16,3072]{2,1,0:T(8,128)(2,1)} %get-tuple-element.64), channel_id=1, source_target_pairs={{0,96},{32,0},{64,32},{96,64},{1,97},{33,1},{65,33},{97,65},{2,98}... | collective-permute-start | bytes 589832 | tf_op jit(solution)/shard_map/ppermute | solution.py:378
  141.9 15.7 %collective-permute-start.32 = (bf16[2,16,3072]{2,1,0:T(8,128)(2,1)}, bf16[2,16,3072]{2,1,0:T(8,128)(2,1)S(1)}, u32[]{:S(2)}, u32[]{:S(2)}) collective-permute-start(bf16[2,16,3072]{2,1,0:T(8,128)(2,1)} %get-tuple-element.65), channel_id=1, source_target_pairs={{0,8},{8,16},{16,24},{24,0},{1,9},{9,17},{17,25},{25,1},{2,10},{10... | collective-permute-start | bytes 589832 | tf_op jit(solution)/shard_map/ppermute | solution.py:378
  147.8 9.8 %collective-permute-start.33 = (bf16[2,16,3072]{2,1,0:T(8,128)(2,1)}, bf16[2,16,3072]{2,1,0:T(8,128)(2,1)S(1)}, u32[]{:S(2)}, u32[]{:S(2)}) collective-permute-start(bf16[2,16,3072]{2,1,0:T(8,128)(2,1)} %get-tuple-element.66), channel_id=1, source_target_pairs={{0,24},{8,0},{16,8},{24,16},{1,25},{9,1},{17,9},{25,17},{2,26},{10... | collective-permute-start | bytes 589832 | tf_op jit(solution)/shard_map/ppermute | solution.py:378
  149.1 12.3 %collective-permute-start.34 = (bf16[2,16,3072]{2,1,0:T(8,128)(2,1)}, bf16[2,16,3072]{2,1,0:T(8,128)(2,1)S(1)}, u32[]{:S(2)}, u32[]{:S(2)}) collective-permute-start(bf16[2,16,3072]{2,1,0:T(8,128)(2,1)} %get-tuple-element.67), channel_id=1, source_target_pairs={{0,8},{8,16},{16,24},{24,0},{1,9},{9,17},{17,25},{25,1},{2,10},{10... | collective-permute-start | bytes 589832 | tf_op jit(solution)/shard_map/ppermute | solution.py:378
  156.2 11.4 %collective-permute-start.35 = (bf16[2,16,3072]{2,1,0:T(8,128)(2,1)}, bf16[2,16,3072]{2,1,0:T(8,128)(2,1)S(1)}, u32[]{:S(2)}, u32[]{:S(2)}) collective-permute-start(bf16[2,16,3072]{2,1,0:T(8,128)(2,1)} %get-tuple-element.68), channel_id=1, source_target_pairs={{0,24},{8,0},{16,8},{24,16},{1,25},{9,1},{17,9},{25,17},{2,26},{10... | collective-permute-start | bytes 589832 | tf_op jit(solution)/shard_map/ppermute | solution.py:378
  209.3 13.9 %copy-start.12 = (bf16[2,16,3072]{2,1,0:T(8,128)(2,1)S(1)}, bf16[2,16,3072]{2,1,0:T(8,128)(2,1)}, u32[]{:S(2)}) copy-start(bf16[2,16,3072]{2,1,0:T(8,128)(2,1)} %get-tuple-element.82) | copy-start | bytes 589828
  209.3 103.6 %copy-start.20 = (s32[32,2]{0,1:T(2,128)S(1)}, s32[32,2]{0,1:T(2,128)}, u32[]{:S(2)}) copy-start(s32[32,2]{0,1:T(2,128)} %param.18) | copy-start | bytes 772
  209.3 104.3 %copy-start.21 = (f32[32,2]{0,1:T(2,128)S(1)}, f32[32,2]{0,1:T(2,128)}, u32[]{:S(2)}) copy-start(f32[32,2]{0,1:T(2,128)} %param.19) | copy-start | bytes 772
  210.2 7.0 %collective-permute-start.36 = (bf16[2,16,3072]{2,1,0:T(8,128)(2,1)S(1)}, bf16[2,16,3072]{2,1,0:T(8,128)(2,1)S(1)}, u32[]{:S(2)}, u32[]{:S(2)}) collective-permute-start(bf16[2,16,3072]{2,1,0:T(8,128)(2,1)S(1)} %add_convert_fusion.7), channel_id=1, source_target_pairs={{0,32},{32,64},{64,96},{96,0},{1,33},{33,65},{65,97},{97,1},{2,34}... | collective-permute-start | bytes 589832 | tf_op jit(solution)/shard_map/ppermute | solution.py:378
  211.4 8.5 %collective-permute-start.38 = (bf16[2,16,3072]{2,1,0:T(8,128)(2,1)S(1)}, bf16[2,16,3072]{2,1,0:T(8,128)(2,1)S(1)}, u32[]{:S(2)}, u32[]{:S(2)}) collective-permute-start(bf16[2,16,3072]{2,1,0:T(8,128)(2,1)S(1)} %add_convert_fusion.5), channel_id=1, source_target_pairs={{0,96},{32,0},{64,32},{96,64},{1,97},{33,1},{65,33},{97,65},{2,98}... | collective-permute-start | bytes 589832 | tf_op jit(solution)/shard_map/ppermute | solution.py:378
  213.1 8.1 %collective-permute-start.41 = (bf16[2,16,3072]{2,1,0:T(8,128)(2,1)S(1)}, bf16[2,16,3072]{2,1,0:T(8,128)(2,1)S(1)}, u32[]{:S(2)}, u32[]{:S(2)}) collective-permute-start(bf16[2,16,3072]{2,1,0:T(8,128)(2,1)S(1)} %add_convert_fusion.3), channel_id=1, source_target_pairs={{0,8},{8,16},{16,24},{24,0},{1,9},{9,17},{17,25},{25,1},{2,10},{10... | collective-permute-start | bytes 589832 | tf_op jit(solution)/shard_map/ppermute | solution.py:378
  214.5 8.7 %collective-permute-start.43 = (bf16[2,16,3072]{2,1,0:T(8,128)(2,1)S(1)}, bf16[2,16,3072]{2,1,0:T(8,128)(2,1)S(1)}, u32[]{:S(2)}, u32[]{:S(2)}) collective-permute-start(bf16[2,16,3072]{2,1,0:T(8,128)(2,1)S(1)} %add_convert_fusion.1), channel_id=1, source_target_pairs={{0,24},{8,0},{16,8},{24,16},{1,25},{9,1},{17,9},{25,17},{2,26},{10... | collective-permute-start | bytes 589832 | tf_op jit(solution)/shard_map/ppermute | solution.py:378
  217.4 7.4 %collective-permute-start.37 = (bf16[16,3072]{1,0:T(8,128)(2,1)S(1)}, bf16[16,3072]{1,0:T(8,128)(2,1)S(1)}, u32[]{:S(2)}, u32[]{:S(2)}) collective-permute-start(bf16[16,3072]{1,0:T(8,128)(2,1)S(1)} %slice_bitcast_fusion.6), channel_id=1, source_target_pairs={{0,24},{8,0},{16,8},{24,16},{1,25},{9,1},{17,9},{25,17},{2,26},{10... | collective-permute-start | bytes 294920 | tf_op jit(solution)/shard_map/ppermute | solution.py:378
  220.0 7.7 %collective-permute-start.39 = (bf16[16,3072]{1,0:T(8,128)(2,1)S(1)}, bf16[16,3072]{1,0:T(8,128)(2,1)S(1)}, u32[]{:S(2)}, u32[]{:S(2)}) collective-permute-start(bf16[16,3072]{1,0:T(8,128)(2,1)S(1)} %get-tuple-element.91), channel_id=1, source_target_pairs={{0,16},{8,24},{16,0},{24,8},{1,17},{9,25},{17,1},{25,9},{2,18},{10... | collective-permute-start | bytes 294920 | tf_op jit(solution)/shard_map/ppermute | solution.py:378
  220.6 9.5 %collective-permute-start.40 = (bf16[16,3072]{1,0:T(8,128)(2,1)S(1)}, bf16[16,3072]{1,0:T(8,128)(2,1)S(1)}, u32[]{:S(2)}, u32[]{:S(2)}) collective-permute-start(bf16[16,3072]{1,0:T(8,128)(2,1)S(1)} %get-tuple-element.92), channel_id=1, source_target_pairs={{0,8},{8,16},{16,24},{24,0},{1,9},{9,17},{17,25},{25,1},{2,10},{10... | collective-permute-start | bytes 294920 | tf_op jit(solution)/shard_map/ppermute | solution.py:378
  221.3 8.9 %collective-permute-start.42 = (bf16[16,3072]{1,0:T(8,128)(2,1)S(1)}, bf16[16,3072]{1,0:T(8,128)(2,1)S(1)}, u32[]{:S(2)}, u32[]{:S(2)}) collective-permute-start(bf16[16,3072]{1,0:T(8,128)(2,1)S(1)} %slice_bitcast_fusion.2), channel_id=1, source_target_pairs={{0,96},{32,0},{64,32},{96,64},{1,97},{33,1},{65,33},{97,65},{2,98}... | collective-permute-start | bytes 294920 | tf_op jit(solution)/shard_map/ppermute | solution.py:378
  223.2 7.0 %collective-permute-start.44 = (bf16[16,3072]{1,0:T(8,128)(2,1)S(1)}, bf16[16,3072]{1,0:T(8,128)(2,1)S(1)}, u32[]{:S(2)}, u32[]{:S(2)}) collective-permute-start(bf16[16,3072]{1,0:T(8,128)(2,1)S(1)} %get-tuple-element.93), channel_id=1, source_target_pairs={{0,64},{32,96},{64,0},{96,32},{1,65},{33,97},{65,1},{97,33},{2,66}... | collective-permute-start | bytes 294920 | tf_op jit(solution)/shard_map/ppermute | solution.py:378
  224.8 6.9 %collective-permute-start.45 = (bf16[16,3072]{1,0:T(8,128)(2,1)S(1)}, bf16[16,3072]{1,0:T(8,128)(2,1)S(1)}, u32[]{:S(2)}, u32[]{:S(2)}) collective-permute-start(bf16[16,3072]{1,0:T(8,128)(2,1)S(1)} %get-tuple-element.94), channel_id=1, source_target_pairs={{0,32},{32,64},{64,96},{96,0},{1,33},{33,65},{65,97},{97,1},{2,34}... | collective-permute-start | bytes 294920 | tf_op jit(solution)/shard_map/ppermute | solution.py:378
  232.5 17.2 %all-to-all-start.1 = ((bf16[8,96,128]{2,1,0:T(8,128)(2,1)}), bf16[8,96,128]{2,1,0:T(8,128)(2,1)S(1)}, u32[]{:S(2)}, u32[]{:S(2)}) async-start(bf16[8,96,128]{2,1,0:T(8,128)(2,1)} %reshape.65), calls=%async_computation.2 | async-start | bytes 393216 | tf_op jit(solution)/shard_map/all_to_all | solution.py:427
  249.7 12.4 %all-to-all-start.2 = ((bf16[8,32,768]{2,1,0:T(8,128)(2,1)}), bf16[8,32,768]{2,1,0:T(8,128)(2,1)S(1)}, u32[]{:S(2)}, u32[]{:S(2)}) async-start(bf16[8,32,768]{2,1,0:T(8,128)(2,1)} %bitcast.28), calls=%async_computation.3 | async-start | bytes 786432 | tf_op jit(solution)/shard_map/all_to_all | solution.py:563
  262.1 63.1 %copy-start.1 = (bf16[8,32,768]{2,1,0:T(8,128)(2,1)}, bf16[8,32,768]{2,1,0:T(8,128)(2,1)S(1)}, u32[]{:S(2)}) copy-start(bf16[8,32,768]{2,1,0:T(8,128)(2,1)S(1)} %all-to-all-done.2.mixed_ref) | copy-start | bytes 1179652
  307.8 17.5 %all-to-all-start.3 = ((bf16[8,8,6144]{2,1,0:T(8,128)(2,1)}), bf16[8,8,6144]{2,1,0:T(8,128)(2,1)S(1)}, u32[]{:S(2)}, u32[]{:S(2)}) async-start(bf16[8,8,6144]{2,1,0:T(8,128)(2,1)} %bitcast.46), calls=%async_computation.4 | async-start | bytes 1572864 | tf_op jit(solution)/shard_map/all_to_all | solution.py:427
  (21 other events, 96.0 us)
Sparse Core Ops, SparseCore 0:
  75.1 105.8 all-gather.1
  209.4 98.2 reduce-scatter.1
